TPU v7x, 32 devices: a whole 2x2x4 slice. The times are simulated.
32 devices in a mesh: dp: 8 (over y, x, core), expert: 4 (over z).
Axes of the slice: x: 2, y: 2, z: 4, core: 2. Of those that a mesh axis runs over, the one named last changes fastest.
Arguments:
- tokens: bfloat16 [2048, 4096], P('dp', 'expert'), may hold values from -100 to 100
- w_gate: bfloat16 [4, 4096, 14336], P('expert', None, 'dp'), may hold values from -0.09375 to 0.09375
- w_up: bfloat16 [4, 4096, 14336], P('expert', None, 'dp'), may hold values from -0.09375 to 0.09375
- w_down: bfloat16 [4, 14336, 4096], P('expert', 'dp'), may hold values from -0.046875 to 0.046875
- pick_block: int32 [4, 4], replicated, may hold values from 0 to 3
- pick_live: int32 [4, 4], replicated, may hold values from 0 to 1, as said below
- combine_weight: float32 [4, 4], replicated, may hold values from 0.25 to 1
Outputs:
- combined: bfloat16 [2048, 4096], P('dp', 'expert')
Inputs may be any that keep to these rules, and one draw needn't show every extreme that they name: `pick_live`: each expert takes at least one block, and some expert takes a block from every pair of dp rows.
All inputs are finite; a program needn't handle non-finite values.
Results may differ from a plain program's by a relative error of at most 0.02.
Values may be sent and summed in bfloat16 or wider, within the bound.
No kernel may reach another device: no remote copies, remote signals or barrier semaphores. Data moves between devices by JAX's collectives and lax.ppermute only.
A program may use at most 128 MiB of HBM per device.

v0:
```python
import jax
import jax.numpy as jnp
from jax import lax
from jax.sharding import PartitionSpec as P

BLOCK = 128


def from_partner(value, axis, stride):
    return lax.ppermute(value, axis, [(i, i ^ 1 << stride) for i in range(lax.axis_size(axis))])


def rms_normalize(values, square_sums, model_width):
    values_f32 = values.astype(jnp.float32)
    inv_rms = lax.rsqrt(square_sums / model_width + 1e-05)
    return (values_f32 * inv_rms[:, None]).astype(jnp.bfloat16)


def on_device(tokens, w_gate, w_up, w_down, pick_block, pick_live, combine_weight):
    expert_count = lax.axis_size("expert")
    features_dev = tokens.shape[1]
    model_width = features_dev * expert_count
    blocks_here = tokens.shape[0] // BLOCK
    half_rows = BLOCK // 2
    row_index = lax.axis_index("dp")
    half_bit = row_index % 2
    pair_index = row_index // 2
    tokens_f32 = tokens.astype(jnp.float32)
    square_sums = lax.psum(jnp.sum(tokens_f32 * tokens_f32, axis=1), "expert")
    source = rms_normalize(tokens, square_sums, model_width)
    picked = lax.dynamic_index_in_dim(pick_block, pair_index, axis=1, keepdims=False)
    live_flags = lax.dynamic_index_in_dim(pick_live, pair_index, axis=1, keepdims=False)
    weights_here = lax.dynamic_index_in_dim(combine_weight, pair_index, axis=1, keepdims=False)
    owned_here = (live_flags == 1) & (picked // blocks_here == half_bit)
    local_block = picked % blocks_here
    blocks = source.reshape(blocks_here, BLOCK, features_dev)
    chosen = jnp.take(blocks, local_block, axis=0)
    chosen = jnp.where(owned_here[:, None, None], chosen, jnp.zeros((), jnp.bfloat16))
    arrived = lax.all_to_all(chosen, "expert", split_axis=0, concat_axis=2, tiled=True)[0]
    outgoing = lax.dynamic_slice_in_dim(arrived, (1 - half_bit) * half_rows, half_rows, 0)
    partner = from_partner(outgoing, "dp", 0)
    own_half = lax.dynamic_slice_in_dim(arrived, half_bit * half_rows, half_rows, 0)
    merged = own_half + partner
    gate_weights = w_gate[0]
    up_weights = w_up[0]
    down_weights = w_down[0]
    rows_piece = lax.all_gather(merged, "dp", axis=0, tiled=True)
    gate_proj = jnp.dot(rows_piece, gate_weights, preferred_element_type=jnp.float32)
    up_proj = jnp.dot(rows_piece, up_weights, preferred_element_type=jnp.float32)
    hidden = (jax.nn.silu(gate_proj) * up_proj).astype(jnp.bfloat16)
    partial_value = jnp.dot(hidden, down_weights, preferred_element_type=jnp.float32).astype(
        jnp.bfloat16
    )
    summed = lax.psum_scatter(
        lax.optimization_barrier(partial_value).astype(jnp.float32).astype(jnp.bfloat16),
        "dp",
        scatter_dimension=0,
        tiled=True,
    )
    spread = lax.all_to_all(summed[:, None, :], "expert", split_axis=2, concat_axis=1, tiled=True)
    other_half = from_partner(spread, "dp", 0)
    assembled = jnp.where(
        half_bit == 0,
        jnp.concatenate([spread, other_half], axis=0),
        jnp.concatenate([other_half, spread], axis=0),
    )
    slot_match = local_block[None, :] == jnp.arange(blocks_here, dtype=jnp.int32)[:, None]
    combine_coef = jnp.where(
        slot_match & owned_here[None, :], weights_here[None, :], jnp.zeros((), jnp.float32)
    )
    combined = jnp.einsum("le,red->lrd", combine_coef, assembled.astype(jnp.float32))
    return combined.astype(jnp.bfloat16).reshape(blocks_here * BLOCK, features_dev)


def solution(mesh):
    in_specs = (
        P("dp", "expert"),
        P("expert", None, "dp"),
        P("expert", None, "dp"),
        P("expert", "dp", None),
        P(),
        P(),
        P(),
    )
    out_specs = P("dp", "expert")
    return jax.shard_map(
        on_device, mesh=mesh, in_specs=in_specs, out_specs=out_specs, check_vma=False
    )
```

profile of v0, /device:TPU:0, one launch (start us, length us, event | category | flops | bytes accessed | tf_op | source)
XLA Modules:
  0.0 251.2 jit_solution(14037097235350133238)
XLA Ops:
  6.5 0.9 dynamic-slice_reduce_fusion.1
  7.4 0.9 and_reduce_fusion
  8.5 1.2 fusion.14
  9.7 13.5 %psum.7 = f32[256]{0:T(256)S(1)} all-reduce(f32[256]{0:T(256)S(1)} %fusion.14), channel_id=1, replica_groups=mesh['dp'=8,'expert'=4] {'expert'}, use_global_device_ids=true, to_apply=%region_1.2 | all-reduce | flops 256 | bytes 2048 | tf_op jit(solution)/shard_map/psum | solution.py:29
  23.2 1.2 fusion.15
  25.0 1.2 select_select_fusion
  26.2 3.5 %all-to-all-start = ((bf16[4,128,1024]{2,1,0:T(8,128)(2,1)}), bf16[4,128,1024]{2,1,0:T(8,128)(2,1)S(1)}, u32[]{:S(2)}, u32[]{:S(2)}) async-start(bf16[4,128,1024]{2,1,0:T(8,128)(2,1)} %select_select_fusion), calls=%async_computation | async-start | bytes 2097152 | tf_op jit(solution)/shard_map/all_to_all | solution.py:39
  29.8 23.8 %all-to-all-done = bf16[4,128,1024]{2,1,0:T(8,128)(2,1)S(1)} async-done(((bf16[4,128,1024]{2,1,0:T(8,128)(2,1)}), bf16[4,128,1024]{2,1,0:T(8,128)(2,1)S(1)}, u32[]{:S(2)}, u32[]{:S(2)}) %all-to-all-start) | async-done | bytes 1048608 | tf_op jit(solution)/shard_map/all_to_all | solution.py:39
  53.6 0.7 copy.27
  55.7 1.5 collective-permute-done
  57.3 0.9 add.73
  58.4 35.7 %all-gather.2.cloned.1.call-done = bf16[512,4096]{1,0:T(8,128)(2,1)} async-done(((bf16[64,4096]{1,0:T(8,128)(2,1)}), bf16[512,4096]{1,0:T(8,128)(2,1)}) %all-gather.2.cloned.1.call-update) | async-done | bytes 4194320 | tf_op jit(solution)/shard_map/all_gather | solution.py:47
  94.2 14.8 %fusion.2 = f32[512,1792]{1,0:T(8,128)} fusion(bf16[512,4096]{1,0:T(8,128)(2,1)} %all-gather.2.cloned.1.call-done, bf16[1,4096,1792]{2,1,0:T(8,128)(2,1)} %param.9), kind=kOutput, calls=%fused_computation.3 | convolution fusion | flops 7516192768 | bytes 22544384 | tf_op jit(solution)/shard_map/dot_general | solution.py:49
  109.0 28.6 %fusion.6 = bf16[512,4096]{1,0:T(8,128)(2,1)} fusion(bf16[1,1792,4096]{2,1,0:T(8,128)(2,1)} %param.10, f32[512,1792]{1,0:T(8,128)} %fusion.2, bf16[512,4096]{1,0:T(8,128)(2,1)} %all-gather.2.cloned.1.call-done, bf16[1,4096,1792]{2,1,0:T(8,128)(2,1)} %param.8), kind=kOutput, calls=%fused_computation.7 | convolution fusion | flops 15039987712 | bytes 41418752 | tf_op jit(solution)/shard_map/dot_general | solution.py:51
  137.6 51.5 %reduce-scatter.2.cloned.1.call-done = bf16[64,4096]{1,0:T(8,128)(2,1)} async-done(((bf16[512,4096]{1,0:T(8,128)(2,1)}), bf16[64,4096]{1,0:T(8,128)(2,1)}) %reduce-scatter.2.cloned.1.call-update) | async-done | bytes 524304 | tf_op jit(solution)/shard_map/reduce_scatter | solution.py:54
  189.1 4.9 %copy.30 = bf16[64,1,4096]{0,1,2:T(2,128)(2,1)S(1)} copy(bf16[64,1,4096]{2,0,1:T(8,128)(2,1)} %bitcast.36) | data formatting | bytes 1048576 | tf_op jit(solution)/shard_map/broadcast_in_dim | solution.py:60
  194.5 22.6 %reduce.9 = bf16[4096,64]{1,0:T(8,128)(2,1)S(1)} reduce(bf16[4096,1,64]{2,1,0:T(2,128)(2,1)S(1)} %bitcast.33, bf16[]{:T(256)} %broadcast.167), dimensions={1}, to_apply=%bitcast.27.reduce_sub_computation | reduce | bytes 1048578
  217.1 0.9 reshape.126
  218.0 18.9 %all_to_all.27 = bf16[4,2,32768]{2,1,0:T(2,128)(2,1)S(1)} all-to-all(bf16[4,2,32768]{2,1,0:T(2,128)(2,1)S(1)} %reshape.126), channel_id=1, replica_groups=mesh['dp'=8,'expert'=4] {'expert'}, dimensions={0} | all-to-all | bytes 1048576 | tf_op jit(solution)/shard_map/all_to_all | solution.py:60
  236.9 0.9 reshape.127
  237.8 2.3 copy.31
  240.7 1.7 collective-permute-done.1
  242.4 1.0 convolution_convert_fusion
  243.4 0.9 copy.32
  (20 shorter events, 3.6 us)
Async XLA Ops:
  6.5 234.0 %copy-start = (f32[4,4]{1,0:T(4,128)S(1)}, f32[4,4]{1,0:T(4,128)}, u32[]{:S(2)}) copy-start(f32[4,4]{1,0:T(4,128)} %param.13) | copy-start | bytes 196
  26.2 27.4 %all-to-all-start = ((bf16[4,128,1024]{2,1,0:T(8,128)(2,1)}), bf16[4,128,1024]{2,1,0:T(8,128)(2,1)S(1)}, u32[]{:S(2)}, u32[]{:S(2)}) async-start(bf16[4,128,1024]{2,1,0:T(8,128)(2,1)} %select_select_fusion), calls=%async_computation | async-start | bytes 2097152 | tf_op jit(solution)/shard_map/all_to_all | solution.py:39
  29.7 64.5 %all-gather.2.cloned.1.call-start = ((), (), s32[]{:S(2)}) async-start(), calls=%async_computation.3 | async-start | bytes 4718592 | tf_op jit(solution)/shard_map/all_gather | solution.py:47
  55.3 2.0 collective-permute-start
  58.2 130.9 %reduce-scatter.2.cloned.1.call-start = ((), (), s32[]{:S(2)}) async-start(), calls=%async_computation.4 | async-start | bytes 4718592 | tf_op jit(solution)/shard_map/reduce_scatter | solution.py:54
  240.5 2.0 collective-permute-start.1
Sparse Core Ops, SparseCore 0:
  58.3 35.8 all-gather.1
  137.7 51.3 reduce-scatter.1
where the time goes:
time: 252 us; the launch traced here: 251 us
  waiting for transfers between devices  114 us (45%)
  matrix products  44.4 us (18%)
  blocking collectives  32.3 us (13%)
  other arithmetic  28.2 us (11%)
  local copies, waits for them, and re-layouts  14.4 us (6%)
  between operations  13.6 us (5%)
  starting transfers between devices  3.92 us (2%)
    reduce_scatter x1, waiting for transfers between devices, on_device(): lax.psum_scatter(lax.optimization_barrier(partial_value).astype(jnp.float...  51.5 us
    all_gather x1, waiting for transfers between devices, on_device(): rows_piece = lax.all_gather(merged, 'dp', axis=0, tiled=True)  35.7 us
    dot_general x1, matrix products, on_device(): jnp.dot(hidden, down_weights, preferred_element_type=jnp.float32)  28.6 us
    all_to_all x1, waiting for transfers between devices, on_device(): lax.all_to_all(chosen, 'expert', split_axis=0, concat_axis=2, tiled=True)[0]  23.8 us
    unnamed x1, other arithmetic  22.6 us
    all_to_all x1, blocking collectives, on_device(): lax.all_to_all(summed[:, None, :], 'expert', split_axis=2, concat_axis=1,...  18.9 us
    dot_general x1, matrix products, on_device(): jnp.dot(rows_piece, up_weights, preferred_element_type=jnp.float32)  14.8 us
    psum x1, blocking collectives, on_device(): square_sums = lax.psum(jnp.sum(tokens_f32 * tokens_f32, axis=1), 'expert')  13.5 us
  transfers between devices with their start and end apart: 5, of which 5 were waited for; matrix products, arithmetic and copies ran while one was open for 0% of the time, Pallas kernels for 0%

commit v1 on v0

v1 whole, which is shorter than its diff:
```python
import functools

import jax
import jax.numpy as jnp
from jax import lax
from jax.experimental import pallas as pl
from jax.experimental.pallas import tpu as pltpu
from jax.sharding import PartitionSpec as P

BLOCK = 128
HALF = BLOCK // 2
VMEM_LIMIT = 40 * 1024 * 1024
GROUPS = ((0,), (1,), (2,), (3,))


def exchange(value, axis, offset):
    count = lax.axis_size(axis)
    return lax.ppermute(value, axis, [(i, i ^ offset) for i in range(count)])


def col_block(width, most):
    best = 128
    for size in range(128, most + 1, 128):
        if width % size == 0:
            best = size
    return best


def top_bit(value):
    return 1 << (value.bit_length() - 1)


def low_bit(value):
    return value & -value


def gather_pieces(own, chips):
    rows = own.shape[0] // 2
    got = {0: own}
    for j in range(1, chips):
        if top_bit(j) == j:
            got[j] = exchange(own, "dp", 2 * j)
    for j in range(1, chips):
        if top_bit(j) != j:
            top, low = top_bit(j), low_bit(j)
            first = exchange(got[j ^ top][:rows], "dp", 2 * top)
            second = exchange(got[j ^ low][rows:], "dp", 2 * low)
            got[j] = jnp.concatenate([first, second], axis=0)
    return jnp.concatenate([got[j] for j in range(chips)], axis=0)


def add_rounded(a, b):
    return (a.astype(jnp.float32) + b.astype(jnp.float32)).astype(jnp.bfloat16)


def scatter_pieces(sums, chips):
    rows = sums[0].shape[0] // 2
    halves = {j: [sums[j][:rows], sums[j][rows:]] for j in range(chips)}
    for j in range(chips - 1, 0, -1):
        if top_bit(j) != j:
            top, low = top_bit(j), low_bit(j)
            first = exchange(halves[j][0], "dp", 2 * top)
            second = exchange(halves[j][1], "dp", 2 * low)
            halves[j ^ top][0] = add_rounded(halves[j ^ top][0], first)
            halves[j ^ low][1] = add_rounded(halves[j ^ low][1], second)
    total = sums[0].astype(jnp.float32)
    for j in range(1, chips):
        if top_bit(j) == j:
            moved = exchange(jnp.concatenate(halves[j], axis=0), "dp", 2 * j)
            total = total + moved.astype(jnp.float32)
    return total.astype(jnp.bfloat16)


def gate_up_kernel(count, first, last, model_width, ids, *refs):
    x_refs = refs[: 2 * count]
    wg_refs = refs[2 * count : 3 * count]
    wu_refs = refs[3 * count : 4 * count]
    refs = refs[4 * count :]
    if not first:
        gate_in, up_in, squares_in = refs[:3]
        refs = refs[3:]
    if last:
        hidden_out, xs, squares = refs
    else:
        gate_out, up_out, squares_out, xs = refs
        squares = squares_out
    features = x_refs[0].shape[1]
    half = x_refs[0].shape[0]

    @pl.when(pl.program_id(0) == 0)
    def _():
        for c in range(count):
            for k in range(2):
                xs[k * half : (k + 1) * half, c * features : (c + 1) * features] = x_refs[2 * c + k][...]
        total = jnp.zeros((2 * half, 1), jnp.float32)
        for c in range(count):
            values = xs[:, c * features : (c + 1) * features].astype(jnp.float32)
            total = total + jnp.sum(values * values, axis=1, keepdims=True)
        total = jnp.broadcast_to(total, squares.shape)
        if not first:
            total = total + squares_in[...]
        squares[...] = total

    gate = None if first else gate_in[...]
    up = None if first else up_in[...]
    for c in range(count):
        part = xs[:, c * features : (c + 1) * features]
        dot_gate = jnp.dot(part, wg_refs[c][0], preferred_element_type=jnp.float32)
        dot_up = jnp.dot(part, wu_refs[c][0], preferred_element_type=jnp.float32)
        gate = dot_gate if gate is None else gate + dot_gate
        up = dot_up if up is None else up + dot_up
    if last:
        inv_rms = lax.rsqrt(squares[:, :1] / model_width + 1e-05)
        gate = gate * inv_rms
        hidden_out[...] = (gate / (1.0 + jnp.exp(-gate)) * (up * inv_rms)).astype(jnp.bfloat16)
    else:
        gate_out[...] = gate
        up_out[...] = up


def gate_up(ids, pieces, w_gate, w_up, carry, last, model_width):
    count = len(pieces)
    first = carry is None
    half, features = pieces[0][0].shape
    rows = 2 * half
    hid = w_gate.shape[2]
    block = col_block(hid, 256)
    whole = pl.BlockSpec((half, features), lambda j, s: (0, 0))
    weight = [
        pl.BlockSpec((1, features, block), functools.partial(lambda c, j, s: (0, s[c], j), c)) for c in range(count)
    ]
    acc = pl.BlockSpec((rows, block), lambda j, s: (0, j))
    sq = pl.BlockSpec((rows, 128), lambda j, s: (0, 0))
    acc_shape = jax.ShapeDtypeStruct((rows, hid), jnp.float32)
    sq_shape = jax.ShapeDtypeStruct((rows, 128), jnp.float32)
    in_specs = [whole] * (2 * count) + weight + weight + ([] if first else [acc, acc, sq])
    scratch = [pltpu.VMEM((rows, count * features), jnp.bfloat16)]
    if last:
        out_specs, out_shape = acc, jax.ShapeDtypeStruct((rows, hid), jnp.bfloat16)
        scratch.append(pltpu.VMEM((rows, 128), jnp.float32))
    else:
        out_specs, out_shape = [acc, acc, sq], [acc_shape, acc_shape, sq_shape]
    flat = [half_piece for piece in pieces for half_piece in piece]
    return pl.pallas_call(
        functools.partial(gate_up_kernel, count, first, last, model_width),
        grid_spec=pltpu.PrefetchScalarGridSpec(
            num_scalar_prefetch=1,
            grid=(hid // block,),
            in_specs=in_specs,
            out_specs=out_specs,
            scratch_shapes=scratch,
        ),
        out_shape=out_shape,
        cost_estimate=pl.CostEstimate(
            flops=4 * rows * features * count * hid,
            bytes_accessed=4 * features * count * hid,
            transcendentals=0,
        ),
        compiler_params=pltpu.CompilerParams(vmem_limit_bytes=VMEM_LIMIT),
    )(ids, *flat, *[w_gate] * count, *[w_up] * count, *(() if first else carry))


def down_kernel(ids, hidden, weight, mine, other):
    half = mine.shape[0]
    value = jnp.dot(hidden[...], weight[0], preferred_element_type=jnp.float32).astype(jnp.bfloat16)
    mine[...] = value[:half]
    other[...] = value[half:]


def down(ids, hidden, w_down, features):
    rows, hid = hidden.shape
    block = col_block(features, 256)
    steps = features // block
    out = pl.BlockSpec((rows // 2, block), lambda j, s: (0, j))
    shape = jax.ShapeDtypeStruct((rows // 2, features), jnp.bfloat16)
    return pl.pallas_call(
        down_kernel,
        grid_spec=pltpu.PrefetchScalarGridSpec(
            num_scalar_prefetch=1,
            grid=(steps,),
            in_specs=[
                pl.BlockSpec((rows, hid), lambda j, s: (0, 0)),
                pl.BlockSpec((1, hid, block), lambda j, s: (0, 0, s[0] * steps + j)),
            ],
            out_specs=[out, out],
        ),
        out_shape=[shape, shape],
        cost_estimate=pl.CostEstimate(
            flops=2 * rows * hid * features, bytes_accessed=2 * hid * features, transcendentals=0
        ),
        compiler_params=pltpu.CompilerParams(vmem_limit_bytes=VMEM_LIMIT),
    )(ids, hidden, w_down)


def select_kernel(count, sources, live, mine, other, *outs):
    here = mine.shape[0]
    for c in range(count):
        source = sources[c]
        keep = live[c] == 1

        @pl.when(keep & (source < here))
        def _():
            outs[c][...] = mine[jnp.minimum(source, here - 1)]

        @pl.when(keep & (source >= here))
        def _():
            outs[c][...] = other[jnp.maximum(source - here, 0)]

        @pl.when(jnp.logical_not(keep))
        def _():
            outs[c][...] = jnp.zeros_like(outs[c])


def select(sources, live, mine, other, count):
    whole = pl.BlockSpec(memory_space=pltpu.VMEM)
    scalars = pl.BlockSpec(memory_space=pltpu.SMEM)
    shape = jax.ShapeDtypeStruct(mine.shape[1:], jnp.bfloat16)
    return pl.pallas_call(
        functools.partial(select_kernel, count),
        in_specs=[scalars, scalars, whole, whole],
        out_specs=[whole] * count,
        out_shape=[shape] * count,
    )(sources, live, mine, other)


def combine_kernel(count, here, coefs, *refs):
    values = refs[:count]
    mine, other = refs[count:]
    for b in range(2 * here):
        total = None
        for c in range(count):
            term = coefs[c, b] * values[c][...].astype(jnp.float32)
            total = term if total is None else total + term
        target = mine if b < here else other
        target[b % here] = total.astype(jnp.bfloat16)


def combine(coefs, values, here):
    whole = pl.BlockSpec(memory_space=pltpu.VMEM)
    shape = jax.ShapeDtypeStruct((here,) + values[0].shape, jnp.bfloat16)
    return pl.pallas_call(
        functools.partial(combine_kernel, len(values), here),
        in_specs=[pl.BlockSpec(memory_space=pltpu.SMEM)] + [whole] * len(values),
        out_specs=[whole, whole],
        out_shape=[shape, shape],
    )(coefs, *values)


def on_device(tokens, w_gate, w_up, w_down, pick_block, pick_live, combine_weight):
    experts = lax.axis_size("expert")
    chips = lax.axis_size("dp") // 2
    features = tokens.shape[1]
    model_width = features * experts
    here = tokens.shape[0] // BLOCK
    row_index = lax.axis_index("dp")
    my_expert = lax.axis_index("expert")
    half_bit = row_index % 2
    pair_index = row_index // 2
    offsets = jnp.arange(experts, dtype=jnp.int32) ^ my_expert
    groups = GROUPS if experts == 4 else tuple((d,) for d in range(experts))

    picked = lax.dynamic_index_in_dim(pick_block, pair_index, axis=1, keepdims=False)[offsets]
    live = lax.dynamic_index_in_dim(pick_live, pair_index, axis=1, keepdims=False)[offsets]
    weight = lax.dynamic_index_in_dim(combine_weight, pair_index, axis=1, keepdims=False)[offsets]
    sources = jnp.bitwise_xor(picked // here, half_bit) * here + picked % here

    halves = tokens.reshape(here, 2, HALF, features)
    mine = lax.dynamic_index_in_dim(halves, half_bit, axis=1, keepdims=False)
    theirs = lax.dynamic_index_in_dim(halves, 1 - half_bit, axis=1, keepdims=False)
    other = exchange(theirs, "dp", 1)
    chosen = select(sources, live, mine, other, experts)

    arrived = [chosen[d] if d == 0 else exchange(chosen[d], "expert", d) for d in range(experts)]
    pieces = []
    for d in range(experts):
        gathered = gather_pieces(arrived[d], chips)
        pieces.append((gathered, exchange(gathered, "dp", 1)))
    carry = None
    for g, group in enumerate(groups):
        carry = gate_up(
            offsets[group[0] : group[-1] + 1],
            [pieces[d] for d in group],
            w_gate,
            w_up,
            carry,
            g == len(groups) - 1,
            model_width,
        )
    hidden = carry

    outputs = [None] * experts
    for d in range(experts - 1, -1, -1):
        kept, sent = down(offsets[d : d + 1], hidden, w_down, features)
        received = exchange(sent, "dp", 1)
        sums = add_rounded(kept, received).reshape(chips, HALF, features)
        total = scatter_pieces([sums[j] for j in range(chips)], chips)
        outputs[d] = total if d == 0 else exchange(total, "expert", d)

    slots = jnp.arange(2 * here, dtype=jnp.int32)
    coefs = jnp.where(
        (sources[:, None] == slots[None, :]) & (live[:, None] == 1), weight[:, None], jnp.zeros((), jnp.float32)
    )
    kept, sent = combine(coefs, outputs, here)
    received = exchange(sent, "dp", 1)
    first = jnp.where(half_bit == 0, kept, received)
    second = jnp.where(half_bit == 0, received, kept)
    return jnp.stack([first, second], axis=1).reshape(here * BLOCK, features)


def solution(mesh):
    in_specs = (
        P("dp", "expert"),
        P("expert", None, "dp"),
        P("expert", None, "dp"),
        P("expert", "dp", None),
        P(),
        P(),
        P(),
    )
    out_specs = P("dp", "expert")
    return jax.shard_map(
        on_device, mesh=mesh, in_specs=in_specs, out_specs=out_specs, check_vma=False
    )
```

time: 252 us -> 147 us (0.58)
  waiting for transfers between devices: 114 us -> 21.1 us
  Pallas kernels: 0 us -> 62.4 us
  matrix products: 44.4 us -> 0 us
  starting transfers between devices: 3.92 us -> 44.9 us
  blocking collectives: 32.3 us -> 0 us
  other arithmetic: 28.2 us -> 3.6 us
  between operations: 13.6 us -> 0.57 us
    pallas_call x0 -> x10, Pallas kernels: none -> 62.4 us  [the longest x4 37.7 us: gate_up(): pl.pallas_call(functools.partial(gate_up_kernel, count, first, last, mode...]
    reduce_scatter x1 -> x0, waiting for transfers between devices: 51.5 us -> none  [on_device(): lax.psum_scatter(lax.optimization_barrier(partial_value).astype(jnp.float...]
    ppermute x2 -> x48, starting transfers between devices: 0.14 us -> 44.9 us  [exchange(): return lax.ppermute(value, axis, [(i, i ^ offset) for i in range(count)])]
    dot_general x3 -> x0, matrix products: 44.4 us -> none  [the longest x1 28.6 us: on_device(): jnp.dot(hidden, down_weights, preferred_element_type=jnp.float32)]
    all_gather x1 -> x0, waiting for transfers between devices: 35.7 us -> none  [on_device(): rows_piece = lax.all_gather(merged, 'dp', axis=0, tiled=True)]
    all_to_all x1 -> x0, waiting for transfers between devices: 23.8 us -> none  [on_device(): lax.all_to_all(chosen, 'expert', split_axis=0, concat_axis=2, tiled=True)[0]]
    unnamed x1 -> x0, other arithmetic: 22.6 us -> none
    all_to_all x1 -> x0, blocking collectives: 18.9 us -> none  [on_device(): lax.all_to_all(summed[:, None, :], 'expert', split_axis=2, concat_axis=1,...]
  transfers between devices with their start and end apart: 5 -> 48, of which waited for: 5 -> 12; matrix products, arithmetic and copies ran while one was open for 0% -> 6% of each run, Pallas kernels for 0% -> 30%
where the time goes in v1:
time: 147 us; the launch traced here: 146 us
  Pallas kernels  62.4 us (42%)
  starting transfers between devices  44.9 us (31%)
  waiting for transfers between devices  21.1 us (14%)
  local copies, waits for them, and re-layouts  13.9 us (9%)
  other arithmetic  3.6 us (2%)
    ppermute x48, starting transfers between devices, exchange(): return lax.ppermute(value, axis, [(i, i ^ offset) for i in range(count)])  44.9 us
    pallas_call x4, Pallas kernels, gate_up(): pl.pallas_call(functools.partial(gate_up_kernel, count, first, last, mode...  37.7 us
    ppermute x48, waiting for transfers between devices, exchange(): return lax.ppermute(value, axis, [(i, i ^ offset) for i in range(count)])  21.1 us
    pallas_call x4, Pallas kernels, down(): pl.pallas_call(down_kernel, grid_spec=pltpu.PrefetchScalarGridSpec(num_sc...  20.6 us
    unnamed x36, local copies, waits for them, and re-layouts  6.62 us
  transfers between devices with their start and end apart: 48, of which 12 were waited for; matrix products, arithmetic and copies ran while one was open for 6% of the time, Pallas kernels for 30%

profile of v1, /device:TPU:0, one launch (start us, length us, event | category | flops | bytes accessed | tf_op | source)
XLA Modules:
  0.0 146.4 jit_solution(15224617813085650027)
XLA Ops:
  0.0 1.8 %dynamic-slice_bitcast_fusion = (bf16[2,64,1024]{2,1,0:T(8,128)(2,1)S(1)}, bf16[2,64,1024]{2,1,0:T(8,128)(2,1)}) fusion(bf16[2,2,64,1024]{3,2,1,0:T(8,128)(2,1)} %bitcast.16, s32[]{:T(128)S(6)} %select_n.81, s32[]{:T(128)S(6)} %select_n.80), kind=kLoop, calls=%fused_computation.14 | loop fusion | bytes 1048584 | tf_op jit(solution)/shard_map/jit(dynamic_index_in_dim)/squeeze | solution.py:269
  7.5 2.0 %shard_map.73 = (bf16[64,1024]{1,0:T(8,128)(2,1)}, bf16[64,1024]{1,0:T(8,128)(2,1)}, bf16[64,1024]{1,0:T(8,128)(2,1)}, bf16[64,1024]{1,0:T(8,128)(2,1)}) custom-call(s32[4]{0:T(128)} %copy-done.8, s32[4]{0:T(128)} %copy-done.9, bf16[2,64,1024]{2,1,0:T(8,128)(2,1)} %get-tuple-element.78.mine, bf16[2,64,1024]{2,1,0:T(8,128)(2,1)} %copy-done.4), custom_call_target="tpu_custom_call" | custom-call | tf_op jit(solution)/shard_map/pallas_call | solution.py:218
  9.4 2.5 %collective-permute-start.19 = (bf16[64,1024]{1,0:T(8,128)(2,1)}, bf16[64,1024]{1,0:T(8,128)(2,1)S(1)}, u32[]{:S(2)}, u32[]{:S(2)}) collective-permute-start(bf16[64,1024]{1,0:T(8,128)(2,1)} %get-tuple-element.31), channel_id=1, source_target_pairs={{0,8},{4,12},{8,0},{12,4},{16,24},{20,28},{24,16},{28,20},{1,9},{5... | collective-permute-start | bytes 393224 | tf_op jit(solution)/shard_map/ppermute | solution.py:18
  15.7 2.6 %collective-permute-start.7 = (bf16[64,1024]{1,0:T(8,128)(2,1)}, bf16[64,1024]{1,0:T(8,128)(2,1)S(1)}, u32[]{:S(2)}, u32[]{:S(2)}) collective-permute-start(bf16[64,1024]{1,0:T(8,128)(2,1)} %get-tuple-element.29), channel_id=1, source_target_pairs={{0,2},{1,3},{2,0},{3,1},{4,6},{5,7},{6,4},{7,5},{8,10},{9,11},{10,... | collective-permute-start | bytes 393224 | tf_op jit(solution)/shard_map/ppermute | solution.py:18
  20.5 1.7 %collective-permute-start.14 = (bf16[64,1024]{1,0:T(8,128)(2,1)S(1)}, bf16[64,1024]{1,0:T(8,128)(2,1)S(1)}, u32[]{:S(2)}, u32[]{:S(2)}) collective-permute-start(bf16[64,1024]{1,0:T(8,128)(2,1)S(1)} %collective-permute-done.13), channel_id=1, source_target_pairs={{0,8},{4,12},{8,0},{12,4},{16,24},{20,28},{24,16},{28,20},{1,9},{5... | collective-permute-start | bytes 393224 | tf_op jit(solution)/shard_map/ppermute | solution.py:18
  22.2 6.4 %collective-permute-done.7 = bf16[64,1024]{1,0:T(8,128)(2,1)S(1)} collective-permute-done((bf16[64,1024]{1,0:T(8,128)(2,1)}, bf16[64,1024]{1,0:T(8,128)(2,1)S(1)}, u32[]{:S(2)}, u32[]{:S(2)}) %collective-permute-start.7) | collective-permute-done | bytes 131104 | tf_op jit(solution)/shard_map/ppermute | solution.py:18
  41.1 1.9 %collective-permute-done.11 = bf16[32,1024]{1,0:T(8,128)(2,1)S(1)} collective-permute-done((bf16[32,1024]{1,0:T(8,128)(2,1)S(1)}, bf16[32,1024]{1,0:T(8,128)(2,1)S(1)}, u32[]{:S(2)}, u32[]{:S(2)}) %collective-permute-start.11) | collective-permute-done | bytes 65568 | tf_op jit(solution)/shard_map/ppermute | solution.py:18
  45.1 9.0 %shard_map.74 = (f32[512,1792]{1,0:T(8,128)S(1)}, f32[512,1792]{1,0:T(8,128)S(1)}, f32[512,128]{1,0:T(8,128)S(1)}) custom-call(s32[1]{0:T(128)} %get-tuple-element.82.ids, bf16[256,1024]{1,0:T(8,128)(2,1)S(1)} %constant_dynamic-update-slice_fusion.15.refs_0_, bf16[256,1024]{1,0:T(8,128)(2,1)S(1)} %collective-permute-done.23.refs_1_, ...), custom_call_target="tpu_custom_call" | custom-call | flops 3758096384 | bytes 7340032 | tf_op jit(solution)/shard_map/pallas_call | solution.py:144
  54.1 1.8 %copy-done.3 = f32[512,1792]{1,0:T(8,128)} copy-done((f32[512,1792]{1,0:T(8,128)}, f32[512,1792]{1,0:T(8,128)S(1)}, u32[]{:S(2)}) %copy-start.3) | copy-done | bytes 3670040
  55.9 9.8 %shard_map.75 = (f32[512,1792]{1,0:T(8,128)S(1)}, f32[512,1792]{1,0:T(8,128)S(1)}, f32[512,128]{1,0:T(8,128)S(1)}) custom-call(s32[1]{0:T(128)} %get-tuple-element.79.ids, bf16[256,1024]{1,0:T(8,128)(2,1)S(1)} %constant_dynamic-update-slice_fusion.10.refs_0_, bf16[256,1024]{1,0:T(8,128)(2,1)S(1)} %collective-permute-done.18.refs_1_, ...), custom_call_target="tpu_custom_call" | custom-call | flops 3758096384 | bytes 7340032 | tf_op jit(solution)/shard_map/pallas_call | solution.py:144
  65.7 1.8 %copy-done.2 = f32[512,1792]{1,0:T(8,128)} copy-done((f32[512,1792]{1,0:T(8,128)}, f32[512,1792]{1,0:T(8,128)S(1)}, u32[]{:S(2)}) %copy-start.2) | copy-done | bytes 3670040
  67.5 9.7 %shard_map.76 = (f32[512,1792]{1,0:T(8,128)S(1)}, f32[512,1792]{1,0:T(8,128)S(1)}, f32[512,128]{1,0:T(8,128)S(1)}) custom-call(s32[1]{0:T(128)} %get-tuple-element.80.ids, bf16[256,1024]{1,0:T(8,128)(2,1)S(1)} %constant_dynamic-update-slice_fusion.5.refs_0_, bf16[256,1024]{1,0:T(8,128)(2,1)S(1)} %collective-permute-done.12.refs_1_, ...), custom_call_target="tpu_custom_call" | custom-call | flops 3758096384 | bytes 7340032 | tf_op jit(solution)/shard_map/pallas_call | solution.py:144
  77.2 9.2 %shard_map.77.hidden = bf16[512,1792]{1,0:T(8,128)(2,1)S(1)} custom-call(s32[1]{0:T(128)} %get-tuple-element.81.ids, bf16[256,1024]{1,0:T(8,128)(2,1)S(1)} %constant_dynamic-update-slice_fusion.refs_0_, bf16[256,1024]{1,0:T(8,128)(2,1)S(1)} %collective-permute-done.6.refs_1_, bf16[1,4096,1792]{2,1,0:T(8,128)(2,1)} %refs_2_.7, ...), custom_call_target="tpu_custom_call" | custom-call | flops 3758096384 | bytes 7340032 | tf_op jit(solution)/shard_map/pallas_call | solution.py:144
  86.4 5.2 %shard_map.81 = (bf16[256,1024]{1,0:T(8,128)(2,1)S(1)}, bf16[256,1024]{1,0:T(8,128)(2,1)S(1)}) custom-call(s32[1]{0:T(128)} %get-tuple-element.81.ids, bf16[512,1792]{1,0:T(8,128)(2,1)S(1)} %shard_map.77.hidden, bf16[1,1792,4096]{2,1,0:T(8,128)(2,1)} %weight.7), custom_call_target="tpu_custom_call" | custom-call | flops 1879048192 | bytes 3670016 | tf_op jit(solution)/shard_map/pallas_call | solution.py:176
  92.1 5.1 %shard_map.80 = (bf16[256,1024]{1,0:T(8,128)(2,1)S(1)}, bf16[256,1024]{1,0:T(8,128)(2,1)S(1)}) custom-call(s32[1]{0:T(128)} %get-tuple-element.80.ids, bf16[512,1792]{1,0:T(8,128)(2,1)S(1)} %shard_map.77.hidden, bf16[1,1792,4096]{2,1,0:T(8,128)(2,1)} %weight.7), custom_call_target="tpu_custom_call" | custom-call | flops 1879048192 | bytes 3670016 | tf_op jit(solution)/shard_map/pallas_call | solution.py:176
  97.3 5.1 %shard_map.79 = (bf16[256,1024]{1,0:T(8,128)(2,1)S(1)}, bf16[256,1024]{1,0:T(8,128)(2,1)S(1)}) custom-call(s32[1]{0:T(128)} %get-tuple-element.79.ids, bf16[512,1792]{1,0:T(8,128)(2,1)S(1)} %shard_map.77.hidden, bf16[1,1792,4096]{2,1,0:T(8,128)(2,1)} %weight.7), custom_call_target="tpu_custom_call" | custom-call | flops 1879048192 | bytes 3670016 | tf_op jit(solution)/shard_map/pallas_call | solution.py:176
  102.5 5.2 %shard_map.78 = (bf16[256,1024]{1,0:T(8,128)(2,1)S(1)}, bf16[256,1024]{1,0:T(8,128)(2,1)S(1)}) custom-call(s32[1]{0:T(128)} %get-tuple-element.82.ids, bf16[512,1792]{1,0:T(8,128)(2,1)S(1)} %shard_map.77.hidden, bf16[1,1792,4096]{2,1,0:T(8,128)(2,1)} %weight.7), custom_call_target="tpu_custom_call" | custom-call | flops 1879048192 | bytes 3670016 | tf_op jit(solution)/shard_map/pallas_call | solution.py:176
  111.2 1.7 %collective-permute-start.38 = (bf16[32,1024]{1,0:T(8,128)(2,1)S(1)}, bf16[32,1024]{1,0:T(8,128)(2,1)S(1)}, u32[]{:S(2)}, u32[]{:S(2)}) collective-permute-start(bf16[32,1024]{1,0:T(8,128)(2,1)S(1)} %get-tuple-element.62), channel_id=1, source_target_pairs={{0,8},{4,12},{8,0},{12,4},{16,24},{20,28},{24,16},{28,20},{1,9},{5... | collective-permute-start | bytes 196616 | tf_op jit(solution)/shard_map/ppermute | solution.py:18
  116.0 1.8 %collective-permute-start.27 = (bf16[32,1024]{1,0:T(8,128)(2,1)S(1)}, bf16[32,1024]{1,0:T(8,128)(2,1)S(1)}, u32[]{:S(2)}, u32[]{:S(2)}) collective-permute-start(bf16[32,1024]{1,0:T(8,128)(2,1)S(1)} %get-tuple-element.74), channel_id=1, source_target_pairs={{0,8},{4,12},{8,0},{12,4},{16,24},{20,28},{24,16},{28,20},{1,9},{5... | collective-permute-start | bytes 196616 | tf_op jit(solution)/shard_map/ppermute | solution.py:18
  118.1 2.0 %collective-permute-start.45 = (bf16[64,1024]{1,0:T(8,128)(2,1)S(1)}, bf16[64,1024]{1,0:T(8,128)(2,1)S(1)}, u32[]{:S(2)}, u32[]{:S(2)}) collective-permute-start(bf16[64,1024]{1,0:T(8,128)(2,1)S(1)} %pad_maximum_fusion.8), channel_id=1, source_target_pairs={{0,16},{4,20},{8,24},{12,28},{16,0},{20,4},{24,8},{28,12},{1,17},{... | collective-permute-start | bytes 393224 | tf_op jit(solution)/shard_map/ppermute | solution.py:18
  128.6 2.7 %collective-permute-start.46 = (bf16[64,1024]{1,0:T(8,128)(2,1)S(1)}, bf16[64,1024]{1,0:T(8,128)(2,1)S(1)}, u32[]{:S(2)}, u32[]{:S(2)}) collective-permute-start(bf16[64,1024]{1,0:T(8,128)(2,1)S(1)} %add_convert_fusion.4), channel_id=1, source_target_pairs={{0,3},{1,2},{2,1},{3,0},{4,7},{5,6},{6,5},{7,4},{8,11},{9,10},{10,... | collective-permute-start | bytes 393224 | tf_op jit(solution)/shard_map/ppermute | solution.py:18
  135.5 3.8 %collective-permute-done.40.refs_2_ = bf16[64,1024]{1,0:T(8,128)(2,1)S(1)} collective-permute-done((bf16[64,1024]{1,0:T(8,128)(2,1)S(1)}, bf16[64,1024]{1,0:T(8,128)(2,1)S(1)}, u32[]{:S(2)}, u32[]{:S(2)}) %collective-permute-start.40) | collective-permute-done | bytes 131104 | tf_op jit(solution)/shard_map/ppermute | solution.py:18
  140.6 2.2 %shard_map.82 = (bf16[2,64,1024]{2,1,0:T(8,128)(2,1)}, bf16[2,64,1024]{2,1,0:T(8,128)(2,1)}) custom-call(f32[4,4]{1,0:T(4,128)} %fusion.1.coefs, bf16[64,1024]{1,0:T(8,128)(2,1)} %add_convert_fusion.7.refs_0_, bf16[64,1024]{1,0:T(8,128)(2,1)} %copy-done.7, bf16[64,1024]{1,0:T(8,128)(2,1)} %copy-done.6, bf16[64,1024]{1,0:T(8,128)(2,1)} %copy-done.5), custom_call_target="tpu_custom_call" | custom-call | tf_op jit(solution)/shard_map/pallas_call | solution.py:241
  142.8 1.7 %collective-permute-done.47 = bf16[2,64,1024]{2,1,0:T(8,128)(2,1)S(1)} collective-permute-done((bf16[2,64,1024]{2,1,0:T(8,128)(2,1)}, bf16[2,64,1024]{2,1,0:T(8,128)(2,1)S(1)}, u32[]{:S(2)}, u32[]{:S(2)}) %collective-permute-start.47) | collective-permute-done | bytes 262176 | tf_op jit(solution)/shard_map/ppermute | solution.py:18
  (171 shorter events, 49.1 us)
Async XLA Ops:
  9.4 10.0 %collective-permute-start.19 = (bf16[64,1024]{1,0:T(8,128)(2,1)}, bf16[64,1024]{1,0:T(8,128)(2,1)S(1)}, u32[]{:S(2)}, u32[]{:S(2)}) collective-permute-start(bf16[64,1024]{1,0:T(8,128)(2,1)} %get-tuple-element.31), channel_id=1, source_target_pairs={{0,8},{4,12},{8,0},{12,4},{16,24},{20,28},{24,16},{28,20},{1,9},{5... | collective-permute-start | bytes 393224 | tf_op jit(solution)/shard_map/ppermute | solution.py:18
  11.9 8.1 %collective-permute-start.20 = (bf16[64,1024]{1,0:T(8,128)(2,1)}, bf16[64,1024]{1,0:T(8,128)(2,1)S(1)}, u32[]{:S(2)}, u32[]{:S(2)}) collective-permute-start(bf16[64,1024]{1,0:T(8,128)(2,1)} %get-tuple-element.31), channel_id=1, source_target_pairs={{0,16},{4,20},{8,24},{12,28},{16,0},{20,4},{24,8},{28,12},{1,17},{... | collective-permute-start | bytes 393224 | tf_op jit(solution)/shard_map/ppermute | solution.py:18
  13.5 7.0 %collective-permute-start.13 = (bf16[64,1024]{1,0:T(8,128)(2,1)}, bf16[64,1024]{1,0:T(8,128)(2,1)S(1)}, u32[]{:S(2)}, u32[]{:S(2)}) collective-permute-start(bf16[64,1024]{1,0:T(8,128)(2,1)} %get-tuple-element.30), channel_id=1, source_target_pairs={{0,1},{1,0},{2,3},{3,2},{4,5},{5,4},{6,7},{7,6},{8,9},{9,8},{10,11... | collective-permute-start | bytes 393224 | tf_op jit(solution)/shard_map/ppermute | solution.py:18
  15.7 13.0 %collective-permute-start.7 = (bf16[64,1024]{1,0:T(8,128)(2,1)}, bf16[64,1024]{1,0:T(8,128)(2,1)S(1)}, u32[]{:S(2)}, u32[]{:S(2)}) collective-permute-start(bf16[64,1024]{1,0:T(8,128)(2,1)} %get-tuple-element.29), channel_id=1, source_target_pairs={{0,2},{1,3},{2,0},{3,1},{4,6},{5,7},{6,4},{7,5},{8,10},{9,11},{10,... | collective-permute-start | bytes 393224 | tf_op jit(solution)/shard_map/ppermute | solution.py:18
  18.3 10.9 %collective-permute-start.1 = (bf16[64,1024]{1,0:T(8,128)(2,1)}, bf16[64,1024]{1,0:T(8,128)(2,1)S(1)}, u32[]{:S(2)}, u32[]{:S(2)}) collective-permute-start(bf16[64,1024]{1,0:T(8,128)(2,1)} %get-tuple-element.28), channel_id=1, source_target_pairs={{0,3},{1,2},{2,1},{3,0},{4,7},{5,6},{6,5},{7,4},{8,11},{9,10},{10,... | collective-permute-start | bytes 393224 | tf_op jit(solution)/shard_map/ppermute | solution.py:18
  19.4 10.4 %collective-permute-start.21 = (bf16[32,1024]{1,0:T(8,128)(2,1)S(1)}, bf16[32,1024]{1,0:T(8,128)(2,1)S(1)}, u32[]{:S(2)}, u32[]{:S(2)}) collective-permute-start(bf16[32,1024]{1,0:T(8,128)(2,1)S(1)} %slice.240), channel_id=1, source_target_pairs={{0,16},{4,20},{8,24},{12,28},{16,0},{20,4},{24,8},{28,12},{1,17},{... | collective-permute-start | bytes 196616 | tf_op jit(solution)/shard_map/ppermute | solution.py:18
  20.0 11.4 %collective-permute-start.22 = (bf16[32,1024]{1,0:T(8,128)(2,1)S(1)}, bf16[32,1024]{1,0:T(8,128)(2,1)S(1)}, u32[]{:S(2)}, u32[]{:S(2)}) collective-permute-start(bf16[32,1024]{1,0:T(8,128)(2,1)S(1)} %slice.241), channel_id=1, source_target_pairs={{0,8},{4,12},{8,0},{12,4},{16,24},{20,28},{24,16},{28,20},{1,9},{5... | collective-permute-start | bytes 196616 | tf_op jit(solution)/shard_map/ppermute | solution.py:18
  20.5 12.5 %collective-permute-start.14 = (bf16[64,1024]{1,0:T(8,128)(2,1)S(1)}, bf16[64,1024]{1,0:T(8,128)(2,1)S(1)}, u32[]{:S(2)}, u32[]{:S(2)}) collective-permute-start(bf16[64,1024]{1,0:T(8,128)(2,1)S(1)} %collective-permute-done.13), channel_id=1, source_target_pairs={{0,8},{4,12},{8,0},{12,4},{16,24},{20,28},{24,16},{28,20},{1,9},{5... | collective-permute-start | bytes 393224 | tf_op jit(solution)/shard_map/ppermute | solution.py:18
  33.6 11.4 %collective-permute-start.23 = (bf16[256,1024]{1,0:T(8,128)(2,1)S(1)}, bf16[256,1024]{1,0:T(8,128)(2,1)S(1)}, u32[]{:S(2)}, u32[]{:S(2)}) collective-permute-start(bf16[256,1024]{1,0:T(8,128)(2,1)S(1)} %constant_dynamic-update-slice_fusion.15.refs_0_), channel_id=1, source_target_pairs={{0,4},{4,0},{8,12},{12,8},{16,20},{20,16},{24,28},{28,24},{1,5},{5... | collective-permute-start | bytes 1572872 | tf_op jit(solution)/shard_map/ppermute | solution.py:18
  41.0 14.9 %collective-permute-start.18 = (bf16[256,1024]{1,0:T(8,128)(2,1)S(1)}, bf16[256,1024]{1,0:T(8,128)(2,1)S(1)}, u32[]{:S(2)}, u32[]{:S(2)}) collective-permute-start(bf16[256,1024]{1,0:T(8,128)(2,1)S(1)} %constant_dynamic-update-slice_fusion.10.refs_0_), channel_id=1, source_target_pairs={{0,4},{4,0},{8,12},{12,8},{16,20},{20,16},{24,28},{28,24},{1,5},{5... | collective-permute-start | bytes 1572872 | tf_op jit(solution)/shard_map/ppermute | solution.py:18
  43.1 24.4 %collective-permute-start.12 = (bf16[256,1024]{1,0:T(8,128)(2,1)S(1)}, bf16[256,1024]{1,0:T(8,128)(2,1)S(1)}, u32[]{:S(2)}, u32[]{:S(2)}) collective-permute-start(bf16[256,1024]{1,0:T(8,128)(2,1)S(1)} %constant_dynamic-update-slice_fusion.5.refs_0_), channel_id=1, source_target_pairs={{0,4},{4,0},{8,12},{12,8},{16,20},{20,16},{24,28},{28,24},{1,5},{5... | collective-permute-start | bytes 1572872 | tf_op jit(solution)/shard_map/ppermute | solution.py:18
  45.0 32.2 %collective-permute-start.6 = (bf16[256,1024]{1,0:T(8,128)(2,1)S(1)}, bf16[256,1024]{1,0:T(8,128)(2,1)S(1)}, u32[]{:S(2)}, u32[]{:S(2)}) collective-permute-start(bf16[256,1024]{1,0:T(8,128)(2,1)S(1)} %constant_dynamic-update-slice_fusion.refs_0_), channel_id=1, source_target_pairs={{0,4},{4,0},{8,12},{12,8},{16,20},{20,16},{24,28},{28,24},{1,5},{5... | collective-permute-start | bytes 1572872 | tf_op jit(solution)/shard_map/ppermute | solution.py:18
  91.6 16.7 %collective-permute-start.41 = (bf16[256,1024]{1,0:T(8,128)(2,1)S(1)}, bf16[256,1024]{1,0:T(8,128)(2,1)S(1)}, u32[]{:S(2)}, u32[]{:S(2)}) collective-permute-start(bf16[256,1024]{1,0:T(8,128)(2,1)S(1)} %get-tuple-element.48), channel_id=1, source_target_pairs={{0,4},{4,0},{8,12},{12,8},{16,20},{20,16},{24,28},{28,24},{1,5},{5... | collective-permute-start | bytes 1572872 | tf_op jit(solution)/shard_map/ppermute | solution.py:18
  97.2 13.6 %collective-permute-start.35 = (bf16[256,1024]{1,0:T(8,128)(2,1)S(1)}, bf16[256,1024]{1,0:T(8,128)(2,1)S(1)}, u32[]{:S(2)}, u32[]{:S(2)}) collective-permute-start(bf16[256,1024]{1,0:T(8,128)(2,1)S(1)} %get-tuple-element.46), channel_id=1, source_target_pairs={{0,4},{4,0},{8,12},{12,8},{16,20},{20,16},{24,28},{28,24},{1,5},{5... | collective-permute-start | bytes 1572872 | tf_op jit(solution)/shard_map/ppermute | solution.py:18
  111.2 6.5 %collective-permute-start.38 = (bf16[32,1024]{1,0:T(8,128)(2,1)S(1)}, bf16[32,1024]{1,0:T(8,128)(2,1)S(1)}, u32[]{:S(2)}, u32[]{:S(2)}) collective-permute-start(bf16[32,1024]{1,0:T(8,128)(2,1)S(1)} %get-tuple-element.62), channel_id=1, source_target_pairs={{0,8},{4,12},{8,0},{12,4},{16,24},{20,28},{24,16},{28,20},{1,9},{5... | collective-permute-start | bytes 196616 | tf_op jit(solution)/shard_map/ppermute | solution.py:18
  118.1 7.7 %collective-permute-start.45 = (bf16[64,1024]{1,0:T(8,128)(2,1)S(1)}, bf16[64,1024]{1,0:T(8,128)(2,1)S(1)}, u32[]{:S(2)}, u32[]{:S(2)}) collective-permute-start(bf16[64,1024]{1,0:T(8,128)(2,1)S(1)} %pad_maximum_fusion.8), channel_id=1, source_target_pairs={{0,16},{4,20},{8,24},{12,28},{16,0},{20,4},{24,8},{28,12},{1,17},{... | collective-permute-start | bytes 393224 | tf_op jit(solution)/shard_map/ppermute | solution.py:18
  120.2 6.9 %collective-permute-start.37 = (bf16[64,1024]{1,0:T(8,128)(2,1)S(1)}, bf16[64,1024]{1,0:T(8,128)(2,1)S(1)}, u32[]{:S(2)}, u32[]{:S(2)}) collective-permute-start(bf16[64,1024]{1,0:T(8,128)(2,1)S(1)} %pad_maximum_fusion.5), channel_id=1, source_target_pairs={{0,8},{4,12},{8,0},{12,4},{16,24},{20,28},{24,16},{28,20},{1,9},{5... | collective-permute-start | bytes 393224 | tf_op jit(solution)/shard_map/ppermute | solution.py:18
  121.5 7.2 %collective-permute-start.39 = (bf16[64,1024]{1,0:T(8,128)(2,1)S(1)}, bf16[64,1024]{1,0:T(8,128)(2,1)S(1)}, u32[]{:S(2)}, u32[]{:S(2)}) collective-permute-start(bf16[64,1024]{1,0:T(8,128)(2,1)S(1)} %pad_maximum_fusion.6), channel_id=1, source_target_pairs={{0,16},{4,20},{8,24},{12,28},{16,0},{20,4},{24,8},{28,12},{1,17},{... | collective-permute-start | bytes 393224 | tf_op jit(solution)/shard_map/ppermute | solution.py:18
  122.1 9.3 %collective-permute-start.31 = (bf16[64,1024]{1,0:T(8,128)(2,1)S(1)}, bf16[64,1024]{1,0:T(8,128)(2,1)S(1)}, u32[]{:S(2)}, u32[]{:S(2)}) collective-permute-start(bf16[64,1024]{1,0:T(8,128)(2,1)S(1)} %pad_maximum_fusion.3), channel_id=1, source_target_pairs={{0,8},{4,12},{8,0},{12,4},{16,24},{20,28},{24,16},{28,20},{1,9},{5... | collective-permute-start | bytes 393224 | tf_op jit(solution)/shard_map/ppermute | solution.py:18
  124.2 8.2 %collective-permute-start.33 = (bf16[64,1024]{1,0:T(8,128)(2,1)S(1)}, bf16[64,1024]{1,0:T(8,128)(2,1)S(1)}, u32[]{:S(2)}, u32[]{:S(2)}) collective-permute-start(bf16[64,1024]{1,0:T(8,128)(2,1)S(1)} %pad_maximum_fusion.4), channel_id=1, source_target_pairs={{0,16},{4,20},{8,24},{12,28},{16,0},{20,4},{24,8},{28,12},{1,17},{... | collective-permute-start | bytes 393224 | tf_op jit(solution)/shard_map/ppermute | solution.py:18
  125.8 7.5 %collective-permute-start.26 = (bf16[64,1024]{1,0:T(8,128)(2,1)S(1)}, bf16[64,1024]{1,0:T(8,128)(2,1)S(1)}, u32[]{:S(2)}, u32[]{:S(2)}) collective-permute-start(bf16[64,1024]{1,0:T(8,128)(2,1)S(1)} %pad_maximum_fusion.1), channel_id=1, source_target_pairs={{0,8},{4,12},{8,0},{12,4},{16,24},{20,28},{24,16},{28,20},{1,9},{5... | collective-permute-start | bytes 393224 | tf_op jit(solution)/shard_map/ppermute | solution.py:18
  128.6 6.9 %collective-permute-start.46 = (bf16[64,1024]{1,0:T(8,128)(2,1)S(1)}, bf16[64,1024]{1,0:T(8,128)(2,1)S(1)}, u32[]{:S(2)}, u32[]{:S(2)}) collective-permute-start(bf16[64,1024]{1,0:T(8,128)(2,1)S(1)} %add_convert_fusion.4), channel_id=1, source_target_pairs={{0,3},{1,2},{2,1},{3,0},{4,7},{5,6},{6,5},{7,4},{8,11},{9,10},{10,... | collective-permute-start | bytes 393224 | tf_op jit(solution)/shard_map/ppermute | solution.py:18
  131.4 7.8 %collective-permute-start.40 = (bf16[64,1024]{1,0:T(8,128)(2,1)S(1)}, bf16[64,1024]{1,0:T(8,128)(2,1)S(1)}, u32[]{:S(2)}, u32[]{:S(2)}) collective-permute-start(bf16[64,1024]{1,0:T(8,128)(2,1)S(1)} %add_convert_fusion.5), channel_id=1, source_target_pairs={{0,2},{1,3},{2,0},{3,1},{4,6},{5,7},{6,4},{7,5},{8,10},{9,11},{10,... | collective-permute-start | bytes 393224 | tf_op jit(solution)/shard_map/ppermute | solution.py:18
  132.5 6.8 %collective-permute-start.34 = (bf16[64,1024]{1,0:T(8,128)(2,1)S(1)}, bf16[64,1024]{1,0:T(8,128)(2,1)S(1)}, u32[]{:S(2)}, u32[]{:S(2)}) collective-permute-start(bf16[64,1024]{1,0:T(8,128)(2,1)S(1)} %add_convert_fusion.6), channel_id=1, source_target_pairs={{0,1},{1,0},{2,3},{3,2},{4,5},{5,4},{6,7},{7,6},{8,9},{9,8},{10,11... | collective-permute-start | bytes 393224 | tf_op jit(solution)/shard_map/ppermute | solution.py:18
  (34 other events, 164.6 us)

commit v2 on v0

v2 whole, which is shorter than its diff:
```python
import functools

import jax
import jax.numpy as jnp
from jax import lax
from jax.experimental import pallas as pl
from jax.experimental.pallas import tpu as pltpu
from jax.sharding import PartitionSpec as P

BLOCK = 128
HALF = BLOCK // 2
MIB = 1024 * 1024
UP_GROUPS = ((0, 1), (2, 3))
DOWN_GROUPS = ((3,), (2,), (1,), (0,))
VMEM = pl.BlockSpec(memory_space=pltpu.VMEM)
SMEM = pl.BlockSpec(memory_space=pltpu.SMEM)
ANY = pl.BlockSpec(memory_space=pl.ANY)
HBM = pl.BlockSpec(memory_space=pltpu.HBM)


def in_hbm(value):
    return pltpu.with_memory_space_constraint(value, pltpu.HBM)


def params(mib):
    return pltpu.CompilerParams(vmem_limit_bytes=mib * MIB)


def exchange(value, axis, offset):
    count = lax.axis_size(axis)
    return lax.ppermute(value, axis, [(i, i ^ offset) for i in range(count)])


def hop(value, step, steps):
    count = lax.axis_size("dp")
    turn = [i ^ (2 << (step if i % 2 == 0 else steps - 1 - step)) for i in range(count)]
    return lax.ppermute(value, "dp", list(enumerate(turn)))


def hop_and_join(value, step, steps):
    return jnp.concatenate([value, hop(value, step, steps)], axis=0)


def after(value, *others):
    return lax.optimization_barrier((value,) + others)[0]


def as_f32(value):
    return value.astype(jnp.float32)


def upper_rows(terms):
    rows = terms[0].shape[0] // 2
    return sum(as_f32(term[rows:]) for term in terms).astype(jnp.bfloat16)


def lower_rows(terms):
    return [term[: term.shape[0] // 2] for term in terms]


def select_kernel(count, pick_block, pick_live, mine, other, *outs):
    here = mine.shape[0] // BLOCK
    expert = lax.axis_index("expert")
    row = lax.axis_index("dp")
    half = row % 2
    for c in range(count):
        picked = pick_block[expert ^ c, row // 2]
        live = pick_live[expert ^ c, row // 2] == 1
        rows = pl.ds(pl.multiple_of((picked % here) * BLOCK + half * HALF, HALF), HALF)
        near = picked // here == half

        @pl.when(live & near)
        def _():
            outs[c][...] = mine[rows, :]

        @pl.when(live & jnp.logical_not(near))
        def _():
            outs[c][...] = other[rows, :]

        @pl.when(jnp.logical_not(live))
        def _():
            outs[c][...] = jnp.zeros_like(outs[c])


def select(pick_block, pick_live, mine, other, count):
    shape = jax.ShapeDtypeStruct((HALF, mine.shape[1]), jnp.bfloat16)
    return pl.pallas_call(
        functools.partial(select_kernel, count),
        in_specs=[SMEM, SMEM, VMEM, VMEM],
        out_specs=[VMEM] * count,
        out_shape=[shape] * count,
        compiler_params=params(6),
    )(pick_block, pick_live, mine, other)


def marker_kernel(*refs):
    refs[-1][...] = jnp.zeros_like(refs[-1])


def marker(flops, *values):
    return pl.pallas_call(
        marker_kernel,
        in_specs=[ANY] * len(values),
        out_specs=VMEM,
        out_shape=jax.ShapeDtypeStruct((8, 128), jnp.float32),
        cost_estimate=pl.CostEstimate(flops=flops, bytes_accessed=0, transcendentals=0),
        compiler_params=params(1),
    )(*values)


def gate_kernel(*refs):
    pass


def gate(value, *others):
    return pl.pallas_call(
        gate_kernel,
        in_specs=[ANY] * (1 + len(others)),
        out_specs=ANY,
        out_shape=jax.ShapeDtypeStruct(value.shape, value.dtype),
        input_output_aliases={0: 0},
        cost_estimate=pl.CostEstimate(flops=0, bytes_accessed=0, transcendentals=0),
        compiler_params=params(1),
    )(value, *others)


def row_copies(offset, place, features, weight, out, sem):
    begin = pl.multiple_of((lax.axis_index("expert") ^ offset) * features, features)
    target = out.at[pl.ds(place * features, features)]
    return [pltpu.make_async_copy(weight.at[0, pl.ds(begin, features)], target, sem)]


def fetch_kernel(group, features, weight, out, sem):
    copies = []
    for c, offset in enumerate(group):
        copies += row_copies(offset, c, features, weight, out, sem.at[c])
    for copy in copies:
        copy.start()
    for copy in copies:
        copy.wait()


def fetch_rows(group, weight, features):
    rows = len(group) * features
    hid = weight.shape[2]
    return pl.pallas_call(
        functools.partial(fetch_kernel, group, features),
        in_specs=[HBM],
        out_specs=VMEM,
        out_shape=pltpu.VMEM((rows, hid), jnp.bfloat16),
        scratch_shapes=[pltpu.SemaphoreType.DMA((len(group),))],
        cost_estimate=pl.CostEstimate(flops=0, bytes_accessed=0, transcendentals=0),
        compiler_params=params(4),
    )(in_hbm(weight))


def gate_up_kernel(count, parts, first, last, model_width, *refs):
    sources, (w_gate, w_up), refs = refs[: 2 * parts], refs[2 * parts : 2 * parts + 2], refs[2 * parts + 2 :]
    features = sources[0].shape[1]
    if not first:
        gate_in, up_in, squares_in = refs[:3]
        refs = refs[3:]
    if last:
        hidden_out, xs, squares = refs
    else:
        gate_out, up_out, squares, xs = refs
    total = jnp.zeros((xs.shape[0], 1), jnp.float32)
    for c in range(count):
        columns = slice(c * features, (c + 1) * features)
        place = 0
        for source in sources:
            for j in range(source.shape[0] // (count * HALF)):
                begin = (j * count + c) * HALF
                xs[place : place + HALF, columns] = source[begin : begin + HALF, :]
                place += HALF
        values = as_f32(xs[:, columns])
        total = total + jnp.sum(values * values, axis=1, keepdims=True)
    total = jnp.broadcast_to(total, squares.shape)
    squares[...] = total if first else total + squares_in[...]
    if last:
        inv_rms = lax.rsqrt(squares[:, :1] / model_width + 1e-05)
    hid = w_gate.shape[1]
    block = next(size for size in (256, 128) if hid % size == 0)

    for b in range(hid // block):
        cols = slice(b * block, (b + 1) * block)
        gate = None if first else gate_in[:, cols]
        up = None if first else up_in[:, cols]
        for c in range(count):
            part = xs[:, c * features : (c + 1) * features]
            rows = slice(c * features, (c + 1) * features)
            dot_gate = jnp.dot(part, w_gate[rows, cols], preferred_element_type=jnp.float32)
            dot_up = jnp.dot(part, w_up[rows, cols], preferred_element_type=jnp.float32)
            gate = dot_gate if gate is None else gate + dot_gate
            up = dot_up if up is None else up + dot_up
        if last:
            gate = gate * inv_rms
            hidden_out[:, cols] = (gate / (1.0 + jnp.exp(-gate)) * (up * inv_rms)).astype(jnp.bfloat16)
        else:
            gate_out[:, cols] = gate
            up_out[:, cols] = up


def gate_up(count, mine, theirs, gate_rows, up_rows, carry, last, model_width):
    first = carry is None
    features = mine[0].shape[1]
    rows = sum(part.shape[0] for part in mine + theirs) // count
    hid = gate_rows.shape[1]
    acc = pltpu.VMEM((rows, hid), jnp.float32)
    scratch = [pltpu.VMEM((rows, count * features), jnp.bfloat16)]
    operands = mine + theirs + [gate_rows, up_rows] + list(carry or ())
    if last:
        out_shape = jax.ShapeDtypeStruct((rows, hid), jnp.bfloat16)
        scratch.append(pltpu.VMEM((rows, 128), jnp.float32))
    else:
        out_shape = [acc, acc, pltpu.VMEM((rows, 128), jnp.float32)]
    return pl.pallas_call(
        functools.partial(gate_up_kernel, count, len(mine), first, last, model_width),
        in_specs=[VMEM] * len(operands),
        out_specs=VMEM if last else [VMEM] * 3,
        out_shape=out_shape,
        scratch_shapes=scratch,
        input_output_aliases={} if first or last else {len(operands) - 3 + i: i for i in range(3)},
        cost_estimate=pl.CostEstimate(
            flops=4 * rows * features * count * hid,
            bytes_accessed=4 * features * count * hid,
            transcendentals=0,
        ),
        compiler_params=params(8),
    )(*operands)


def down_kernel(group, features, hidden, weight, mine, other):
    half = mine.shape[0] // len(group)
    expert = lax.axis_index("expert")
    block = next(size for size in (512, 256, 128) if features % size == 0)
    for c, offset in enumerate(group):
        for b in range(features // block):
            begin = pl.multiple_of((expert ^ offset) * features + b * block, block)
            value = jnp.dot(hidden[...], weight[0, :, pl.ds(begin, block)], preferred_element_type=jnp.float32)
            value = value.astype(jnp.bfloat16)
            cols = slice(c * features + b * block, c * features + (b + 1) * block)
            mine[:, cols] = value[:half]
            other[:, cols] = value[half:]


def down(group, hidden, w_down, features):
    rows, hid = hidden.shape
    width = len(group) * features
    shape = jax.ShapeDtypeStruct((rows // 2, width), jnp.bfloat16)
    return pl.pallas_call(
        functools.partial(down_kernel, group, features),
        in_specs=[VMEM, VMEM],
        out_specs=[VMEM, VMEM],
        out_shape=[shape, shape],
        cost_estimate=pl.CostEstimate(
            flops=2 * rows * hid * width, bytes_accessed=2 * hid * width, transcendentals=0
        ),
        compiler_params=params(8),
    )(hidden, w_down)


def combine_kernel(count, here, pick_block, pick_live, combine_weight, *refs):
    values = refs[:count]
    mine, other = refs[count:]
    expert = lax.axis_index("expert")
    row = lax.axis_index("dp")
    pair = row // 2
    half = row % 2
    for b in range(2 * here):
        slot = (half if b < here else 1 - half) * here + b % here
        total = None
        for c in range(count):
            taken = (pick_live[expert ^ c, pair] == 1) & (pick_block[expert ^ c, pair] == slot)
            coef = jnp.where(taken, combine_weight[expert ^ c, pair], jnp.float32(0))
            term = coef * as_f32(values[c][...])
            total = term if total is None else total + term
        target = mine if b < here else other
        target[b % here] = total.astype(jnp.bfloat16)


def combine(pick_block, pick_live, combine_weight, values, here):
    shape = jax.ShapeDtypeStruct((here,) + values[0].shape, jnp.bfloat16)
    return pl.pallas_call(
        functools.partial(combine_kernel, len(values), here),
        in_specs=[SMEM] * 3 + [VMEM] * len(values),
        out_specs=[VMEM, VMEM],
        out_shape=[shape, shape],
        compiler_params=params(6),
    )(pick_block, pick_live, combine_weight, *values)


def assemble_kernel(kept, received, out):
    half = lax.axis_index("dp") % 2
    for b in range(kept.shape[0]):
        out[pl.ds(pl.multiple_of(b * BLOCK + half * HALF, HALF), HALF), :] = kept[b]
        out[pl.ds(pl.multiple_of(b * BLOCK + (1 - half) * HALF, HALF), HALF), :] = received[b]


def assemble(kept, received):
    here, _, features = kept.shape
    return pl.pallas_call(
        assemble_kernel,
        in_specs=[VMEM, VMEM],
        out_specs=VMEM,
        out_shape=jax.ShapeDtypeStruct((here * BLOCK, features), jnp.bfloat16),
        compiler_params=params(6),
    )(kept, received)


def on_device(tokens, w_gate, w_up, w_down, pick_block, pick_live, combine_weight):
    experts = lax.axis_size("expert")
    steps = (lax.axis_size("dp") // 2).bit_length() - 1
    features = tokens.shape[1]
    model_width = features * experts
    here = tokens.shape[0] // BLOCK
    up_groups = UP_GROUPS if experts == 4 else tuple((d, d + 1) for d in range(0, experts, 2))
    down_groups = DOWN_GROUPS if experts == 4 else tuple((d,) for d in range(experts - 1, -1, -1))

    chosen = select(pick_block, pick_live, tokens, exchange(tokens, "dp", 1), experts)
    arrived = [chosen[d] if d == 0 else exchange(chosen[d], "expert", d) for d in range(experts)]
    own = [jnp.concatenate([arrived[d] for d in group], axis=0) for group in up_groups]
    token = marker(3000000000, *(arrived[d] for group in up_groups[1:] for d in group))
    gate_rows, up_rows, joined, mine, theirs = [], [], [], [], []
    for g, group in enumerate(up_groups):
        if g == 0:
            gate_rows.append(fetch_rows(group, after(w_gate, chosen[0]), features))
            own[g] = after(own[g], gate_rows[g])
        up_rows.append(fetch_rows(group, after(w_up, own[g], *joined[-1:]), features))
        if g + 1 < len(up_groups):
            gate_rows.append(fetch_rows(up_groups[g + 1], after(w_gate, up_rows[g]), features))
        value = own[g]
        for step in range(steps - 1):
            value = hop_and_join(value, step, steps)
        if g == 0:
            value = gate(value, token)
        joined.append(after(value, up_rows[g], gate_rows[-1]))
    for g in range(len(up_groups)):
        last_hop = hop(joined[g], steps - 1, steps)
        if g + 1 < len(up_groups):
            whole = jnp.concatenate([joined[g], last_hop], axis=0)
            whole = after(whole, joined[g + 1])
            mine.append([whole])
            theirs.append([exchange(whole, "dp", 1)])
        else:
            mine.append([joined[g], last_hop])
            theirs.append([exchange(joined[g], "dp", 1)])
    carry = None
    for g, group in enumerate(up_groups):
        last = g == len(up_groups) - 1
        if last:
            mine[g][1] = after(mine[g][1], carry[2])
            theirs[g].append(exchange(mine[g][1], "dp", 1))
        carry = gate_up(len(group), mine[g], theirs[g], gate_rows[g], up_rows[g], carry, last, model_width)
    hidden = carry

    terms, firsts = [], []
    for i, group in enumerate(down_groups):
        ready = hidden if i < 2 else after(hidden, firsts[i - 2])
        kept, sent = down(group, ready, w_down, features)
        terms.append([kept, exchange(sent, "dp", 1)])
        firsts.append(upper_rows(terms[i]))
    outputs = [None] * experts
    for i, group in enumerate(down_groups):
        sent = firsts[i]
        for step in range(steps - 1, -1, -1):
            if step < steps - 1:
                sent = upper_rows(terms[i])
                if step == 0 and i + 2 < len(firsts):
                    sent = after(sent, firsts[i + 2])
            terms[i] = lower_rows(terms[i]) + [hop(sent, step, steps)]
        total = sum(as_f32(term) for term in terms[i]).astype(jnp.bfloat16)
        for c, d in enumerate(group):
            value = total[:, c * features : (c + 1) * features]
            outputs[d] = value if d == 0 else exchange(value, "expert", d)

    kept, sent = combine(pick_block, pick_live, combine_weight, outputs, here)
    return assemble(kept, exchange(sent, "dp", 1))


def solution(mesh):
    in_specs = (
        P("dp", "expert"),
        P("expert", None, "dp"),
        P("expert", None, "dp"),
        P("expert", "dp", None),
        P(),
        P(),
        P(),
    )
    out_specs = P("dp", "expert")
    return jax.shard_map(
        on_device, mesh=mesh, in_specs=in_specs, out_specs=out_specs, check_vma=False
    )
```

time: 252 us -> 97 us (0.38)
  waiting for transfers between devices: 114 us -> 26.3 us
  matrix products: 44.4 us -> 0 us
  Pallas kernels: 0 us -> 40 us
  blocking collectives: 32.3 us -> 0 us
  other arithmetic: 28.2 us -> 0.94 us
  starting transfers between devices: 3.92 us -> 26.8 us
  between operations: 13.6 us -> 0.33 us
  local copies, waits for them, and re-layouts: 14.4 us -> 2.45 us
    reduce_scatter x1 -> x0, waiting for transfers between devices: 51.5 us -> none  [on_device(): lax.psum_scatter(lax.optimization_barrier(partial_value).astype(jnp.float...]
    dot_general x3 -> x0, matrix products: 44.4 us -> none  [the longest x1 28.6 us: on_device(): jnp.dot(hidden, down_weights, preferred_element_type=jnp.float32)]
    pallas_call x0 -> x15, Pallas kernels: none -> 40 us  [the longest x2 16.2 us: gate_up(): pl.pallas_call(functools.partial(gate_up_kernel, count, len(mine), first,...]
    all_gather x1 -> x0, waiting for transfers between devices: 35.7 us -> none  [on_device(): rows_piece = lax.all_gather(merged, 'dp', axis=0, tiled=True)]
    ppermute x2 -> x27, starting transfers between devices: 0.14 us -> 26.8 us  [the longest x15 14.7 us: exchange(): return lax.ppermute(value, axis, [(i, i ^ offset) for i in range(count)])]
    all_to_all x1 -> x0, waiting for transfers between devices: 23.8 us -> none  [on_device(): lax.all_to_all(chosen, 'expert', split_axis=0, concat_axis=2, tiled=True)[0]]
    ppermute x2 -> x27, waiting for transfers between devices: 3.22 us -> 26.3 us  [the longest x12 14.8 us: hop(): return lax.ppermute(value, 'dp', list(enumerate(turn)))]
    unnamed x1, other arithmetic: 22.6 us -> 0.01 us
  transfers between devices with their start and end apart: 5 -> 27, of which waited for: 5 -> 12; matrix products, arithmetic and copies ran while one was open for 0% -> 1% of each run, Pallas kernels for 0% -> 28%
where the time goes in v2:
time: 97 us; the launch traced here: 96.8 us
  Pallas kernels  40 us (41%)
  starting transfers between devices  26.8 us (28%)
  waiting for transfers between devices  26.3 us (27%)
  local copies, waits for them, and re-layouts  2.45 us (3%)
    pallas_call x2, Pallas kernels, gate_up(): pl.pallas_call(functools.partial(gate_up_kernel, count, len(mine), first,...  16.2 us
    ppermute x12, waiting for transfers between devices, hop(): return lax.ppermute(value, 'dp', list(enumerate(turn)))  14.8 us
    ppermute x15, starting transfers between devices, exchange(): return lax.ppermute(value, axis, [(i, i ^ offset) for i in range(count)])  14.7 us
    pallas_call x4, Pallas kernels, fetch_rows(): pl.pallas_call(functools.partial(fetch_kernel, group, features), in_specs...  12.7 us
    ppermute x12, starting transfers between devices, hop(): return lax.ppermute(value, 'dp', list(enumerate(turn)))  12.1 us
    ppermute x15, waiting for transfers between devices, exchange(): return lax.ppermute(value, axis, [(i, i ^ offset) for i in range(count)])  11.5 us
    pallas_call x4, Pallas kernels, down(): pl.pallas_call(functools.partial(down_kernel, group, features), in_specs=...  8.49 us
    unnamed x21, local copies, waits for them, and re-layouts  2.44 us
  transfers between devices with their start and end apart: 27, of which 12 were waited for; matrix products, arithmetic and copies ran while one was open for 1% of the time, Pallas kernels for 28%

profile of v2, /device:TPU:0, one launch (start us, length us, event | category | flops | bytes accessed | tf_op | source)
XLA Modules:
  0.0 96.8 jit_solution(9513461897333532047)
XLA Ops:
  0.5 1.7 %collective-permute-done.other = bf16[256,1024]{1,0:T(8,128)(2,1)S(1)} collective-permute-done((bf16[256,1024]{1,0:T(8,128)(2,1)}, bf16[256,1024]{1,0:T(8,128)(2,1)S(1)}, u32[]{:S(2)}, u32[]{:S(2)}) %collective-permute-start) | collective-permute-done | bytes 524320 | tf_op jit(solution)/shard_map/ppermute | solution.py:31
  5.4 3.0 %collective-permute-start.4 = (bf16[64,1024]{1,0:T(8,128)(2,1)S(1)}, bf16[64,1024]{1,0:T(8,128)(2,1)S(1)}, u32[]{:S(2)}, u32[]{:S(2)}) collective-permute-start(bf16[64,1024]{1,0:T(8,128)(2,1)S(1)} %get-tuple-element.38), channel_id=1, source_target_pairs={{0,1},{1,0},{2,3},{3,2},{4,5},{5,4},{6,7},{7,6},{8,9},{9,8},{10,11... | collective-permute-start | bytes 393224 | tf_op jit(solution)/shard_map/ppermute | solution.py:31
  8.4 2.6 %collective-permute-start.1 = (bf16[64,1024]{1,0:T(8,128)(2,1)S(1)}, bf16[64,1024]{1,0:T(8,128)(2,1)S(1)}, u32[]{:S(2)}, u32[]{:S(2)}) collective-permute-start(bf16[64,1024]{1,0:T(8,128)(2,1)S(1)} %get-tuple-element.35), channel_id=1, source_target_pairs={{0,2},{1,3},{2,0},{3,1},{4,6},{5,7},{6,4},{7,5},{8,10},{9,11},{10,... | collective-permute-start | bytes 393224 | tf_op jit(solution)/shard_map/ppermute | solution.py:31
  11.0 3.2 %shard_map.74.refs_2_ = bf16[2048,1792]{1,0:T(8,128)(2,1)S(1)} custom-call(bf16[1,4096,1792]{2,1,0:T(8,128)(2,1)} %weight.6), custom_call_target="tpu_custom_call" | custom-call | tf_op jit(solution)/shard_map/pallas_call | solution.py:146
  14.2 1.8 %collective-permute-start.5 = (bf16[128,1024]{1,0:T(8,128)(2,1)S(1)}, bf16[128,1024]{1,0:T(8,128)(2,1)S(1)}, u32[]{:S(2)}, u32[]{:S(2)}) collective-permute-start(bf16[128,1024]{1,0:T(8,128)(2,1)S(1)} %pad_maximum_fusion.3), channel_id=1, source_target_pairs={{0,8},{4,20},{8,0},{12,28},{16,24},{20,4},{24,16},{28,12},{1,9},{5... | collective-permute-start | bytes 786440 | tf_op jit(solution)/shard_map/ppermute | solution.py:37
  16.0 3.2 %shard_map.77.refs_3_ = bf16[2048,1792]{1,0:T(8,128)(2,1)S(1)} custom-call(bf16[1,4096,1792]{2,1,0:T(8,128)(2,1)} %weight.7), custom_call_target="tpu_custom_call" | custom-call | tf_op jit(solution)/shard_map/pallas_call | solution.py:146
  19.1 3.2 %shard_map.78.refs_4_ = bf16[2048,1792]{1,0:T(8,128)(2,1)S(1)} custom-call(bf16[1,4096,1792]{2,1,0:T(8,128)(2,1)} %weight.6), custom_call_target="tpu_custom_call" | custom-call | tf_op jit(solution)/shard_map/pallas_call | solution.py:146
  22.4 1.6 %collective-permute-start.7 = (bf16[256,1024]{1,0:T(8,128)(2,1)S(1)}, bf16[256,1024]{1,0:T(8,128)(2,1)S(1)}, u32[]{:S(2)}, u32[]{:S(2)}) collective-permute-start(bf16[256,1024]{1,0:T(8,128)(2,1)S(1)} %shard_map.76), channel_id=1, source_target_pairs={{0,16},{4,12},{8,24},{12,4},{16,0},{20,28},{24,8},{28,20},{1,17},{... | collective-permute-start | bytes 1572872 | tf_op jit(solution)/shard_map/ppermute | solution.py:37
  24.6 3.2 %shard_map.79.refs_5_ = bf16[2048,1792]{1,0:T(8,128)(2,1)S(1)} custom-call(bf16[1,4096,1792]{2,1,0:T(8,128)(2,1)} %weight.7), custom_call_target="tpu_custom_call" | custom-call | tf_op jit(solution)/shard_map/pallas_call | solution.py:146
  27.8 4.8 %collective-permute-done.3 = bf16[128,1024]{1,0:T(8,128)(2,1)S(1)} collective-permute-done((bf16[128,1024]{1,0:T(8,128)(2,1)S(1)}, bf16[128,1024]{1,0:T(8,128)(2,1)S(1)}, u32[]{:S(2)}, u32[]{:S(2)}) %collective-permute-start.3) | collective-permute-done | bytes 262176 | tf_op jit(solution)/shard_map/ppermute | solution.py:37
  34.8 1.9 %collective-permute-done.8.refs_1_ = bf16[512,1024]{1,0:T(8,128)(2,1)S(1)} collective-permute-done((bf16[512,1024]{1,0:T(8,128)(2,1)S(1)}, bf16[512,1024]{1,0:T(8,128)(2,1)S(1)}, u32[]{:S(2)}, u32[]{:S(2)}) %collective-permute-start.8) | collective-permute-done | bytes 1048608 | tf_op jit(solution)/shard_map/ppermute | solution.py:31
  36.7 7.8 %shard_map.80 = (f32[512,1792]{1,0:T(8,128)S(1)}, f32[512,1792]{1,0:T(8,128)S(1)}, f32[512,128]{1,0:T(8,128)S(1)}) custom-call(bf16[512,1024]{1,0:T(8,128)(2,1)S(1)} %pad_maximum_fusion.refs_0_, bf16[512,1024]{1,0:T(8,128)(2,1)S(1)} %collective-permute-done.8.refs_1_, bf16[2048,1792]{1,0:T(8,128)(2,1)S(1)} %shard_map.74.refs_2_, ...), custom_call_target="tpu_custom_call" | custom-call | flops 7516192768 | bytes 14680064 | tf_op jit(solution)/shard_map/pallas_call | solution.py:217
  44.8 1.8 %collective-permute-done.10.refs_3_ = bf16[256,1024]{1,0:T(8,128)(2,1)S(1)} collective-permute-done((bf16[256,1024]{1,0:T(8,128)(2,1)S(1)}, bf16[256,1024]{1,0:T(8,128)(2,1)S(1)}, u32[]{:S(2)}, u32[]{:S(2)}) %collective-permute-start.10) | collective-permute-done | bytes 524320 | tf_op jit(solution)/shard_map/ppermute | solution.py:31
  46.6 8.4 %shard_map.81.hidden = bf16[512,1792]{1,0:T(8,128)(2,1)S(1)} custom-call(bf16[256,1024]{1,0:T(8,128)(2,1)S(1)} %pad_maximum_fusion.1.refs_0_, bf16[256,1024]{1,0:T(8,128)(2,1)S(1)} %collective-permute-done.6.refs_1_, bf16[256,1024]{1,0:T(8,128)(2,1)S(1)} %collective-permute-done.9.refs_2_, bf16[256,1024]{1,0:T(8,128)(2,1)S(1)} %collective-permute-done.10.refs_3_, ...), custom_call_target="tpu_custom_call" | custom-call | flops 7516192768 | bytes 14680064 | tf_op jit(solution)/shard_map/pallas_call | solution.py:217
  55.0 2.3 %shard_map.84 = (bf16[256,1024]{1,0:T(8,128)(2,1)S(1)}, bf16[256,1024]{1,0:T(8,128)(2,1)S(1)}) custom-call(bf16[512,1792]{1,0:T(8,128)(2,1)S(1)} %shard_map.81.hidden, bf16[1,1792,4096]{2,1,0:T(8,128)(2,1)S(1)} %bitcast.1), custom_call_target="tpu_custom_call" | custom-call | flops 1879048192 | bytes 3670016 | tf_op jit(solution)/shard_map/pallas_call | solution.py:251
  57.4 2.1 %shard_map.82 = (bf16[256,1024]{1,0:T(8,128)(2,1)S(1)}, bf16[256,1024]{1,0:T(8,128)(2,1)S(1)}) custom-call(bf16[512,1792]{1,0:T(8,128)(2,1)S(1)} %shard_map.81.hidden, bf16[1,1792,4096]{2,1,0:T(8,128)(2,1)S(1)} %bitcast.1), custom_call_target="tpu_custom_call" | custom-call | flops 1879048192 | bytes 3670016 | tf_op jit(solution)/shard_map/pallas_call | solution.py:251
  61.6 2.1 %shard_map.85 = (bf16[256,1024]{1,0:T(8,128)(2,1)S(1)}, bf16[256,1024]{1,0:T(8,128)(2,1)S(1)}) custom-call(bf16[512,1792]{1,0:T(8,128)(2,1)S(1)} %shard_map.81.hidden, bf16[1,1792,4096]{2,1,0:T(8,128)(2,1)S(1)} %bitcast.1), custom_call_target="tpu_custom_call" | custom-call | flops 1879048192 | bytes 3670016 | tf_op jit(solution)/shard_map/pallas_call | solution.py:251
  64.4 2.1 %shard_map.83 = (bf16[256,1024]{1,0:T(8,128)(2,1)S(1)}, bf16[256,1024]{1,0:T(8,128)(2,1)S(1)}) custom-call(bf16[512,1792]{1,0:T(8,128)(2,1)S(1)} %shard_map.81.hidden, bf16[1,1792,4096]{2,1,0:T(8,128)(2,1)S(1)} %bitcast.1), custom_call_target="tpu_custom_call" | custom-call | flops 1879048192 | bytes 3670016 | tf_op jit(solution)/shard_map/pallas_call | solution.py:251
  67.1 3.0 %collective-permute-done.20 = bf16[128,1024]{1,0:T(8,128)(2,1)S(1)} collective-permute-done((bf16[128,1024]{1,0:T(8,128)(2,1)S(1)}, bf16[128,1024]{1,0:T(8,128)(2,1)S(1)}, u32[]{:S(2)}, u32[]{:S(2)}) %collective-permute-start.20) | collective-permute-done | bytes 262176 | tf_op jit(solution)/shard_map/ppermute | solution.py:37
  74.5 2.9 %collective-permute-done.24 = bf16[64,1024]{1,0:T(8,128)(2,1)S(1)} collective-permute-done((bf16[64,1024]{1,0:T(8,128)(2,1)S(1)}, bf16[64,1024]{1,0:T(8,128)(2,1)S(1)}, u32[]{:S(2)}, u32[]{:S(2)}) %collective-permute-start.24) | collective-permute-done | bytes 131104 | tf_op jit(solution)/shard_map/ppermute | solution.py:37
  77.5 3.6 %collective-permute-start.25 = (bf16[64,1024]{1,0:T(8,128)(2,1)S(1)}, bf16[64,1024]{1,0:T(8,128)(2,1)S(1)}, u32[]{:S(2)}, u32[]{:S(2)}) collective-permute-start(bf16[64,1024]{1,0:T(8,128)(2,1)S(1)} %add_convert_fusion.4), channel_id=1, source_target_pairs={{0,3},{1,2},{2,1},{3,0},{4,7},{5,6},{6,5},{7,4},{8,11},{9,10},{10,... | collective-permute-start | bytes 393224 | tf_op jit(solution)/shard_map/ppermute | solution.py:31
  81.1 2.0 %collective-permute-start.22 = (bf16[64,1024]{1,0:T(8,128)(2,1)S(1)}, bf16[64,1024]{1,0:T(8,128)(2,1)S(1)}, u32[]{:S(2)}, u32[]{:S(2)}) collective-permute-start(bf16[64,1024]{1,0:T(8,128)(2,1)S(1)} %add_convert_fusion.6), channel_id=1, source_target_pairs={{0,2},{1,3},{2,0},{3,1},{4,6},{5,7},{6,4},{7,5},{8,10},{9,11},{10,... | collective-permute-start | bytes 393224 | tf_op jit(solution)/shard_map/ppermute | solution.py:31
  85.4 2.8 %collective-permute-done.18 = bf16[64,1024]{1,0:T(8,128)(2,1)S(1)} collective-permute-done((bf16[64,1024]{1,0:T(8,128)(2,1)S(1)}, bf16[64,1024]{1,0:T(8,128)(2,1)S(1)}, u32[]{:S(2)}, u32[]{:S(2)}) %collective-permute-start.18) | collective-permute-done | bytes 131104 | tf_op jit(solution)/shard_map/ppermute | solution.py:37
  89.9 3.4 %collective-permute-done.19.refs_1_ = bf16[64,1024]{1,0:T(8,128)(2,1)S(1)} collective-permute-done((bf16[64,1024]{1,0:T(8,128)(2,1)S(1)}, bf16[64,1024]{1,0:T(8,128)(2,1)S(1)}, u32[]{:S(2)}, u32[]{:S(2)}) %collective-permute-start.19) | collective-permute-done | bytes 131104 | tf_op jit(solution)/shard_map/ppermute | solution.py:31
  (84 shorter events, 22.3 us)
Async XLA Ops:
  0.0 2.2 %collective-permute-start = (bf16[256,1024]{1,0:T(8,128)(2,1)}, bf16[256,1024]{1,0:T(8,128)(2,1)S(1)}, u32[]{:S(2)}, u32[]{:S(2)}) collective-permute-start(bf16[256,1024]{1,0:T(8,128)(2,1)} %mine.1), channel_id=1, source_target_pairs={{0,4},{4,0},{8,12},{12,8},{16,20},{20,16},{24,28},{28,24},{1,5},{5... | collective-permute-start | bytes 1572872 | tf_op jit(solution)/shard_map/ppermute | solution.py:31
  5.4 8.8 %collective-permute-start.4 = (bf16[64,1024]{1,0:T(8,128)(2,1)S(1)}, bf16[64,1024]{1,0:T(8,128)(2,1)S(1)}, u32[]{:S(2)}, u32[]{:S(2)}) collective-permute-start(bf16[64,1024]{1,0:T(8,128)(2,1)S(1)} %get-tuple-element.38), channel_id=1, source_target_pairs={{0,1},{1,0},{2,3},{3,2},{4,5},{5,4},{6,7},{7,6},{8,9},{9,8},{10,11... | collective-permute-start | bytes 393224 | tf_op jit(solution)/shard_map/ppermute | solution.py:31
  8.4 14.0 %collective-permute-start.1 = (bf16[64,1024]{1,0:T(8,128)(2,1)S(1)}, bf16[64,1024]{1,0:T(8,128)(2,1)S(1)}, u32[]{:S(2)}, u32[]{:S(2)}) collective-permute-start(bf16[64,1024]{1,0:T(8,128)(2,1)S(1)} %get-tuple-element.35), channel_id=1, source_target_pairs={{0,2},{1,3},{2,0},{3,1},{4,6},{5,7},{6,4},{7,5},{8,10},{9,11},{10,... | collective-permute-start | bytes 393224 | tf_op jit(solution)/shard_map/ppermute | solution.py:31
  11.0 11.4 %collective-permute-start.2 = (bf16[64,1024]{1,0:T(8,128)(2,1)S(1)}, bf16[64,1024]{1,0:T(8,128)(2,1)S(1)}, u32[]{:S(2)}, u32[]{:S(2)}) collective-permute-start(bf16[64,1024]{1,0:T(8,128)(2,1)S(1)} %get-tuple-element.36), channel_id=1, source_target_pairs={{0,3},{1,2},{2,1},{3,0},{4,7},{5,6},{6,5},{7,4},{8,11},{9,10},{10,... | collective-permute-start | bytes 393224 | tf_op jit(solution)/shard_map/ppermute | solution.py:31
  14.2 8.2 %collective-permute-start.5 = (bf16[128,1024]{1,0:T(8,128)(2,1)S(1)}, bf16[128,1024]{1,0:T(8,128)(2,1)S(1)}, u32[]{:S(2)}, u32[]{:S(2)}) collective-permute-start(bf16[128,1024]{1,0:T(8,128)(2,1)S(1)} %pad_maximum_fusion.3), channel_id=1, source_target_pairs={{0,8},{4,20},{8,0},{12,28},{16,24},{20,4},{24,16},{28,12},{1,9},{5... | collective-permute-start | bytes 786440 | tf_op jit(solution)/shard_map/ppermute | solution.py:37
  22.4 11.5 %collective-permute-start.7 = (bf16[256,1024]{1,0:T(8,128)(2,1)S(1)}, bf16[256,1024]{1,0:T(8,128)(2,1)S(1)}, u32[]{:S(2)}, u32[]{:S(2)}) collective-permute-start(bf16[256,1024]{1,0:T(8,128)(2,1)S(1)} %shard_map.76), channel_id=1, source_target_pairs={{0,16},{4,12},{8,24},{12,4},{16,0},{20,28},{24,8},{28,20},{1,17},{... | collective-permute-start | bytes 1572872 | tf_op jit(solution)/shard_map/ppermute | solution.py:37
  24.0 8.6 %collective-permute-start.3 = (bf16[128,1024]{1,0:T(8,128)(2,1)S(1)}, bf16[128,1024]{1,0:T(8,128)(2,1)S(1)}, u32[]{:S(2)}, u32[]{:S(2)}) collective-permute-start(bf16[128,1024]{1,0:T(8,128)(2,1)S(1)} %constant_dynamic-update-slice_fusion), channel_id=1, source_target_pairs={{0,8},{4,20},{8,0},{12,28},{16,24},{20,4},{24,16},{28,12},{1,9},{5... | collective-permute-start | bytes 786440 | tf_op jit(solution)/shard_map/ppermute | solution.py:37
  34.0 2.7 %collective-permute-start.8 = (bf16[512,1024]{1,0:T(8,128)(2,1)S(1)}, bf16[512,1024]{1,0:T(8,128)(2,1)S(1)}, u32[]{:S(2)}, u32[]{:S(2)}) collective-permute-start(bf16[512,1024]{1,0:T(8,128)(2,1)S(1)} %pad_maximum_fusion.refs_0_), channel_id=1, source_target_pairs={{0,4},{4,0},{8,12},{12,8},{16,20},{20,16},{24,28},{28,24},{1,5},{5... | collective-permute-start | bytes 3145736 | tf_op jit(solution)/shard_map/ppermute | solution.py:31
  34.1 10.5 %collective-permute-start.6 = (bf16[256,1024]{1,0:T(8,128)(2,1)S(1)}, bf16[256,1024]{1,0:T(8,128)(2,1)S(1)}, u32[]{:S(2)}, u32[]{:S(2)}) collective-permute-start(bf16[256,1024]{1,0:T(8,128)(2,1)S(1)} %pad_maximum_fusion.1.refs_0_), channel_id=1, source_target_pairs={{0,16},{4,12},{8,24},{12,4},{16,0},{20,28},{24,8},{28,20},{1,17},{... | collective-permute-start | bytes 1572872 | tf_op jit(solution)/shard_map/ppermute | solution.py:37
  34.6 10.1 %collective-permute-start.9 = (bf16[256,1024]{1,0:T(8,128)(2,1)S(1)}, bf16[256,1024]{1,0:T(8,128)(2,1)S(1)}, u32[]{:S(2)}, u32[]{:S(2)}) collective-permute-start(bf16[256,1024]{1,0:T(8,128)(2,1)S(1)} %pad_maximum_fusion.1.refs_0_), channel_id=1, source_target_pairs={{0,4},{4,0},{8,12},{12,8},{16,20},{20,16},{24,28},{28,24},{1,5},{5... | collective-permute-start | bytes 1572872 | tf_op jit(solution)/shard_map/ppermute | solution.py:31
  57.3 2.7 %collective-permute-start.15 = (bf16[256,1024]{1,0:T(8,128)(2,1)S(1)}, bf16[256,1024]{1,0:T(8,128)(2,1)S(1)}, u32[]{:S(2)}, u32[]{:S(2)}) collective-permute-start(bf16[256,1024]{1,0:T(8,128)(2,1)S(1)} %get-tuple-element.57), channel_id=1, source_target_pairs={{0,4},{4,0},{8,12},{12,8},{16,20},{20,16},{24,28},{28,24},{1,5},{5... | collective-permute-start | bytes 1572872 | tf_op jit(solution)/shard_map/ppermute | solution.py:31
  60.1 7.0 %collective-permute-start.23 = (bf16[128,1024]{1,0:T(8,128)(2,1)S(1)}, bf16[128,1024]{1,0:T(8,128)(2,1)S(1)}, u32[]{:S(2)}, u32[]{:S(2)}) collective-permute-start(bf16[128,1024]{1,0:T(8,128)(2,1)S(1)} %add_convert_fusion.1), channel_id=1, source_target_pairs={{0,16},{4,12},{8,24},{12,4},{16,0},{20,28},{24,8},{28,20},{1,17},{... | collective-permute-start | bytes 786440 | tf_op jit(solution)/shard_map/ppermute | solution.py:37
  63.7 6.4 %collective-permute-start.20 = (bf16[128,1024]{1,0:T(8,128)(2,1)S(1)}, bf16[128,1024]{1,0:T(8,128)(2,1)S(1)}, u32[]{:S(2)}, u32[]{:S(2)}) collective-permute-start(bf16[128,1024]{1,0:T(8,128)(2,1)S(1)} %add_convert_fusion.3), channel_id=1, source_target_pairs={{0,16},{4,12},{8,24},{12,4},{16,0},{20,28},{24,8},{28,20},{1,17},{... | collective-permute-start | bytes 786440 | tf_op jit(solution)/shard_map/ppermute | solution.py:37
  64.4 5.8 %collective-permute-start.16 = (bf16[256,1024]{1,0:T(8,128)(2,1)S(1)}, bf16[256,1024]{1,0:T(8,128)(2,1)S(1)}, u32[]{:S(2)}, u32[]{:S(2)}) collective-permute-start(bf16[256,1024]{1,0:T(8,128)(2,1)S(1)} %get-tuple-element.60), channel_id=1, source_target_pairs={{0,4},{4,0},{8,12},{12,8},{16,20},{20,16},{24,28},{28,24},{1,5},{5... | collective-permute-start | bytes 1572872 | tf_op jit(solution)/shard_map/ppermute | solution.py:31
  66.5 5.0 %collective-permute-start.12 = (bf16[256,1024]{1,0:T(8,128)(2,1)S(1)}, bf16[256,1024]{1,0:T(8,128)(2,1)S(1)}, u32[]{:S(2)}, u32[]{:S(2)}) collective-permute-start(bf16[256,1024]{1,0:T(8,128)(2,1)S(1)} %get-tuple-element.55), channel_id=1, source_target_pairs={{0,4},{4,0},{8,12},{12,8},{16,20},{20,16},{24,28},{28,24},{1,5},{5... | collective-permute-start | bytes 1572872 | tf_op jit(solution)/shard_map/ppermute | solution.py:31
  70.3 12.9 %collective-permute-start.17 = (bf16[128,1024]{1,0:T(8,128)(2,1)S(1)}, bf16[128,1024]{1,0:T(8,128)(2,1)S(1)}, u32[]{:S(2)}, u32[]{:S(2)}) collective-permute-start(bf16[128,1024]{1,0:T(8,128)(2,1)S(1)} %add_convert_fusion), channel_id=1, source_target_pairs={{0,16},{4,12},{8,24},{12,4},{16,0},{20,28},{24,8},{28,20},{1,17},{... | collective-permute-start | bytes 786440 | tf_op jit(solution)/shard_map/ppermute | solution.py:37
  71.0 6.4 %collective-permute-start.24 = (bf16[64,1024]{1,0:T(8,128)(2,1)S(1)}, bf16[64,1024]{1,0:T(8,128)(2,1)S(1)}, u32[]{:S(2)}, u32[]{:S(2)}) collective-permute-start(bf16[64,1024]{1,0:T(8,128)(2,1)S(1)} %add_convert_fusion.5), channel_id=1, source_target_pairs={{0,8},{4,20},{8,0},{12,28},{16,24},{20,4},{24,16},{28,12},{1,9},{5... | collective-permute-start | bytes 393224 | tf_op jit(solution)/shard_map/ppermute | solution.py:37
  71.5 12.2 %collective-permute-start.13 = (bf16[128,1024]{1,0:T(8,128)(2,1)S(1)}, bf16[128,1024]{1,0:T(8,128)(2,1)S(1)}, u32[]{:S(2)}, u32[]{:S(2)}) collective-permute-start(bf16[128,1024]{1,0:T(8,128)(2,1)S(1)} %add_convert_fusion.2), channel_id=1, source_target_pairs={{0,16},{4,12},{8,24},{12,4},{16,0},{20,28},{24,8},{28,20},{1,17},{... | collective-permute-start | bytes 786440 | tf_op jit(solution)/shard_map/ppermute | solution.py:37
  73.0 8.0 %collective-permute-start.21 = (bf16[64,1024]{1,0:T(8,128)(2,1)S(1)}, bf16[64,1024]{1,0:T(8,128)(2,1)S(1)}, u32[]{:S(2)}, u32[]{:S(2)}) collective-permute-start(bf16[64,1024]{1,0:T(8,128)(2,1)S(1)} %add_convert_fusion.7), channel_id=1, source_target_pairs={{0,8},{4,20},{8,0},{12,28},{16,24},{20,4},{24,16},{28,12},{1,9},{5... | collective-permute-start | bytes 393224 | tf_op jit(solution)/shard_map/ppermute | solution.py:37
  77.5 12.3 %collective-permute-start.25 = (bf16[64,1024]{1,0:T(8,128)(2,1)S(1)}, bf16[64,1024]{1,0:T(8,128)(2,1)S(1)}, u32[]{:S(2)}, u32[]{:S(2)}) collective-permute-start(bf16[64,1024]{1,0:T(8,128)(2,1)S(1)} %add_convert_fusion.4), channel_id=1, source_target_pairs={{0,3},{1,2},{2,1},{3,0},{4,7},{5,6},{6,5},{7,4},{8,11},{9,10},{10,... | collective-permute-start | bytes 393224 | tf_op jit(solution)/shard_map/ppermute | solution.py:31
  81.1 8.8 %collective-permute-start.22 = (bf16[64,1024]{1,0:T(8,128)(2,1)S(1)}, bf16[64,1024]{1,0:T(8,128)(2,1)S(1)}, u32[]{:S(2)}, u32[]{:S(2)}) collective-permute-start(bf16[64,1024]{1,0:T(8,128)(2,1)S(1)} %add_convert_fusion.6), channel_id=1, source_target_pairs={{0,2},{1,3},{2,0},{3,1},{4,6},{5,7},{6,4},{7,5},{8,10},{9,11},{10,... | collective-permute-start | bytes 393224 | tf_op jit(solution)/shard_map/ppermute | solution.py:31
  83.2 5.0 %collective-permute-start.18 = (bf16[64,1024]{1,0:T(8,128)(2,1)S(1)}, bf16[64,1024]{1,0:T(8,128)(2,1)S(1)}, u32[]{:S(2)}, u32[]{:S(2)}) collective-permute-start(bf16[64,1024]{1,0:T(8,128)(2,1)S(1)} %add_convert_fusion.9), channel_id=1, source_target_pairs={{0,8},{4,20},{8,0},{12,28},{16,24},{20,4},{24,16},{28,12},{1,9},{5... | collective-permute-start | bytes 393224 | tf_op jit(solution)/shard_map/ppermute | solution.py:37
  83.9 5.8 %collective-permute-start.14 = (bf16[64,1024]{1,0:T(8,128)(2,1)S(1)}, bf16[64,1024]{1,0:T(8,128)(2,1)S(1)}, u32[]{:S(2)}, u32[]{:S(2)}) collective-permute-start(bf16[64,1024]{1,0:T(8,128)(2,1)S(1)} %add_convert_fusion.11), channel_id=1, source_target_pairs={{0,8},{4,20},{8,0},{12,28},{16,24},{20,4},{24,16},{28,12},{1,9},{5... | collective-permute-start | bytes 393224 | tf_op jit(solution)/shard_map/ppermute | solution.py:37
  88.3 5.0 %collective-permute-start.19 = (bf16[64,1024]{1,0:T(8,128)(2,1)S(1)}, bf16[64,1024]{1,0:T(8,128)(2,1)S(1)}, u32[]{:S(2)}, u32[]{:S(2)}) collective-permute-start(bf16[64,1024]{1,0:T(8,128)(2,1)S(1)} %add_convert_fusion.8), channel_id=1, source_target_pairs={{0,1},{1,0},{2,3},{3,2},{4,5},{5,4},{6,7},{7,6},{8,9},{9,8},{10,11... | collective-permute-start | bytes 393224 | tf_op jit(solution)/shard_map/ppermute | solution.py:31
  (13 other events, 128.5 us)

commit v3 on v2

--- a/solution.py
+++ b/solution.py
@@ -11,7 +11,10 @@
 HALF = BLOCK // 2
 MIB = 1024 * 1024
 UP_GROUPS = ((0, 1), (2, 3))
-DOWN_GROUPS = ((3,), (2,), (1,), (0,))
+DOWN_ORDER = (
+    ("o3",), ("m3", "o2"), ("h3",), ("m2", "o1"), ("h2",), ("m1", "o0", "m0"), ("h3",), ("h1",), ("h2",),
+    ("h0",), ("f3",), ("f2",), ("h1",), ("h0",), ("f1",), ("f0",),
+)
 VMEM = pl.BlockSpec(memory_space=pltpu.VMEM)
 SMEM = pl.BlockSpec(memory_space=pltpu.SMEM)
 ANY = pl.BlockSpec(memory_space=pl.ANY)
@@ -58,39 +61,80 @@
     return [term[: term.shape[0] // 2] for term in terms]
 
 
-def select_kernel(count, pick_block, pick_live, mine, other, *outs):
-    here = mine.shape[0] // BLOCK
+def plan_kernel(count, pick_block, pick_live, tokens, near, mask, blocks, picked, live, block_sem, sem):
+    here = tokens.shape[0] // BLOCK
     expert = lax.axis_index("expert")
     row = lax.axis_index("dp")
     half = row % 2
+    loads = []
+    for b in range(here):
+        rows = pl.ds(pl.multiple_of(b * BLOCK + half * HALF, HALF), HALF)
+        loads.append(pltpu.make_async_copy(tokens.at[rows], blocks.at[b], block_sem.at[b]))
+    loads.append(pltpu.make_async_copy(pick_block, picked, sem.at[0]))
+    loads.append(pltpu.make_async_copy(pick_live, live, sem.at[1]))
+    for load in loads:
+        load.start()
+    for load in loads:
+        load.wait()
     for c in range(count):
-        picked = pick_block[expert ^ c, row // 2]
-        live = pick_live[expert ^ c, row // 2] == 1
-        rows = pl.ds(pl.multiple_of((picked % here) * BLOCK + half * HALF, HALF), HALF)
-        near = picked // here == half
-
-        @pl.when(live & near)
-        def _():
-            outs[c][...] = mine[rows, :]
-
-        @pl.when(live & jnp.logical_not(near))
-        def _():
-            outs[c][...] = other[rows, :]
-
-        @pl.when(jnp.logical_not(live))
-        def _():
-            outs[c][...] = jnp.zeros_like(outs[c])
-
-
-def select(pick_block, pick_live, mine, other, count):
-    shape = jax.ShapeDtypeStruct((HALF, mine.shape[1]), jnp.bfloat16)
+        slot = picked[expert ^ c, row // 2]
+        taken = live[expert ^ c, row // 2] == 1
+        held = taken & (slot // here == half)
+        value = jnp.zeros(near.shape[1:], jnp.float32)
+        for b in range(here):
+            keep = jnp.where(held & (slot % here == b), jnp.float32(1), jnp.float32(0))
+            value = value + keep * as_f32(blocks[b])
+            away = taken & (slot // here != half) & (slot % here == b)
+            mask[c * here + b] = jnp.full(mask.shape[1:], jnp.where(away, jnp.float32(1), jnp.float32(0)))
+        near[c] = value.astype(jnp.bfloat16)
+
+
+def plan(pick_block, pick_live, tokens, count):
+    here = tokens.shape[0] // BLOCK
+    features = tokens.shape[1]
+    return pl.pallas_call(
+        functools.partial(plan_kernel, count),
+        in_specs=[HBM] * 3,
+        out_specs=[VMEM, VMEM],
+        out_shape=[
+            jax.ShapeDtypeStruct((count, HALF, features), jnp.bfloat16),
+            jax.ShapeDtypeStruct((count * here, 8, 128), jnp.float32),
+        ],
+        scratch_shapes=[
+            pltpu.VMEM((here, HALF, features), jnp.bfloat16),
+            pltpu.SMEM(pick_block.shape, pick_block.dtype),
+            pltpu.SMEM(pick_live.shape, pick_live.dtype),
+            pltpu.SemaphoreType.DMA((here,)),
+            pltpu.SemaphoreType.DMA((2,)),
+        ],
+        cost_estimate=pl.CostEstimate(flops=0, bytes_accessed=0, transcendentals=0),
+        compiler_params=params(6),
+    )(in_hbm(pick_block), in_hbm(pick_live), in_hbm(tokens))
+
+
+def select_kernel(count, near, mask, other, *outs):
+    here = other.shape[0] // BLOCK
+    half = lax.axis_index("dp") % 2
+    blocks = []
+    for b in range(here):
+        rows = pl.ds(pl.multiple_of(b * BLOCK + half * HALF, HALF), HALF)
+        blocks.append(as_f32(other[rows, :]))
+    for c in range(count):
+        value = as_f32(near[c])
+        for b in range(here):
+            value = value + mask[c * here + b, 0:1, 0:1] * blocks[b]
+        outs[c][...] = value.astype(jnp.bfloat16)
+
+
+def select(near, mask, other, count):
+    shape = jax.ShapeDtypeStruct((HALF, other.shape[1]), jnp.bfloat16)
     return pl.pallas_call(
         functools.partial(select_kernel, count),
-        in_specs=[SMEM, SMEM, VMEM, VMEM],
+        in_specs=[VMEM] * 3,
         out_specs=[VMEM] * count,
         out_shape=[shape] * count,
         compiler_params=params(6),
-    )(pick_block, pick_live, mine, other)
+    )(near, mask, other)
 
 
 def marker_kernel(*refs):
@@ -154,25 +198,24 @@
     )(in_hbm(weight))
 
 
-def gate_up_kernel(count, parts, first, last, model_width, *refs):
-    sources, (w_gate, w_up), refs = refs[: 2 * parts], refs[2 * parts : 2 * parts + 2], refs[2 * parts + 2 :]
-    features = sources[0].shape[1]
+def gate_up_kernel(count, first, place, model_width, mine, theirs, w_gate, w_up, *refs):
+    last = place is not None
     if not first:
         gate_in, up_in, squares_in = refs[:3]
         refs = refs[3:]
     if last:
-        hidden_out, xs, squares = refs
+        hidden_out, xs, squares = refs[-3:]
     else:
         gate_out, up_out, squares, xs = refs
-    total = jnp.zeros((xs.shape[0], 1), jnp.float32)
+    features = mine.shape[1]
+    half = xs.shape[0] // 2
+    total = jnp.zeros((2 * half, 1), jnp.float32)
     for c in range(count):
         columns = slice(c * features, (c + 1) * features)
-        place = 0
-        for source in sources:
-            for j in range(source.shape[0] // (count * HALF)):
+        for k, source in enumerate((mine, theirs)):
+            for j in range(half // HALF):
                 begin = (j * count + c) * HALF
-                xs[place : place + HALF, columns] = source[begin : begin + HALF, :]
-                place += HALF
+                xs[k * half + j * HALF : k * half + (j + 1) * HALF, columns] = source[begin : begin + HALF, :]
         values = as_f32(xs[:, columns])
         total = total + jnp.sum(values * values, axis=1, keepdims=True)
     total = jnp.broadcast_to(total, squares.shape)
@@ -195,32 +238,42 @@
             up = dot_up if up is None else up + dot_up
         if last:
             gate = gate * inv_rms
-            hidden_out[:, cols] = (gate / (1.0 + jnp.exp(-gate)) * (up * inv_rms)).astype(jnp.bfloat16)
+            value = (gate / (1.0 + jnp.exp(-gate)) * (up * inv_rms)).astype(jnp.bfloat16)
+            hidden_out[place * half : (place + 1) * half, cols] = value[:half]
+            hidden_out[(2 + place) * half : (3 + place) * half, cols] = value[half:]
         else:
             gate_out[:, cols] = gate
             up_out[:, cols] = up
 
 
-def gate_up(count, mine, theirs, gate_rows, up_rows, carry, last, model_width):
+def gate_up(count, mine, theirs, gate_rows, up_rows, carry, place, hidden, model_width):
     first = carry is None
-    features = mine[0].shape[1]
-    rows = sum(part.shape[0] for part in mine + theirs) // count
+    features = mine.shape[1]
+    rows = 2 * mine.shape[0] // count
     hid = gate_rows.shape[1]
     acc = pltpu.VMEM((rows, hid), jnp.float32)
     scratch = [pltpu.VMEM((rows, count * features), jnp.bfloat16)]
-    operands = mine + theirs + [gate_rows, up_rows] + list(carry or ())
-    if last:
-        out_shape = jax.ShapeDtypeStruct((rows, hid), jnp.bfloat16)
+    operands = [mine, theirs, gate_rows, up_rows] + list(carry or ())
+    in_specs = [VMEM] * len(operands)
+    aliases = {}
+    if place is not None:
+        out_shape = [pltpu.VMEM((2 * rows, hid), jnp.bfloat16)]
         scratch.append(pltpu.VMEM((rows, 128), jnp.float32))
+        if hidden is not None:
+            aliases = {len(operands): 0}
+            operands.append(hidden)
+            in_specs.append(ANY)
     else:
         out_shape = [acc, acc, pltpu.VMEM((rows, 128), jnp.float32)]
-    return pl.pallas_call(
-        functools.partial(gate_up_kernel, count, len(mine), first, last, model_width),
-        in_specs=[VMEM] * len(operands),
-        out_specs=VMEM if last else [VMEM] * 3,
+        if not first:
+            aliases = {4: 0, 5: 1, 6: 2}
+    return pl.pallas_call(
+        functools.partial(gate_up_kernel, count, first, place, model_width),
+        in_specs=in_specs,
+        out_specs=[VMEM] * len(out_shape),
         out_shape=out_shape,
         scratch_shapes=scratch,
-        input_output_aliases={} if first or last else {len(operands) - 3 + i: i for i in range(3)},
+        input_output_aliases=aliases,
         cost_estimate=pl.CostEstimate(
             flops=4 * rows * features * count * hid,
             bytes_accessed=4 * features * count * hid,
@@ -230,32 +283,29 @@
     )(*operands)
 
 
-def down_kernel(group, features, hidden, weight, mine, other):
-    half = mine.shape[0] // len(group)
-    expert = lax.axis_index("expert")
-    block = next(size for size in (512, 256, 128) if features % size == 0)
-    for c, offset in enumerate(group):
+def down_kernel(parts, hidden, weight, *outs):
+    for (kind, offset), out in zip(parts, outs):
+        rows, features = out.shape
+        first_row = rows if kind == "o" else 0
+        block = next(size for size in (512, 256, 128) if features % size == 0)
         for b in range(features // block):
-            begin = pl.multiple_of((expert ^ offset) * features + b * block, block)
-            value = jnp.dot(hidden[...], weight[0, :, pl.ds(begin, block)], preferred_element_type=jnp.float32)
-            value = value.astype(jnp.bfloat16)
-            cols = slice(c * features + b * block, c * features + (b + 1) * block)
-            mine[:, cols] = value[:half]
-            other[:, cols] = value[half:]
-
-
-def down(group, hidden, w_down, features):
-    rows, hid = hidden.shape
-    width = len(group) * features
-    shape = jax.ShapeDtypeStruct((rows // 2, width), jnp.bfloat16)
-    return pl.pallas_call(
-        functools.partial(down_kernel, group, features),
+            begin = pl.multiple_of((lax.axis_index("expert") ^ offset) * features + b * block, block)
+            value = jnp.dot(
+                hidden[first_row : first_row + rows, :],
+                weight[0, :, pl.ds(begin, block)],
+                preferred_element_type=jnp.float32,
+            )
+            out[:, b * block : (b + 1) * block] = value.astype(jnp.bfloat16)
+
+
+def down(parts, hidden, w_down, features):
+    rows = hidden.shape[0] // 2
+    return pl.pallas_call(
+        functools.partial(down_kernel, parts),
         in_specs=[VMEM, VMEM],
-        out_specs=[VMEM, VMEM],
-        out_shape=[shape, shape],
-        cost_estimate=pl.CostEstimate(
-            flops=2 * rows * hid * width, bytes_accessed=2 * hid * width, transcendentals=0
-        ),
+        out_specs=[VMEM] * len(parts),
+        out_shape=[jax.ShapeDtypeStruct((rows, features), jnp.bfloat16)] * len(parts),
+        cost_estimate=pl.CostEstimate(flops=0, bytes_accessed=0, transcendentals=0),
         compiler_params=params(8),
     )(hidden, w_down)
 
@@ -315,9 +365,9 @@
     model_width = features * experts
     here = tokens.shape[0] // BLOCK
     up_groups = UP_GROUPS if experts == 4 else tuple((d, d + 1) for d in range(0, experts, 2))
-    down_groups = DOWN_GROUPS if experts == 4 else tuple((d,) for d in range(experts - 1, -1, -1))
-
-    chosen = select(pick_block, pick_live, tokens, exchange(tokens, "dp", 1), experts)
+
+    near, mask = plan(pick_block, pick_live, tokens, experts)
+    chosen = select(near, mask, exchange(tokens, "dp", 1), experts)
     arrived = [chosen[d] if d == 0 else exchange(chosen[d], "expert", d) for d in range(experts)]
     own = [jnp.concatenate([arrived[d] for d in group], axis=0) for group in up_groups]
     token = marker(3000000000, *(arrived[d] for group in up_groups[1:] for d in group))
@@ -326,53 +376,73 @@
         if g == 0:
             gate_rows.append(fetch_rows(group, after(w_gate, chosen[0]), features))
             own[g] = after(own[g], gate_rows[g])
-        up_rows.append(fetch_rows(group, after(w_up, own[g], *joined[-1:]), features))
+        if g != 1:
+            up_rows.append(fetch_rows(group, after(w_up, own[g], *joined[-1:]), features))
         if g + 1 < len(up_groups):
-            gate_rows.append(fetch_rows(up_groups[g + 1], after(w_gate, up_rows[g]), features))
+            gate_rows.append(fetch_rows(up_groups[g + 1], after(w_gate, up_rows[-1]), features))
         value = own[g]
-        for step in range(steps - 1):
+        for step in range(steps - 2):
             value = hop_and_join(value, step, steps)
+        received = hop(value, steps - 2, steps)
         if g == 0:
             value = gate(value, token)
-        joined.append(after(value, up_rows[g], gate_rows[-1]))
-    for g in range(len(up_groups)):
-        last_hop = hop(joined[g], steps - 1, steps)
-        if g + 1 < len(up_groups):
-            whole = jnp.concatenate([joined[g], last_hop], axis=0)
-            whole = after(whole, joined[g + 1])
-            mine.append([whole])
-            theirs.append([exchange(whole, "dp", 1)])
-        else:
-            mine.append([joined[g], last_hop])
-            theirs.append([exchange(joined[g], "dp", 1)])
-    carry = None
+        if g != 1:
+            value = jnp.concatenate([value, received], axis=0)
+        if g == 0:
+            value = after(value, up_rows[0], gate_rows[-1])
+        elif g == 1:
+            near_theirs = exchange(joined[0], "dp", 1)
+            near = after(joined[0], own[1])
+            near_sums = gate_up(
+                len(up_groups[0]), near, near_theirs, gate_rows[0], up_rows[0], None, None, None, model_width
+            )
+            up_rows.append(fetch_rows(group, after(w_up, near_sums[2]), features))
+            value = jnp.concatenate([value, after(received, up_rows[1])], axis=0)
+        joined.append(value)
+    far = [hop(value, steps - 1, steps) for value in joined]
+    far[0] = after(far[0], joined[1])
+    far_sums = None
     for g, group in enumerate(up_groups):
         last = g == len(up_groups) - 1
-        if last:
-            mine[g][1] = after(mine[g][1], carry[2])
-            theirs[g].append(exchange(mine[g][1], "dp", 1))
-        carry = gate_up(len(group), mine[g], theirs[g], gate_rows[g], up_rows[g], carry, last, model_width)
-    hidden = carry
-
-    terms, firsts = [], []
-    for i, group in enumerate(down_groups):
-        ready = hidden if i < 2 else after(hidden, firsts[i - 2])
-        kept, sent = down(group, ready, w_down, features)
-        terms.append([kept, exchange(sent, "dp", 1)])
-        firsts.append(upper_rows(terms[i]))
+        weights = (gate_rows[g], up_rows[g])
+        if g > 0:
+            near_theirs = exchange(joined[g], "dp", 1)
+            near = after(joined[g], far_sums[2])
+            near_sums = gate_up(
+                len(group), near, near_theirs, *weights, near_sums, 0 if last else None, None, model_width
+            )
+        rows = after(far[g], near_sums[-1])
+        hidden = near_sums[0] if last else None
+        far_theirs = exchange(rows, "dp", 1)
+        far_sums = gate_up(
+            len(group), rows, far_theirs, *weights, far_sums, 1 if last else None, hidden, model_width
+        )
+    hidden = far_sums[0]
+
+    if experts == 4 and steps == 2:
+        order = DOWN_ORDER
+    else:
+        order = [(kind + str(d),) for d in range(experts - 1, -1, -1) for kind in ["o", "m"] + ["h"] * steps + ["f"]]
+    terms = [[] for _ in range(experts)]
+    hops = [0] * experts
     outputs = [None] * experts
-    for i, group in enumerate(down_groups):
-        sent = firsts[i]
-        for step in range(steps - 1, -1, -1):
-            if step < steps - 1:
-                sent = upper_rows(terms[i])
-                if step == 0 and i + 2 < len(firsts):
-                    sent = after(sent, firsts[i + 2])
-            terms[i] = lower_rows(terms[i]) + [hop(sent, step, steps)]
-        total = sum(as_f32(term) for term in terms[i]).astype(jnp.bfloat16)
-        for c, d in enumerate(group):
-            value = total[:, c * features : (c + 1) * features]
-            outputs[d] = value if d == 0 else exchange(value, "expert", d)
+    done = hidden
+    for entry in order:
+        parts = tuple((part[0], int(part[1:])) for part in entry)
+        if parts[0][0] in "om":
+            for (kind, d), value in zip(parts, down(parts, after(hidden, done), w_down, features)):
+                done = value
+                terms[d].append(exchange(done, "dp", 1) if kind == "o" else done)
+            continue
+        kind, d = parts[0]
+        terms[d][-1] = after(terms[d][-1], done)
+        if kind == "h":
+            hops[d] += 1
+            done = upper_rows(terms[d])
+            terms[d] = lower_rows(terms[d]) + [hop(done, steps - hops[d], steps)]
+        else:
+            done = sum(as_f32(term) for term in terms[d]).astype(jnp.bfloat16)
+            outputs[d] = done if d == 0 else exchange(done, "expert", d)
 
     kept, sent = combine(pick_block, pick_live, combine_weight, outputs, here)
     return assemble(kept, exchange(sent, "dp", 1))

time: 97 us -> 86.9 us (0.90)
  waiting for transfers between devices: 26.3 us -> 14.8 us
  starting transfers between devices: 26.8 us -> 29.8 us
  local copies, waits for them, and re-layouts: 2.45 us -> 0.09 us
    ppermute x12, waiting for transfers between devices: 14.8 us -> 7.73 us  [hop(): return lax.ppermute(value, 'dp', list(enumerate(turn)))]
    ppermute x15 -> x16, waiting for transfers between devices: 11.5 us -> 7.05 us  [exchange(): return lax.ppermute(value, axis, [(i, i ^ offset) for i in range(count)])]
    unnamed x21 -> x15, local copies, waits for them, and re-layouts: 2.44 us -> 0.06 us
    ppermute x12, starting transfers between devices: 12.1 us -> 14.4 us  [hop(): return lax.ppermute(value, 'dp', list(enumerate(turn)))]
    pallas_call x7 -> x10, Pallas kernels: 25.4 us -> 26.3 us  [the longest x4 16.3 us: gate_up(): pl.pallas_call(functools.partial(gate_up_kernel, count, first, place, mod...]
    ppermute x15 -> x16, starting transfers between devices: 14.7 us -> 15.4 us  [exchange(): return lax.ppermute(value, axis, [(i, i ^ offset) for i in range(count)])]
  transfers between devices with their start and end apart: 27 -> 28, of which waited for: 12 -> 10; matrix products, arithmetic and copies ran while one was open for 1% -> 1% of each run, Pallas kernels for 28% -> 38%
where the time goes in v3:
time: 86.9 us; the launch traced here: 86.7 us
  Pallas kernels  40.9 us (47%)
  starting transfers between devices  29.8 us (34%)
  waiting for transfers between devices  14.8 us (17%)
    pallas_call x4, Pallas kernels, gate_up(): pl.pallas_call(functools.partial(gate_up_kernel, count, first, place, mod...  16.3 us
    ppermute x16, starting transfers between devices, exchange(): return lax.ppermute(value, axis, [(i, i ^ offset) for i in range(count)])  15.4 us
    ppermute x12, starting transfers between devices, hop(): return lax.ppermute(value, 'dp', list(enumerate(turn)))  14.4 us
    pallas_call x4, Pallas kernels, fetch_rows(): pl.pallas_call(functools.partial(fetch_kernel, group, features), in_specs...  12.7 us
    pallas_call x4, Pallas kernels, down(): pl.pallas_call(functools.partial(down_kernel, parts), in_specs=[VMEM, VME...  8.46 us
    ppermute x12, waiting for transfers between devices, hop(): return lax.ppermute(value, 'dp', list(enumerate(turn)))  7.73 us
    ppermute x16, waiting for transfers between devices, exchange(): return lax.ppermute(value, axis, [(i, i ^ offset) for i in range(count)])  7.05 us
  transfers between devices with their start and end apart: 28, of which 10 were waited for; matrix products, arithmetic and copies ran while one was open for 1% of the time, Pallas kernels for 38%

profile of v3, /device:TPU:0, one launch (start us, length us, event | category | flops | bytes accessed | tf_op | source)
XLA Modules:
  0.0 86.7 jit_solution(574561649970614808)
XLA Ops:
  2.5 3.0 %collective-permute-start.4 = (bf16[64,1024]{1,0:T(8,128)(2,1)S(1)}, bf16[64,1024]{1,0:T(8,128)(2,1)S(1)}, u32[]{:S(2)}, u32[]{:S(2)}) collective-permute-start(bf16[64,1024]{1,0:T(8,128)(2,1)S(1)} %get-tuple-element.59), channel_id=1, source_target_pairs={{0,1},{1,0},{2,3},{3,2},{4,5},{5,4},{6,7},{7,6},{8,9},{9,8},{10,11... | collective-permute-start | bytes 393224 | tf_op jit(solution)/shard_map/ppermute | solution.py:34
  5.6 2.6 %collective-permute-start.1 = (bf16[64,1024]{1,0:T(8,128)(2,1)S(1)}, bf16[64,1024]{1,0:T(8,128)(2,1)S(1)}, u32[]{:S(2)}, u32[]{:S(2)}) collective-permute-start(bf16[64,1024]{1,0:T(8,128)(2,1)S(1)} %get-tuple-element.56), channel_id=1, source_target_pairs={{0,2},{1,3},{2,0},{3,1},{4,6},{5,7},{6,4},{7,5},{8,10},{9,11},{10,... | collective-permute-start | bytes 393224 | tf_op jit(solution)/shard_map/ppermute | solution.py:34
  8.1 3.2 %shard_map.75.w_gate = bf16[2048,1792]{1,0:T(8,128)(2,1)S(1)} custom-call(bf16[1,4096,1792]{2,1,0:T(8,128)(2,1)} %weight.6), custom_call_target="tpu_custom_call" | custom-call | tf_op jit(solution)/shard_map/pallas_call | solution.py:190
  11.4 1.8 %collective-permute-start.5 = (bf16[128,1024]{1,0:T(8,128)(2,1)S(1)}, bf16[128,1024]{1,0:T(8,128)(2,1)S(1)}, u32[]{:S(2)}, u32[]{:S(2)}) collective-permute-start(bf16[128,1024]{1,0:T(8,128)(2,1)S(1)} %pad_maximum_fusion.1.refs_0_), channel_id=1, source_target_pairs={{0,8},{4,20},{8,0},{12,28},{16,24},{20,4},{24,16},{28,12},{1,9},{5... | collective-permute-start | bytes 786440 | tf_op jit(solution)/shard_map/ppermute | solution.py:40
  13.1 3.2 %shard_map.78.w_up = bf16[2048,1792]{1,0:T(8,128)(2,1)S(1)} custom-call(bf16[1,4096,1792]{2,1,0:T(8,128)(2,1)} %weight.7), custom_call_target="tpu_custom_call" | custom-call | tf_op jit(solution)/shard_map/pallas_call | solution.py:190
  16.3 3.2 %shard_map.79.w_gate = bf16[2048,1792]{1,0:T(8,128)(2,1)S(1)} custom-call(bf16[1,4096,1792]{2,1,0:T(8,128)(2,1)} %weight.6), custom_call_target="tpu_custom_call" | custom-call | tf_op jit(solution)/shard_map/pallas_call | solution.py:190
  19.7 1.6 %collective-permute-start.8 = (bf16[256,1024]{1,0:T(8,128)(2,1)S(1)}, bf16[256,1024]{1,0:T(8,128)(2,1)S(1)}, u32[]{:S(2)}, u32[]{:S(2)}) collective-permute-start(bf16[256,1024]{1,0:T(8,128)(2,1)S(1)} %pad_maximum_fusion.mine), channel_id=1, source_target_pairs={{0,16},{4,12},{8,24},{12,4},{16,0},{20,28},{24,8},{28,20},{1,17},{... | collective-permute-start | bytes 1572872 | tf_op jit(solution)/shard_map/ppermute | solution.py:40
  21.9 4.0 %shard_map.80 = (f32[256,1792]{1,0:T(8,128)S(1)}, f32[256,1792]{1,0:T(8,128)S(1)}, f32[256,128]{1,0:T(8,128)S(1)}) custom-call(bf16[256,1024]{1,0:T(8,128)(2,1)S(1)} %pad_maximum_fusion.mine, bf16[256,1024]{1,0:T(8,128)(2,1)S(1)} %collective-permute-done.6.theirs, bf16[2048,1792]{1,0:T(8,128)(2,1)S(1)} %shard_map.75.w_gate, ...), custom_call_target="tpu_custom_call" | custom-call | flops 3758096384 | bytes 14680064 | tf_op jit(solution)/shard_map/pallas_call | solution.py:270
  25.9 3.2 %shard_map.81.w_up = bf16[2048,1792]{1,0:T(8,128)(2,1)S(1)} custom-call(bf16[1,4096,1792]{2,1,0:T(8,128)(2,1)} %weight.7), custom_call_target="tpu_custom_call" | custom-call | tf_op jit(solution)/shard_map/pallas_call | solution.py:190
  32.0 1.7 %collective-permute-start.7 = (bf16[256,1024]{1,0:T(8,128)(2,1)S(1)}, bf16[256,1024]{1,0:T(8,128)(2,1)S(1)}, u32[]{:S(2)}, u32[]{:S(2)}) collective-permute-start(bf16[256,1024]{1,0:T(8,128)(2,1)S(1)} %constant_dynamic-update-slice_fusion.2.mine), channel_id=1, source_target_pairs={{0,16},{4,12},{8,24},{12,4},{16,0},{20,28},{24,8},{28,20},{1,17},{... | collective-permute-start | bytes 1572872 | tf_op jit(solution)/shard_map/ppermute | solution.py:40
  33.7 4.0 %shard_map.82 = (f32[256,1792]{1,0:T(8,128)S(1)}, f32[256,1792]{1,0:T(8,128)S(1)}, f32[256,128]{1,0:T(8,128)S(1)}) custom-call(bf16[256,1024]{1,0:T(8,128)(2,1)S(1)} %collective-permute-done.8.mine, bf16[256,1024]{1,0:T(8,128)(2,1)S(1)} %collective-permute-done.9.theirs, bf16[2048,1792]{1,0:T(8,128)(2,1)S(1)} %shard_map.75.w_gate, ...), custom_call_target="tpu_custom_call" | custom-call | flops 3758096384 | bytes 14680064 | tf_op jit(solution)/shard_map/pallas_call | solution.py:270
  37.7 4.1 %shard_map.83.refs_3_ = bf16[512,1792]{1,0:T(8,128)(2,1)S(1)} custom-call(bf16[256,1024]{1,0:T(8,128)(2,1)S(1)} %constant_dynamic-update-slice_fusion.2.mine, bf16[256,1024]{1,0:T(8,128)(2,1)S(1)} %collective-permute-done.10.theirs, bf16[2048,1792]{1,0:T(8,128)(2,1)S(1)} %shard_map.79.w_gate, bf16[2048,1792]{1,0:T(8,128)(2,1)S(1)} %shard_map.81.w_up, ...), custom_call_target="tpu_custom_call" | custom-call | flops 3758096384 | bytes 14680064 | tf_op jit(solution)/shard_map/pallas_call | solution.py:270
  41.9 1.9 %collective-permute-done.11.theirs = bf16[256,1024]{1,0:T(8,128)(2,1)S(1)} collective-permute-done((bf16[256,1024]{1,0:T(8,128)(2,1)S(1)}, bf16[256,1024]{1,0:T(8,128)(2,1)S(1)}, u32[]{:S(2)}, u32[]{:S(2)}) %collective-permute-start.11) | collective-permute-done | bytes 524320 | tf_op jit(solution)/shard_map/ppermute | solution.py:34
  43.8 4.3 %shard_map.84.hidden = bf16[512,1792]{1,0:T(8,128)(2,1)S(1)} custom-call(bf16[256,1024]{1,0:T(8,128)(2,1)S(1)} %collective-permute-done.7.mine, bf16[256,1024]{1,0:T(8,128)(2,1)S(1)} %collective-permute-done.11.theirs, bf16[2048,1792]{1,0:T(8,128)(2,1)S(1)} %shard_map.79.w_gate, ...), custom_call_target="tpu_custom_call", output_to_operand_aliasing={{}: (7, {})} | custom-call | flops 3758096384 | bytes 14680064 | tf_op jit(solution)/shard_map/pallas_call | solution.py:270
  49.4 2.1 %shard_map.86 = (bf16[256,1024]{1,0:T(8,128)(2,1)S(1)}, bf16[256,1024]{1,0:T(8,128)(2,1)S(1)}) custom-call(bf16[512,1792]{1,0:T(8,128)(2,1)S(1)} %shard_map.84.hidden, bf16[1,1792,4096]{2,1,0:T(8,128)(2,1)S(1)} %bitcast.1), custom_call_target="tpu_custom_call" | custom-call | tf_op jit(solution)/shard_map/pallas_call | solution.py:303
  52.1 2.1 %shard_map.87 = (bf16[256,1024]{1,0:T(8,128)(2,1)S(1)}, bf16[256,1024]{1,0:T(8,128)(2,1)S(1)}) custom-call(bf16[512,1792]{1,0:T(8,128)(2,1)S(1)} %shard_map.84.hidden, bf16[1,1792,4096]{2,1,0:T(8,128)(2,1)S(1)} %bitcast.1), custom_call_target="tpu_custom_call" | custom-call | tf_op jit(solution)/shard_map/pallas_call | solution.py:303
  56.6 3.1 %shard_map.88 = (bf16[256,1024]{1,0:T(8,128)(2,1)S(1)}, bf16[256,1024]{1,0:T(8,128)(2,1)S(1)}, bf16[256,1024]{1,0:T(8,128)(2,1)S(1)}) custom-call(bf16[512,1792]{1,0:T(8,128)(2,1)S(1)} %shard_map.84.hidden, bf16[1,1792,4096]{2,1,0:T(8,128)(2,1)S(1)} %bitcast.1), custom_call_target="tpu_custom_call" | custom-call | tf_op jit(solution)/shard_map/pallas_call | solution.py:303
  61.6 2.5 %collective-permute-done.15 = bf16[128,1024]{1,0:T(8,128)(2,1)S(1)} collective-permute-done((bf16[128,1024]{1,0:T(8,128)(2,1)S(1)}, bf16[128,1024]{1,0:T(8,128)(2,1)S(1)}, u32[]{:S(2)}, u32[]{:S(2)}) %collective-permute-start.15) | collective-permute-done | bytes 262176 | tf_op jit(solution)/shard_map/ppermute | solution.py:40
  67.1 3.6 %collective-permute-start.26 = (bf16[64,1024]{1,0:T(8,128)(2,1)S(1)}, bf16[64,1024]{1,0:T(8,128)(2,1)S(1)}, u32[]{:S(2)}, u32[]{:S(2)}) collective-permute-start(bf16[64,1024]{1,0:T(8,128)(2,1)S(1)} %add_convert_fusion.9), channel_id=1, source_target_pairs={{0,3},{1,2},{2,1},{3,0},{4,7},{5,6},{6,5},{7,4},{8,11},{9,10},{10,... | collective-permute-start | bytes 393224 | tf_op jit(solution)/shard_map/ppermute | solution.py:34
  70.9 2.2 %collective-permute-start.25 = (bf16[64,1024]{1,0:T(8,128)(2,1)S(1)}, bf16[64,1024]{1,0:T(8,128)(2,1)S(1)}, u32[]{:S(2)}, u32[]{:S(2)}) collective-permute-start(bf16[64,1024]{1,0:T(8,128)(2,1)S(1)} %add_convert_fusion.8), channel_id=1, source_target_pairs={{0,2},{1,3},{2,0},{3,1},{4,6},{5,7},{6,4},{7,5},{8,10},{9,11},{10,... | collective-permute-start | bytes 393224 | tf_op jit(solution)/shard_map/ppermute | solution.py:34
  74.6 1.7 %collective-permute-start.22 = (bf16[64,1024]{1,0:T(8,128)(2,1)S(1)}, bf16[64,1024]{1,0:T(8,128)(2,1)S(1)}, u32[]{:S(2)}, u32[]{:S(2)}) collective-permute-start(bf16[64,1024]{1,0:T(8,128)(2,1)S(1)} %add_convert_fusion.6), channel_id=1, source_target_pairs={{0,8},{4,20},{8,0},{12,28},{16,24},{20,4},{24,16},{28,12},{1,9},{5... | collective-permute-start | bytes 393224 | tf_op jit(solution)/shard_map/ppermute | solution.py:40
  76.3 1.9 %collective-permute-done.23 = bf16[64,1024]{1,0:T(8,128)(2,1)S(1)} collective-permute-done((bf16[64,1024]{1,0:T(8,128)(2,1)S(1)}, bf16[64,1024]{1,0:T(8,128)(2,1)S(1)}, u32[]{:S(2)}, u32[]{:S(2)}) %collective-permute-start.23) | collective-permute-done | bytes 131104 | tf_op jit(solution)/shard_map/ppermute | solution.py:40
  78.2 1.9 %collective-permute-start.24 = (bf16[64,1024]{1,0:T(8,128)(2,1)S(1)}, bf16[64,1024]{1,0:T(8,128)(2,1)S(1)}, u32[]{:S(2)}, u32[]{:S(2)}) collective-permute-start(bf16[64,1024]{1,0:T(8,128)(2,1)S(1)} %add_convert_fusion.5), channel_id=1, source_target_pairs={{0,1},{1,0},{2,3},{3,2},{4,5},{5,4},{6,7},{7,6},{8,9},{9,8},{10,11... | collective-permute-start | bytes 393224 | tf_op jit(solution)/shard_map/ppermute | solution.py:34
  80.8 2.5 %collective-permute-done.24.refs_1_ = bf16[64,1024]{1,0:T(8,128)(2,1)S(1)} collective-permute-done((bf16[64,1024]{1,0:T(8,128)(2,1)S(1)}, bf16[64,1024]{1,0:T(8,128)(2,1)S(1)}, u32[]{:S(2)}, u32[]{:S(2)}) %collective-permute-start.24) | collective-permute-done | bytes 131104 | tf_op jit(solution)/shard_map/ppermute | solution.py:34
  (82 shorter events, 21.4 us)
Async XLA Ops:
  2.5 8.8 %collective-permute-start.4 = (bf16[64,1024]{1,0:T(8,128)(2,1)S(1)}, bf16[64,1024]{1,0:T(8,128)(2,1)S(1)}, u32[]{:S(2)}, u32[]{:S(2)}) collective-permute-start(bf16[64,1024]{1,0:T(8,128)(2,1)S(1)} %get-tuple-element.59), channel_id=1, source_target_pairs={{0,1},{1,0},{2,3},{3,2},{4,5},{5,4},{6,7},{7,6},{8,9},{9,8},{10,11... | collective-permute-start | bytes 393224 | tf_op jit(solution)/shard_map/ppermute | solution.py:34
  5.6 14.0 %collective-permute-start.1 = (bf16[64,1024]{1,0:T(8,128)(2,1)S(1)}, bf16[64,1024]{1,0:T(8,128)(2,1)S(1)}, u32[]{:S(2)}, u32[]{:S(2)}) collective-permute-start(bf16[64,1024]{1,0:T(8,128)(2,1)S(1)} %get-tuple-element.56), channel_id=1, source_target_pairs={{0,2},{1,3},{2,0},{3,1},{4,6},{5,7},{6,4},{7,5},{8,10},{9,11},{10,... | collective-permute-start | bytes 393224 | tf_op jit(solution)/shard_map/ppermute | solution.py:34
  8.1 11.4 %collective-permute-start.2 = (bf16[64,1024]{1,0:T(8,128)(2,1)S(1)}, bf16[64,1024]{1,0:T(8,128)(2,1)S(1)}, u32[]{:S(2)}, u32[]{:S(2)}) collective-permute-start(bf16[64,1024]{1,0:T(8,128)(2,1)S(1)} %get-tuple-element.57), channel_id=1, source_target_pairs={{0,3},{1,2},{2,1},{3,0},{4,7},{5,6},{6,5},{7,4},{8,11},{9,10},{10,... | collective-permute-start | bytes 393224 | tf_op jit(solution)/shard_map/ppermute | solution.py:34
  11.4 8.2 %collective-permute-start.5 = (bf16[128,1024]{1,0:T(8,128)(2,1)S(1)}, bf16[128,1024]{1,0:T(8,128)(2,1)S(1)}, u32[]{:S(2)}, u32[]{:S(2)}) collective-permute-start(bf16[128,1024]{1,0:T(8,128)(2,1)S(1)} %pad_maximum_fusion.1.refs_0_), channel_id=1, source_target_pairs={{0,8},{4,20},{8,0},{12,28},{16,24},{20,4},{24,16},{28,12},{1,9},{5... | collective-permute-start | bytes 786440 | tf_op jit(solution)/shard_map/ppermute | solution.py:40
  19.6 2.3 %collective-permute-start.6 = (bf16[256,1024]{1,0:T(8,128)(2,1)S(1)}, bf16[256,1024]{1,0:T(8,128)(2,1)S(1)}, u32[]{:S(2)}, u32[]{:S(2)}) collective-permute-start(bf16[256,1024]{1,0:T(8,128)(2,1)S(1)} %pad_maximum_fusion.mine), channel_id=1, source_target_pairs={{0,4},{4,0},{8,12},{12,8},{16,20},{20,16},{24,28},{28,24},{1,5},{5... | collective-permute-start | bytes 1572872 | tf_op jit(solution)/shard_map/ppermute | solution.py:34
  19.7 11.8 %collective-permute-start.8 = (bf16[256,1024]{1,0:T(8,128)(2,1)S(1)}, bf16[256,1024]{1,0:T(8,128)(2,1)S(1)}, u32[]{:S(2)}, u32[]{:S(2)}) collective-permute-start(bf16[256,1024]{1,0:T(8,128)(2,1)S(1)} %pad_maximum_fusion.mine), channel_id=1, source_target_pairs={{0,16},{4,12},{8,24},{12,4},{16,0},{20,28},{24,8},{28,20},{1,17},{... | collective-permute-start | bytes 1572872 | tf_op jit(solution)/shard_map/ppermute | solution.py:40
  21.3 9.3 %collective-permute-start.3 = (bf16[128,1024]{1,0:T(8,128)(2,1)S(1)}, bf16[128,1024]{1,0:T(8,128)(2,1)S(1)}, u32[]{:S(2)}, u32[]{:S(2)}) collective-permute-start(bf16[128,1024]{1,0:T(8,128)(2,1)S(1)} %get-tuple-element.101), channel_id=1, source_target_pairs={{0,8},{4,20},{8,0},{12,28},{16,24},{20,4},{24,16},{28,12},{1,9},{5... | collective-permute-start | bytes 786440 | tf_op jit(solution)/shard_map/ppermute | solution.py:40
  31.5 6.1 %collective-permute-start.10 = (bf16[256,1024]{1,0:T(8,128)(2,1)S(1)}, bf16[256,1024]{1,0:T(8,128)(2,1)S(1)}, u32[]{:S(2)}, u32[]{:S(2)}) collective-permute-start(bf16[256,1024]{1,0:T(8,128)(2,1)S(1)} %constant_dynamic-update-slice_fusion.2.mine), channel_id=1, source_target_pairs={{0,4},{4,0},{8,12},{12,8},{16,20},{20,16},{24,28},{28,24},{1,5},{5... | collective-permute-start | bytes 1572872 | tf_op jit(solution)/shard_map/ppermute | solution.py:34
  32.0 9.8 %collective-permute-start.7 = (bf16[256,1024]{1,0:T(8,128)(2,1)S(1)}, bf16[256,1024]{1,0:T(8,128)(2,1)S(1)}, u32[]{:S(2)}, u32[]{:S(2)}) collective-permute-start(bf16[256,1024]{1,0:T(8,128)(2,1)S(1)} %constant_dynamic-update-slice_fusion.2.mine), channel_id=1, source_target_pairs={{0,16},{4,12},{8,24},{12,4},{16,0},{20,28},{24,8},{28,20},{1,17},{... | collective-permute-start | bytes 1572872 | tf_op jit(solution)/shard_map/ppermute | solution.py:40
  49.2 2.8 %collective-permute-start.13 = (bf16[256,1024]{1,0:T(8,128)(2,1)S(1)}, bf16[256,1024]{1,0:T(8,128)(2,1)S(1)}, u32[]{:S(2)}, u32[]{:S(2)}) collective-permute-start(bf16[256,1024]{1,0:T(8,128)(2,1)S(1)} %shard_map.85), channel_id=1, source_target_pairs={{0,4},{4,0},{8,12},{12,8},{16,20},{20,16},{24,28},{28,24},{1,5},{5... | collective-permute-start | bytes 1572872 | tf_op jit(solution)/shard_map/ppermute | solution.py:34
  51.6 4.2 %collective-permute-start.12 = (bf16[256,1024]{1,0:T(8,128)(2,1)S(1)}, bf16[256,1024]{1,0:T(8,128)(2,1)S(1)}, u32[]{:S(2)}, u32[]{:S(2)}) collective-permute-start(bf16[256,1024]{1,0:T(8,128)(2,1)S(1)} %get-tuple-element.80), channel_id=1, source_target_pairs={{0,4},{4,0},{8,12},{12,8},{16,20},{20,16},{24,28},{28,24},{1,5},{5... | collective-permute-start | bytes 1572872 | tf_op jit(solution)/shard_map/ppermute | solution.py:34
  54.2 7.4 %collective-permute-start.16 = (bf16[256,1024]{1,0:T(8,128)(2,1)S(1)}, bf16[256,1024]{1,0:T(8,128)(2,1)S(1)}, u32[]{:S(2)}, u32[]{:S(2)}) collective-permute-start(bf16[256,1024]{1,0:T(8,128)(2,1)S(1)} %get-tuple-element.87), channel_id=1, source_target_pairs={{0,4},{4,0},{8,12},{12,8},{16,20},{20,16},{24,28},{28,24},{1,5},{5... | collective-permute-start | bytes 1572872 | tf_op jit(solution)/shard_map/ppermute | solution.py:34
  54.4 6.4 %collective-permute-start.17 = (bf16[128,1024]{1,0:T(8,128)(2,1)S(1)}, bf16[128,1024]{1,0:T(8,128)(2,1)S(1)}, u32[]{:S(2)}, u32[]{:S(2)}) collective-permute-start(bf16[128,1024]{1,0:T(8,128)(2,1)S(1)} %add_convert_fusion.3), channel_id=1, source_target_pairs={{0,16},{4,12},{8,24},{12,4},{16,0},{20,28},{24,8},{28,20},{1,17},{... | collective-permute-start | bytes 786440 | tf_op jit(solution)/shard_map/ppermute | solution.py:40
  55.9 8.2 %collective-permute-start.15 = (bf16[128,1024]{1,0:T(8,128)(2,1)S(1)}, bf16[128,1024]{1,0:T(8,128)(2,1)S(1)}, u32[]{:S(2)}, u32[]{:S(2)}) collective-permute-start(bf16[128,1024]{1,0:T(8,128)(2,1)S(1)} %add_convert_fusion.2), channel_id=1, source_target_pairs={{0,16},{4,12},{8,24},{12,4},{16,0},{20,28},{24,8},{28,20},{1,17},{... | collective-permute-start | bytes 786440 | tf_op jit(solution)/shard_map/ppermute | solution.py:40
  59.7 6.6 %collective-permute-start.14 = (bf16[256,1024]{1,0:T(8,128)(2,1)S(1)}, bf16[256,1024]{1,0:T(8,128)(2,1)S(1)}, u32[]{:S(2)}, u32[]{:S(2)}) collective-permute-start(bf16[256,1024]{1,0:T(8,128)(2,1)S(1)} %get-tuple-element.85), channel_id=1, source_target_pairs={{0,4},{4,0},{8,12},{12,8},{16,20},{20,16},{24,28},{28,24},{1,5},{5... | collective-permute-start | bytes 1572872 | tf_op jit(solution)/shard_map/ppermute | solution.py:34
  60.8 6.2 %collective-permute-start.21 = (bf16[64,1024]{1,0:T(8,128)(2,1)S(1)}, bf16[64,1024]{1,0:T(8,128)(2,1)S(1)}, u32[]{:S(2)}, u32[]{:S(2)}) collective-permute-start(bf16[64,1024]{1,0:T(8,128)(2,1)S(1)} %add_convert_fusion.11), channel_id=1, source_target_pairs={{0,8},{4,20},{8,0},{12,28},{16,24},{20,4},{24,16},{28,12},{1,9},{5... | collective-permute-start | bytes 393224 | tf_op jit(solution)/shard_map/ppermute | solution.py:40
  64.2 6.6 %collective-permute-start.20 = (bf16[64,1024]{1,0:T(8,128)(2,1)S(1)}, bf16[64,1024]{1,0:T(8,128)(2,1)S(1)}, u32[]{:S(2)}, u32[]{:S(2)}) collective-permute-start(bf16[64,1024]{1,0:T(8,128)(2,1)S(1)} %add_convert_fusion.10), channel_id=1, source_target_pairs={{0,8},{4,20},{8,0},{12,28},{16,24},{20,4},{24,16},{28,12},{1,9},{5... | collective-permute-start | bytes 393224 | tf_op jit(solution)/shard_map/ppermute | solution.py:40
  64.9 8.1 %collective-permute-start.19 = (bf16[128,1024]{1,0:T(8,128)(2,1)S(1)}, bf16[128,1024]{1,0:T(8,128)(2,1)S(1)}, u32[]{:S(2)}, u32[]{:S(2)}) collective-permute-start(bf16[128,1024]{1,0:T(8,128)(2,1)S(1)} %add_convert_fusion.1), channel_id=1, source_target_pairs={{0,16},{4,12},{8,24},{12,4},{16,0},{20,28},{24,8},{28,20},{1,17},{... | collective-permute-start | bytes 786440 | tf_op jit(solution)/shard_map/ppermute | solution.py:40
  66.3 8.2 %collective-permute-start.18 = (bf16[128,1024]{1,0:T(8,128)(2,1)S(1)}, bf16[128,1024]{1,0:T(8,128)(2,1)S(1)}, u32[]{:S(2)}, u32[]{:S(2)}) collective-permute-start(bf16[128,1024]{1,0:T(8,128)(2,1)S(1)} %add_convert_fusion), channel_id=1, source_target_pairs={{0,16},{4,12},{8,24},{12,4},{16,0},{20,28},{24,8},{28,20},{1,17},{... | collective-permute-start | bytes 786440 | tf_op jit(solution)/shard_map/ppermute | solution.py:40
  67.1 13.0 %collective-permute-start.26 = (bf16[64,1024]{1,0:T(8,128)(2,1)S(1)}, bf16[64,1024]{1,0:T(8,128)(2,1)S(1)}, u32[]{:S(2)}, u32[]{:S(2)}) collective-permute-start(bf16[64,1024]{1,0:T(8,128)(2,1)S(1)} %add_convert_fusion.9), channel_id=1, source_target_pairs={{0,3},{1,2},{2,1},{3,0},{4,7},{5,6},{6,5},{7,4},{8,11},{9,10},{10,... | collective-permute-start | bytes 393224 | tf_op jit(solution)/shard_map/ppermute | solution.py:34
  70.9 9.9 %collective-permute-start.25 = (bf16[64,1024]{1,0:T(8,128)(2,1)S(1)}, bf16[64,1024]{1,0:T(8,128)(2,1)S(1)}, u32[]{:S(2)}, u32[]{:S(2)}) collective-permute-start(bf16[64,1024]{1,0:T(8,128)(2,1)S(1)} %add_convert_fusion.8), channel_id=1, source_target_pairs={{0,2},{1,3},{2,0},{3,1},{4,6},{5,7},{6,4},{7,5},{8,10},{9,11},{10,... | collective-permute-start | bytes 393224 | tf_op jit(solution)/shard_map/ppermute | solution.py:34
  73.1 5.0 %collective-permute-start.23 = (bf16[64,1024]{1,0:T(8,128)(2,1)S(1)}, bf16[64,1024]{1,0:T(8,128)(2,1)S(1)}, u32[]{:S(2)}, u32[]{:S(2)}) collective-permute-start(bf16[64,1024]{1,0:T(8,128)(2,1)S(1)} %add_convert_fusion.7), channel_id=1, source_target_pairs={{0,8},{4,20},{8,0},{12,28},{16,24},{20,4},{24,16},{28,12},{1,9},{5... | collective-permute-start | bytes 393224 | tf_op jit(solution)/shard_map/ppermute | solution.py:40
  74.6 5.5 %collective-permute-start.22 = (bf16[64,1024]{1,0:T(8,128)(2,1)S(1)}, bf16[64,1024]{1,0:T(8,128)(2,1)S(1)}, u32[]{:S(2)}, u32[]{:S(2)}) collective-permute-start(bf16[64,1024]{1,0:T(8,128)(2,1)S(1)} %add_convert_fusion.6), channel_id=1, source_target_pairs={{0,8},{4,20},{8,0},{12,28},{16,24},{20,4},{24,16},{28,12},{1,9},{5... | collective-permute-start | bytes 393224 | tf_op jit(solution)/shard_map/ppermute | solution.py:40
  78.2 5.0 %collective-permute-start.24 = (bf16[64,1024]{1,0:T(8,128)(2,1)S(1)}, bf16[64,1024]{1,0:T(8,128)(2,1)S(1)}, u32[]{:S(2)}, u32[]{:S(2)}) collective-permute-start(bf16[64,1024]{1,0:T(8,128)(2,1)S(1)} %add_convert_fusion.5), channel_id=1, source_target_pairs={{0,1},{1,0},{2,3},{3,2},{4,5},{5,4},{6,7},{7,6},{8,9},{9,8},{10,11... | collective-permute-start | bytes 393224 | tf_op jit(solution)/shard_map/ppermute | solution.py:34
  (11 other events, 119.4 us)

commit v4 on v3

--- a/solution.py
+++ b/solution.py
@@ -13,7 +13,7 @@
 UP_GROUPS = ((0, 1), (2, 3))
 DOWN_ORDER = (
     ("o3",), ("m3", "o2"), ("h3",), ("m2", "o1"), ("h2",), ("m1", "o0", "m0"), ("h3",), ("h1",), ("h2",),
-    ("h0",), ("f3",), ("f2",), ("h1",), ("h0",), ("f1",), ("f0",),
+    ("h0",), ("f3",), ("h1",), ("f2",), ("h0",), ("f1",), ("f0",),
 )
 VMEM = pl.BlockSpec(memory_space=pltpu.VMEM)
 SMEM = pl.BlockSpec(memory_space=pltpu.SMEM)
@@ -372,6 +372,7 @@
     own = [jnp.concatenate([arrived[d] for d in group], axis=0) for group in up_groups]
     token = marker(3000000000, *(arrived[d] for group in up_groups[1:] for d in group))
     gate_rows, up_rows, joined, mine, theirs = [], [], [], [], []
+    far = []
     for g, group in enumerate(up_groups):
         if g == 0:
             gate_rows.append(fetch_rows(group, after(w_gate, chosen[0]), features))
@@ -384,12 +385,9 @@
         for step in range(steps - 2):
             value = hop_and_join(value, step, steps)
         received = hop(value, steps - 2, steps)
+        early = hop(value, steps - 1, steps)
         if g == 0:
-            value = gate(value, token)
-        if g != 1:
-            value = jnp.concatenate([value, received], axis=0)
-        if g == 0:
-            value = after(value, up_rows[0], gate_rows[-1])
+            received = gate(after(received, up_rows[0], gate_rows[-1], early), token)
         elif g == 1:
             near_theirs = exchange(joined[0], "dp", 1)
             near = after(joined[0], own[1])
@@ -397,23 +395,25 @@
                 len(up_groups[0]), near, near_theirs, gate_rows[0], up_rows[0], None, None, None, model_width
             )
             up_rows.append(fetch_rows(group, after(w_up, near_sums[2]), features))
-            value = jnp.concatenate([value, after(received, up_rows[1])], axis=0)
+            received = after(received, up_rows[1], early)
+        far.append((early, hop(received, steps - 1, steps)))
+        value = jnp.concatenate([value, received], axis=0)
         joined.append(value)
-    far = [hop(value, steps - 1, steps) for value in joined]
-    far[0] = after(far[0], joined[1])
     far_sums = None
     for g, group in enumerate(up_groups):
         last = g == len(up_groups) - 1
         weights = (gate_rows[g], up_rows[g])
+        late = after(far[g][1], near_sums[2] if g == 0 else far_sums[2], joined[1])
+        rows = jnp.concatenate([far[g][0], late], axis=0)
+        far_theirs = exchange(rows, "dp", 1)
         if g > 0:
             near_theirs = exchange(joined[g], "dp", 1)
-            near = after(joined[g], far_sums[2])
+            near = after(joined[g], rows)
             near_sums = gate_up(
                 len(group), near, near_theirs, *weights, near_sums, 0 if last else None, None, model_width
             )
-        rows = after(far[g], near_sums[-1])
+            rows = after(rows, near_sums[-1])
         hidden = near_sums[0] if last else None
-        far_theirs = exchange(rows, "dp", 1)
         far_sums = gate_up(
             len(group), rows, far_theirs, *weights, far_sums, 1 if last else None, hidden, model_width
         )

time: 86.9 us -> 86.2 us (level)
  starting transfers between devices: 29.8 us -> 26.4 us
  waiting for transfers between devices: 14.8 us -> 17.1 us
    ppermute x16, starting transfers between devices: 15.4 us -> 12.1 us  [exchange(): return lax.ppermute(value, axis, [(i, i ^ offset) for i in range(count)])]
    ppermute x12 -> x14, waiting for transfers between devices: 7.73 us -> 10.9 us  [hop(): return lax.ppermute(value, 'dp', list(enumerate(turn)))]
    ppermute x12 -> x14, starting transfers between devices: 14.4 us -> 14.4 us  [hop(): return lax.ppermute(value, 'dp', list(enumerate(turn)))]
  transfers between devices with their start and end apart: 28 -> 30, of which waited for: 10 -> 14; matrix products, arithmetic and copies ran while one was open for 1% -> 1% of each run, Pallas kernels for 38% -> 39%
where the time goes in v4:
time: 86.2 us; the launch traced here: 86.1 us
  Pallas kernels  41.1 us (48%)
  starting transfers between devices  26.4 us (31%)
  waiting for transfers between devices  17.1 us (20%)
    pallas_call x4, Pallas kernels, gate_up(): pl.pallas_call(functools.partial(gate_up_kernel, count, first, place, mod...  16.5 us
    ppermute x14, starting transfers between devices, hop(): return lax.ppermute(value, 'dp', list(enumerate(turn)))  14.4 us
    pallas_call x4, Pallas kernels, fetch_rows(): pl.pallas_call(functools.partial(fetch_kernel, group, features), in_specs...  12.7 us
    ppermute x16, starting transfers between devices, exchange(): return lax.ppermute(value, axis, [(i, i ^ offset) for i in range(count)])  12.1 us
    ppermute x14, waiting for transfers between devices, hop(): return lax.ppermute(value, 'dp', list(enumerate(turn)))  10.9 us
    pallas_call x4, Pallas kernels, down(): pl.pallas_call(functools.partial(down_kernel, parts), in_specs=[VMEM, VME...  8.46 us
    ppermute x16, waiting for transfers between devices, exchange(): return lax.ppermute(value, axis, [(i, i ^ offset) for i in range(count)])  6.19 us
  transfers between devices with their start and end apart: 30, of which 14 were waited for; matrix products, arithmetic and copies ran while one was open for 1% of the time, Pallas kernels for 39%

profile of v4, /device:TPU:0, one launch (start us, length us, event | category | flops | bytes accessed | tf_op | source)
XLA Modules:
  0.0 86.1 jit_solution(4276196734079258110)
XLA Ops:
  2.5 3.0 %collective-permute-start.5 = (bf16[64,1024]{1,0:T(8,128)(2,1)S(1)}, bf16[64,1024]{1,0:T(8,128)(2,1)S(1)}, u32[]{:S(2)}, u32[]{:S(2)}) collective-permute-start(bf16[64,1024]{1,0:T(8,128)(2,1)S(1)} %get-tuple-element.59), channel_id=1, source_target_pairs={{0,1},{1,0},{2,3},{3,2},{4,5},{5,4},{6,7},{7,6},{8,9},{9,8},{10,11... | collective-permute-start | bytes 393224 | tf_op jit(solution)/shard_map/ppermute | solution.py:34
  5.6 2.6 %collective-permute-start.1 = (bf16[64,1024]{1,0:T(8,128)(2,1)S(1)}, bf16[64,1024]{1,0:T(8,128)(2,1)S(1)}, u32[]{:S(2)}, u32[]{:S(2)}) collective-permute-start(bf16[64,1024]{1,0:T(8,128)(2,1)S(1)} %get-tuple-element.56), channel_id=1, source_target_pairs={{0,2},{1,3},{2,0},{3,1},{4,6},{5,7},{6,4},{7,5},{8,10},{9,11},{10,... | collective-permute-start | bytes 393224 | tf_op jit(solution)/shard_map/ppermute | solution.py:34
  8.1 3.2 %shard_map.75.w_gate = bf16[2048,1792]{1,0:T(8,128)(2,1)S(1)} custom-call(bf16[1,4096,1792]{2,1,0:T(8,128)(2,1)} %weight.6), custom_call_target="tpu_custom_call" | custom-call | tf_op jit(solution)/shard_map/pallas_call | solution.py:190
  11.4 1.8 %collective-permute-start.7 = (bf16[128,1024]{1,0:T(8,128)(2,1)S(1)}, bf16[128,1024]{1,0:T(8,128)(2,1)S(1)}, u32[]{:S(2)}, u32[]{:S(2)}) collective-permute-start(bf16[128,1024]{1,0:T(8,128)(2,1)S(1)} %pad_maximum_fusion.1), channel_id=1, source_target_pairs={{0,16},{4,12},{8,24},{12,4},{16,0},{20,28},{24,8},{28,20},{1,17},{... | collective-permute-start | bytes 786440 | tf_op jit(solution)/shard_map/ppermute | solution.py:40
  13.2 1.5 %collective-permute-start.6 = (bf16[128,1024]{1,0:T(8,128)(2,1)S(1)}, bf16[128,1024]{1,0:T(8,128)(2,1)S(1)}, u32[]{:S(2)}, u32[]{:S(2)}) collective-permute-start(bf16[128,1024]{1,0:T(8,128)(2,1)S(1)} %pad_maximum_fusion.1), channel_id=1, source_target_pairs={{0,8},{4,20},{8,0},{12,28},{16,24},{20,4},{24,16},{28,12},{1,9},{5... | collective-permute-start | bytes 786440 | tf_op jit(solution)/shard_map/ppermute | solution.py:40
  14.7 3.2 %shard_map.76.w_up = bf16[2048,1792]{1,0:T(8,128)(2,1)S(1)} custom-call(bf16[1,4096,1792]{2,1,0:T(8,128)(2,1)} %weight.7), custom_call_target="tpu_custom_call" | custom-call | tf_op jit(solution)/shard_map/pallas_call | solution.py:190
  17.8 3.2 %shard_map.77.w_gate = bf16[2048,1792]{1,0:T(8,128)(2,1)S(1)} custom-call(bf16[1,4096,1792]{2,1,0:T(8,128)(2,1)} %weight.6), custom_call_target="tpu_custom_call" | custom-call | tf_op jit(solution)/shard_map/pallas_call | solution.py:190
  23.9 4.0 %shard_map.80 = (f32[256,1792]{1,0:T(8,128)S(1)}, f32[256,1792]{1,0:T(8,128)S(1)}, f32[256,128]{1,0:T(8,128)S(1)}) custom-call(bf16[256,1024]{1,0:T(8,128)(2,1)S(1)} %pad_maximum_fusion.mine, bf16[256,1024]{1,0:T(8,128)(2,1)S(1)} %collective-permute-done.8.theirs, bf16[2048,1792]{1,0:T(8,128)(2,1)S(1)} %shard_map.75.w_gate, ...), custom_call_target="tpu_custom_call" | custom-call | flops 3758096384 | bytes 14680064 | tf_op jit(solution)/shard_map/pallas_call | solution.py:270
  27.9 3.2 %shard_map.81.w_up = bf16[2048,1792]{1,0:T(8,128)(2,1)S(1)} custom-call(bf16[1,4096,1792]{2,1,0:T(8,128)(2,1)} %weight.7), custom_call_target="tpu_custom_call" | custom-call | tf_op jit(solution)/shard_map/pallas_call | solution.py:190
  31.4 1.7 %collective-permute-done.10 = bf16[128,1024]{1,0:T(8,128)(2,1)S(1)} collective-permute-done((bf16[128,1024]{1,0:T(8,128)(2,1)S(1)}, bf16[128,1024]{1,0:T(8,128)(2,1)S(1)}, u32[]{:S(2)}, u32[]{:S(2)}) %collective-permute-start.10) | collective-permute-done | bytes 262176 | tf_op jit(solution)/shard_map/ppermute | solution.py:40
  35.1 4.0 %shard_map.82 = (f32[256,1792]{1,0:T(8,128)S(1)}, f32[256,1792]{1,0:T(8,128)S(1)}, f32[256,128]{1,0:T(8,128)S(1)}) custom-call(bf16[256,1024]{1,0:T(8,128)(2,1)S(1)} %constant_dynamic-update-slice_fusion.5.mine, bf16[256,1024]{1,0:T(8,128)(2,1)S(1)} %collective-permute-done.11.theirs, bf16[2048,1792]{1,0:T(8,128)(2,1)S(1)} %shard_map.75.w_gate, ...), custom_call_target="tpu_custom_call" | custom-call | flops 3758096384 | bytes 14680064 | tf_op jit(solution)/shard_map/pallas_call | solution.py:270
  39.8 4.1 %shard_map.83.refs_3_ = bf16[512,1792]{1,0:T(8,128)(2,1)S(1)} custom-call(bf16[256,1024]{1,0:T(8,128)(2,1)S(1)} %constant_dynamic-update-slice_fusion.2.mine, bf16[256,1024]{1,0:T(8,128)(2,1)S(1)} %collective-permute-done.12.theirs, bf16[2048,1792]{1,0:T(8,128)(2,1)S(1)} %shard_map.77.w_gate, bf16[2048,1792]{1,0:T(8,128)(2,1)S(1)} %shard_map.81.w_up, ...), custom_call_target="tpu_custom_call" | custom-call | flops 3758096384 | bytes 14680064 | tf_op jit(solution)/shard_map/pallas_call | solution.py:270
  44.0 4.4 %shard_map.84.hidden = bf16[512,1792]{1,0:T(8,128)(2,1)S(1)} custom-call(bf16[256,1024]{1,0:T(8,128)(2,1)S(1)} %constant_dynamic-update-slice_fusion.7.mine, bf16[256,1024]{1,0:T(8,128)(2,1)S(1)} %collective-permute-done.13.theirs, bf16[2048,1792]{1,0:T(8,128)(2,1)S(1)} %shard_map.77.w_gate, ...), custom_call_target="tpu_custom_call", output_to_operand_aliasing={{}: (7, {})} | custom-call | flops 3758096384 | bytes 14680064 | tf_op jit(solution)/shard_map/pallas_call | solution.py:270
  50.1 2.1 %shard_map.86 = (bf16[256,1024]{1,0:T(8,128)(2,1)S(1)}, bf16[256,1024]{1,0:T(8,128)(2,1)S(1)}) custom-call(bf16[512,1792]{1,0:T(8,128)(2,1)S(1)} %shard_map.84.hidden, bf16[1,1792,4096]{2,1,0:T(8,128)(2,1)S(1)} %bitcast.1), custom_call_target="tpu_custom_call" | custom-call | tf_op jit(solution)/shard_map/pallas_call | solution.py:303
  52.4 2.1 %shard_map.87 = (bf16[256,1024]{1,0:T(8,128)(2,1)S(1)}, bf16[256,1024]{1,0:T(8,128)(2,1)S(1)}) custom-call(bf16[512,1792]{1,0:T(8,128)(2,1)S(1)} %shard_map.84.hidden, bf16[1,1792,4096]{2,1,0:T(8,128)(2,1)S(1)} %bitcast.1), custom_call_target="tpu_custom_call" | custom-call | tf_op jit(solution)/shard_map/pallas_call | solution.py:303
  57.3 3.1 %shard_map.88 = (bf16[256,1024]{1,0:T(8,128)(2,1)S(1)}, bf16[256,1024]{1,0:T(8,128)(2,1)S(1)}, bf16[256,1024]{1,0:T(8,128)(2,1)S(1)}) custom-call(bf16[512,1792]{1,0:T(8,128)(2,1)S(1)} %shard_map.84.hidden, bf16[1,1792,4096]{2,1,0:T(8,128)(2,1)S(1)} %bitcast.1), custom_call_target="tpu_custom_call" | custom-call | tf_op jit(solution)/shard_map/pallas_call | solution.py:303
  63.3 1.5 %collective-permute-done.17 = bf16[128,1024]{1,0:T(8,128)(2,1)S(1)} collective-permute-done((bf16[128,1024]{1,0:T(8,128)(2,1)S(1)}, bf16[128,1024]{1,0:T(8,128)(2,1)S(1)}, u32[]{:S(2)}, u32[]{:S(2)}) %collective-permute-start.17) | collective-permute-done | bytes 262176 | tf_op jit(solution)/shard_map/ppermute | solution.py:40
  66.7 1.3 %collective-permute-done.23 = bf16[64,1024]{1,0:T(8,128)(2,1)S(1)} collective-permute-done((bf16[64,1024]{1,0:T(8,128)(2,1)S(1)}, bf16[64,1024]{1,0:T(8,128)(2,1)S(1)}, u32[]{:S(2)}, u32[]{:S(2)}) %collective-permute-start.23) | collective-permute-done | bytes 131104 | tf_op jit(solution)/shard_map/ppermute | solution.py:40
  68.0 3.7 %collective-permute-start.28 = (bf16[64,1024]{1,0:T(8,128)(2,1)S(1)}, bf16[64,1024]{1,0:T(8,128)(2,1)S(1)}, u32[]{:S(2)}, u32[]{:S(2)}) collective-permute-start(bf16[64,1024]{1,0:T(8,128)(2,1)S(1)} %add_convert_fusion.9), channel_id=1, source_target_pairs={{0,3},{1,2},{2,1},{3,0},{4,7},{5,6},{6,5},{7,4},{8,11},{9,10},{10,... | collective-permute-start | bytes 393224 | tf_op jit(solution)/shard_map/ppermute | solution.py:34
  75.3 1.5 %collective-permute-done.25 = bf16[64,1024]{1,0:T(8,128)(2,1)S(1)} collective-permute-done((bf16[64,1024]{1,0:T(8,128)(2,1)S(1)}, bf16[64,1024]{1,0:T(8,128)(2,1)S(1)}, u32[]{:S(2)}, u32[]{:S(2)}) %collective-permute-start.25) | collective-permute-done | bytes 131104 | tf_op jit(solution)/shard_map/ppermute | solution.py:40
  77.0 2.2 %collective-permute-done.24 = bf16[64,1024]{1,0:T(8,128)(2,1)S(1)} collective-permute-done((bf16[64,1024]{1,0:T(8,128)(2,1)S(1)}, bf16[64,1024]{1,0:T(8,128)(2,1)S(1)}, u32[]{:S(2)}, u32[]{:S(2)}) %collective-permute-start.24) | collective-permute-done | bytes 131104 | tf_op jit(solution)/shard_map/ppermute | solution.py:40
  79.3 1.3 %collective-permute-done.27.refs_2_ = bf16[64,1024]{1,0:T(8,128)(2,1)S(1)} collective-permute-done((bf16[64,1024]{1,0:T(8,128)(2,1)S(1)}, bf16[64,1024]{1,0:T(8,128)(2,1)S(1)}, u32[]{:S(2)}, u32[]{:S(2)}) %collective-permute-start.27) | collective-permute-done | bytes 131104 | tf_op jit(solution)/shard_map/ppermute | solution.py:34
  80.6 2.0 %collective-permute-done.26.refs_1_ = bf16[64,1024]{1,0:T(8,128)(2,1)S(1)} collective-permute-done((bf16[64,1024]{1,0:T(8,128)(2,1)S(1)}, bf16[64,1024]{1,0:T(8,128)(2,1)S(1)}, u32[]{:S(2)}, u32[]{:S(2)}) %collective-permute-start.26) | collective-permute-done | bytes 131104 | tf_op jit(solution)/shard_map/ppermute | solution.py:34
  83.7 1.5 %collective-permute-done.29.received = bf16[2,64,1024]{2,1,0:T(8,128)(2,1)S(1)} collective-permute-done((bf16[2,64,1024]{2,1,0:T(8,128)(2,1)S(1)}, bf16[2,64,1024]{2,1,0:T(8,128)(2,1)S(1)}, u32[]{:S(2)}, u32[]{:S(2)}) %collective-permute-start.29) | collective-permute-done | bytes 262176 | tf_op jit(solution)/shard_map/ppermute | solution.py:34
  (90 shorter events, 23.7 us)
Async XLA Ops:
  2.5 8.8 %collective-permute-start.5 = (bf16[64,1024]{1,0:T(8,128)(2,1)S(1)}, bf16[64,1024]{1,0:T(8,128)(2,1)S(1)}, u32[]{:S(2)}, u32[]{:S(2)}) collective-permute-start(bf16[64,1024]{1,0:T(8,128)(2,1)S(1)} %get-tuple-element.59), channel_id=1, source_target_pairs={{0,1},{1,0},{2,3},{3,2},{4,5},{5,4},{6,7},{7,6},{8,9},{9,8},{10,11... | collective-permute-start | bytes 393224 | tf_op jit(solution)/shard_map/ppermute | solution.py:34
  5.6 15.5 %collective-permute-start.1 = (bf16[64,1024]{1,0:T(8,128)(2,1)S(1)}, bf16[64,1024]{1,0:T(8,128)(2,1)S(1)}, u32[]{:S(2)}, u32[]{:S(2)}) collective-permute-start(bf16[64,1024]{1,0:T(8,128)(2,1)S(1)} %get-tuple-element.56), channel_id=1, source_target_pairs={{0,2},{1,3},{2,0},{3,1},{4,6},{5,7},{6,4},{7,5},{8,10},{9,11},{10,... | collective-permute-start | bytes 393224 | tf_op jit(solution)/shard_map/ppermute | solution.py:34
  8.1 12.9 %collective-permute-start.2 = (bf16[64,1024]{1,0:T(8,128)(2,1)S(1)}, bf16[64,1024]{1,0:T(8,128)(2,1)S(1)}, u32[]{:S(2)}, u32[]{:S(2)}) collective-permute-start(bf16[64,1024]{1,0:T(8,128)(2,1)S(1)} %get-tuple-element.57), channel_id=1, source_target_pairs={{0,3},{1,2},{2,1},{3,0},{4,7},{5,6},{6,5},{7,4},{8,11},{9,10},{10,... | collective-permute-start | bytes 393224 | tf_op jit(solution)/shard_map/ppermute | solution.py:34
  11.4 9.7 %collective-permute-start.7 = (bf16[128,1024]{1,0:T(8,128)(2,1)S(1)}, bf16[128,1024]{1,0:T(8,128)(2,1)S(1)}, u32[]{:S(2)}, u32[]{:S(2)}) collective-permute-start(bf16[128,1024]{1,0:T(8,128)(2,1)S(1)} %pad_maximum_fusion.1), channel_id=1, source_target_pairs={{0,16},{4,12},{8,24},{12,4},{16,0},{20,28},{24,8},{28,20},{1,17},{... | collective-permute-start | bytes 786440 | tf_op jit(solution)/shard_map/ppermute | solution.py:40
  13.2 7.9 %collective-permute-start.6 = (bf16[128,1024]{1,0:T(8,128)(2,1)S(1)}, bf16[128,1024]{1,0:T(8,128)(2,1)S(1)}, u32[]{:S(2)}, u32[]{:S(2)}) collective-permute-start(bf16[128,1024]{1,0:T(8,128)(2,1)S(1)} %pad_maximum_fusion.1), channel_id=1, source_target_pairs={{0,8},{4,20},{8,0},{12,28},{16,24},{20,4},{24,16},{28,12},{1,9},{5... | collective-permute-start | bytes 786440 | tf_op jit(solution)/shard_map/ppermute | solution.py:40
  21.3 9.8 %collective-permute-start.3 = (bf16[128,1024]{1,0:T(8,128)(2,1)S(1)}, bf16[128,1024]{1,0:T(8,128)(2,1)S(1)}, u32[]{:S(2)}, u32[]{:S(2)}) collective-permute-start(bf16[128,1024]{1,0:T(8,128)(2,1)S(1)} %get-tuple-element.102), channel_id=1, source_target_pairs={{0,16},{4,12},{8,24},{12,4},{16,0},{20,28},{24,8},{28,20},{1,17},{... | collective-permute-start | bytes 786440 | tf_op jit(solution)/shard_map/ppermute | solution.py:40
  22.2 9.2 %collective-permute-start.4 = (bf16[128,1024]{1,0:T(8,128)(2,1)S(1)}, bf16[128,1024]{1,0:T(8,128)(2,1)S(1)}, u32[]{:S(2)}, u32[]{:S(2)}) collective-permute-start(bf16[128,1024]{1,0:T(8,128)(2,1)S(1)} %get-tuple-element.102), channel_id=1, source_target_pairs={{0,8},{4,20},{8,0},{12,28},{16,24},{20,4},{24,16},{28,12},{1,9},{5... | collective-permute-start | bytes 786440 | tf_op jit(solution)/shard_map/ppermute | solution.py:40
  22.7 10.4 %collective-permute-start.10 = (bf16[128,1024]{1,0:T(8,128)(2,1)S(1)}, bf16[128,1024]{1,0:T(8,128)(2,1)S(1)}, u32[]{:S(2)}, u32[]{:S(2)}) collective-permute-start(bf16[128,1024]{1,0:T(8,128)(2,1)S(1)} %shard_map.79), channel_id=1, source_target_pairs={{0,16},{4,12},{8,24},{12,4},{16,0},{20,28},{24,8},{28,20},{1,17},{... | collective-permute-start | bytes 786440 | tf_op jit(solution)/shard_map/ppermute | solution.py:40
  33.2 6.4 %collective-permute-start.9 = (bf16[128,1024]{1,0:T(8,128)(2,1)S(1)}, bf16[128,1024]{1,0:T(8,128)(2,1)S(1)}, u32[]{:S(2)}, u32[]{:S(2)}) collective-permute-start(bf16[128,1024]{1,0:T(8,128)(2,1)S(1)} %collective-permute-done.4), channel_id=1, source_target_pairs={{0,16},{4,12},{8,24},{12,4},{16,0},{20,28},{24,8},{28,20},{1,17},{... | collective-permute-start | bytes 786440 | tf_op jit(solution)/shard_map/ppermute | solution.py:40
  34.2 5.6 %collective-permute-start.12 = (bf16[256,1024]{1,0:T(8,128)(2,1)S(1)}, bf16[256,1024]{1,0:T(8,128)(2,1)S(1)}, u32[]{:S(2)}, u32[]{:S(2)}) collective-permute-start(bf16[256,1024]{1,0:T(8,128)(2,1)S(1)} %constant_dynamic-update-slice_fusion.2.mine), channel_id=1, source_target_pairs={{0,4},{4,0},{8,12},{12,8},{16,20},{20,16},{24,28},{28,24},{1,5},{5... | collective-permute-start | bytes 1572872 | tf_op jit(solution)/shard_map/ppermute | solution.py:34
  39.7 4.3 %collective-permute-start.13 = (bf16[256,1024]{1,0:T(8,128)(2,1)S(1)}, bf16[256,1024]{1,0:T(8,128)(2,1)S(1)}, u32[]{:S(2)}, u32[]{:S(2)}) collective-permute-start(bf16[256,1024]{1,0:T(8,128)(2,1)S(1)} %constant_dynamic-update-slice_fusion.7.mine), channel_id=1, source_target_pairs={{0,4},{4,0},{8,12},{12,8},{16,20},{20,16},{24,28},{28,24},{1,5},{5... | collective-permute-start | bytes 1572872 | tf_op jit(solution)/shard_map/ppermute | solution.py:34
  54.6 7.8 %collective-permute-start.18 = (bf16[256,1024]{1,0:T(8,128)(2,1)S(1)}, bf16[256,1024]{1,0:T(8,128)(2,1)S(1)}, u32[]{:S(2)}, u32[]{:S(2)}) collective-permute-start(bf16[256,1024]{1,0:T(8,128)(2,1)S(1)} %get-tuple-element.87), channel_id=1, source_target_pairs={{0,4},{4,0},{8,12},{12,8},{16,20},{20,16},{24,28},{28,24},{1,5},{5... | collective-permute-start | bytes 1572872 | tf_op jit(solution)/shard_map/ppermute | solution.py:34
  55.1 6.4 %collective-permute-start.19 = (bf16[128,1024]{1,0:T(8,128)(2,1)S(1)}, bf16[128,1024]{1,0:T(8,128)(2,1)S(1)}, u32[]{:S(2)}, u32[]{:S(2)}) collective-permute-start(bf16[128,1024]{1,0:T(8,128)(2,1)S(1)} %add_convert_fusion.3), channel_id=1, source_target_pairs={{0,16},{4,12},{8,24},{12,4},{16,0},{20,28},{24,8},{28,20},{1,17},{... | collective-permute-start | bytes 786440 | tf_op jit(solution)/shard_map/ppermute | solution.py:40
  56.1 8.7 %collective-permute-start.17 = (bf16[128,1024]{1,0:T(8,128)(2,1)S(1)}, bf16[128,1024]{1,0:T(8,128)(2,1)S(1)}, u32[]{:S(2)}, u32[]{:S(2)}) collective-permute-start(bf16[128,1024]{1,0:T(8,128)(2,1)S(1)} %add_convert_fusion.2), channel_id=1, source_target_pairs={{0,16},{4,12},{8,24},{12,4},{16,0},{20,28},{24,8},{28,20},{1,17},{... | collective-permute-start | bytes 786440 | tf_op jit(solution)/shard_map/ppermute | solution.py:40
  60.4 5.3 %collective-permute-start.16 = (bf16[256,1024]{1,0:T(8,128)(2,1)S(1)}, bf16[256,1024]{1,0:T(8,128)(2,1)S(1)}, u32[]{:S(2)}, u32[]{:S(2)}) collective-permute-start(bf16[256,1024]{1,0:T(8,128)(2,1)S(1)} %get-tuple-element.85), channel_id=1, source_target_pairs={{0,4},{4,0},{8,12},{12,8},{16,20},{20,16},{24,28},{28,24},{1,5},{5... | collective-permute-start | bytes 1572872 | tf_op jit(solution)/shard_map/ppermute | solution.py:34
  61.5 6.4 %collective-permute-start.23 = (bf16[64,1024]{1,0:T(8,128)(2,1)S(1)}, bf16[64,1024]{1,0:T(8,128)(2,1)S(1)}, u32[]{:S(2)}, u32[]{:S(2)}) collective-permute-start(bf16[64,1024]{1,0:T(8,128)(2,1)S(1)} %add_convert_fusion.11), channel_id=1, source_target_pairs={{0,8},{4,20},{8,0},{12,28},{16,24},{20,4},{24,16},{28,12},{1,9},{5... | collective-permute-start | bytes 393224 | tf_op jit(solution)/shard_map/ppermute | solution.py:40
  62.4 9.3 %collective-permute-start.22 = (bf16[128,1024]{1,0:T(8,128)(2,1)S(1)}, bf16[128,1024]{1,0:T(8,128)(2,1)S(1)}, u32[]{:S(2)}, u32[]{:S(2)}) collective-permute-start(bf16[128,1024]{1,0:T(8,128)(2,1)S(1)} %add_convert_fusion.1), channel_id=1, source_target_pairs={{0,16},{4,12},{8,24},{12,4},{16,0},{20,28},{24,8},{28,20},{1,17},{... | collective-permute-start | bytes 786440 | tf_op jit(solution)/shard_map/ppermute | solution.py:40
  64.9 7.7 %collective-permute-start.21 = (bf16[64,1024]{1,0:T(8,128)(2,1)S(1)}, bf16[64,1024]{1,0:T(8,128)(2,1)S(1)}, u32[]{:S(2)}, u32[]{:S(2)}) collective-permute-start(bf16[64,1024]{1,0:T(8,128)(2,1)S(1)} %add_convert_fusion.10), channel_id=1, source_target_pairs={{0,8},{4,20},{8,0},{12,28},{16,24},{20,4},{24,16},{28,12},{1,9},{5... | collective-permute-start | bytes 393224 | tf_op jit(solution)/shard_map/ppermute | solution.py:40
  65.7 8.3 %collective-permute-start.20 = (bf16[128,1024]{1,0:T(8,128)(2,1)S(1)}, bf16[128,1024]{1,0:T(8,128)(2,1)S(1)}, u32[]{:S(2)}, u32[]{:S(2)}) collective-permute-start(bf16[128,1024]{1,0:T(8,128)(2,1)S(1)} %add_convert_fusion), channel_id=1, source_target_pairs={{0,16},{4,12},{8,24},{12,4},{16,0},{20,28},{24,8},{28,20},{1,17},{... | collective-permute-start | bytes 786440 | tf_op jit(solution)/shard_map/ppermute | solution.py:40
  68.0 11.3 %collective-permute-start.28 = (bf16[64,1024]{1,0:T(8,128)(2,1)S(1)}, bf16[64,1024]{1,0:T(8,128)(2,1)S(1)}, u32[]{:S(2)}, u32[]{:S(2)}) collective-permute-start(bf16[64,1024]{1,0:T(8,128)(2,1)S(1)} %add_convert_fusion.9), channel_id=1, source_target_pairs={{0,3},{1,2},{2,1},{3,0},{4,7},{5,6},{6,5},{7,4},{8,11},{9,10},{10,... | collective-permute-start | bytes 393224 | tf_op jit(solution)/shard_map/ppermute | solution.py:34
  71.7 5.0 %collective-permute-start.25 = (bf16[64,1024]{1,0:T(8,128)(2,1)S(1)}, bf16[64,1024]{1,0:T(8,128)(2,1)S(1)}, u32[]{:S(2)}, u32[]{:S(2)}) collective-permute-start(bf16[64,1024]{1,0:T(8,128)(2,1)S(1)} %add_convert_fusion.8), channel_id=1, source_target_pairs={{0,8},{4,20},{8,0},{12,28},{16,24},{20,4},{24,16},{28,12},{1,9},{5... | collective-permute-start | bytes 393224 | tf_op jit(solution)/shard_map/ppermute | solution.py:40
  72.6 7.9 %collective-permute-start.27 = (bf16[64,1024]{1,0:T(8,128)(2,1)S(1)}, bf16[64,1024]{1,0:T(8,128)(2,1)S(1)}, u32[]{:S(2)}, u32[]{:S(2)}) collective-permute-start(bf16[64,1024]{1,0:T(8,128)(2,1)S(1)} %add_convert_fusion.7), channel_id=1, source_target_pairs={{0,2},{1,3},{2,0},{3,1},{4,6},{5,7},{6,4},{7,5},{8,10},{9,11},{10,... | collective-permute-start | bytes 393224 | tf_op jit(solution)/shard_map/ppermute | solution.py:34
  74.1 5.0 %collective-permute-start.24 = (bf16[64,1024]{1,0:T(8,128)(2,1)S(1)}, bf16[64,1024]{1,0:T(8,128)(2,1)S(1)}, u32[]{:S(2)}, u32[]{:S(2)}) collective-permute-start(bf16[64,1024]{1,0:T(8,128)(2,1)S(1)} %add_convert_fusion.6), channel_id=1, source_target_pairs={{0,8},{4,20},{8,0},{12,28},{16,24},{20,4},{24,16},{28,12},{1,9},{5... | collective-permute-start | bytes 393224 | tf_op jit(solution)/shard_map/ppermute | solution.py:40
  76.8 5.7 %collective-permute-start.26 = (bf16[64,1024]{1,0:T(8,128)(2,1)S(1)}, bf16[64,1024]{1,0:T(8,128)(2,1)S(1)}, u32[]{:S(2)}, u32[]{:S(2)}) collective-permute-start(bf16[64,1024]{1,0:T(8,128)(2,1)S(1)} %add_convert_fusion.5), channel_id=1, source_target_pairs={{0,1},{1,0},{2,3},{3,2},{4,5},{5,4},{6,7},{7,6},{8,9},{9,8},{10,11... | collective-permute-start | bytes 393224 | tf_op jit(solution)/shard_map/ppermute | solution.py:34
  (13 other events, 120.7 us)

commit v5 on v4

--- a/solution.py
+++ b/solution.py
@@ -381,7 +381,7 @@
             up_rows.append(fetch_rows(group, after(w_up, own[g], *joined[-1:]), features))
         if g + 1 < len(up_groups):
             gate_rows.append(fetch_rows(up_groups[g + 1], after(w_gate, up_rows[-1]), features))
-        value = own[g]
+        value = after(own[g], joined[0]) if g == 1 else own[g]
         for step in range(steps - 2):
             value = hop_and_join(value, step, steps)
         received = hop(value, steps - 2, steps)

time: 86.2 us -> 86.2 us (level)
  no operation moved by 1% of the time
where the time goes in v5:
time: 86.2 us; the launch traced here: 86 us
  Pallas kernels  41.1 us (48%)
  starting transfers between devices  26.5 us (31%)
  waiting for transfers between devices  17 us (20%)
    pallas_call x4, Pallas kernels, gate_up(): pl.pallas_call(functools.partial(gate_up_kernel, count, first, place, mod...  16.5 us
    ppermute x14, starting transfers between devices, hop(): return lax.ppermute(value, 'dp', list(enumerate(turn)))  14.4 us
    pallas_call x4, Pallas kernels, fetch_rows(): pl.pallas_call(functools.partial(fetch_kernel, group, features), in_specs...  12.7 us
    ppermute x16, starting transfers between devices, exchange(): return lax.ppermute(value, axis, [(i, i ^ offset) for i in range(count)])  12.1 us
    ppermute x14, waiting for transfers between devices, hop(): return lax.ppermute(value, 'dp', list(enumerate(turn)))  10.8 us
    pallas_call x4, Pallas kernels, down(): pl.pallas_call(functools.partial(down_kernel, parts), in_specs=[VMEM, VME...  8.46 us
    ppermute x16, waiting for transfers between devices, exchange(): return lax.ppermute(value, axis, [(i, i ^ offset) for i in range(count)])  6.18 us
  transfers between devices with their start and end apart: 30, of which 14 were waited for; matrix products, arithmetic and copies ran while one was open for 1% of the time, Pallas kernels for 39%

profile of v5, /device:TPU:0, one launch (start us, length us, event | category | flops | bytes accessed | tf_op | source)
XLA Modules:
  0.0 86.0 jit_solution(10300050874543327067)
XLA Ops:
  2.5 3.0 %collective-permute-start.3 = (bf16[64,1024]{1,0:T(8,128)(2,1)S(1)}, bf16[64,1024]{1,0:T(8,128)(2,1)S(1)}, u32[]{:S(2)}, u32[]{:S(2)}) collective-permute-start(bf16[64,1024]{1,0:T(8,128)(2,1)S(1)} %get-tuple-element.60), channel_id=1, source_target_pairs={{0,1},{1,0},{2,3},{3,2},{4,5},{5,4},{6,7},{7,6},{8,9},{9,8},{10,11... | collective-permute-start | bytes 393224 | tf_op jit(solution)/shard_map/ppermute | solution.py:34
  5.6 2.6 %collective-permute-start.1 = (bf16[64,1024]{1,0:T(8,128)(2,1)S(1)}, bf16[64,1024]{1,0:T(8,128)(2,1)S(1)}, u32[]{:S(2)}, u32[]{:S(2)}) collective-permute-start(bf16[64,1024]{1,0:T(8,128)(2,1)S(1)} %get-tuple-element.57), channel_id=1, source_target_pairs={{0,2},{1,3},{2,0},{3,1},{4,6},{5,7},{6,4},{7,5},{8,10},{9,11},{10,... | collective-permute-start | bytes 393224 | tf_op jit(solution)/shard_map/ppermute | solution.py:34
  8.1 3.2 %shard_map.75.w_gate = bf16[2048,1792]{1,0:T(8,128)(2,1)S(1)} custom-call(bf16[1,4096,1792]{2,1,0:T(8,128)(2,1)} %weight.6), custom_call_target="tpu_custom_call" | custom-call | tf_op jit(solution)/shard_map/pallas_call | solution.py:190
  11.4 1.8 %collective-permute-start.5 = (bf16[128,1024]{1,0:T(8,128)(2,1)S(1)}, bf16[128,1024]{1,0:T(8,128)(2,1)S(1)}, u32[]{:S(2)}, u32[]{:S(2)}) collective-permute-start(bf16[128,1024]{1,0:T(8,128)(2,1)S(1)} %pad_maximum_fusion.1), channel_id=1, source_target_pairs={{0,16},{4,12},{8,24},{12,4},{16,0},{20,28},{24,8},{28,20},{1,17},{... | collective-permute-start | bytes 786440 | tf_op jit(solution)/shard_map/ppermute | solution.py:40
  13.2 1.5 %collective-permute-start.4 = (bf16[128,1024]{1,0:T(8,128)(2,1)S(1)}, bf16[128,1024]{1,0:T(8,128)(2,1)S(1)}, u32[]{:S(2)}, u32[]{:S(2)}) collective-permute-start(bf16[128,1024]{1,0:T(8,128)(2,1)S(1)} %pad_maximum_fusion.1), channel_id=1, source_target_pairs={{0,8},{4,20},{8,0},{12,28},{16,24},{20,4},{24,16},{28,12},{1,9},{5... | collective-permute-start | bytes 786440 | tf_op jit(solution)/shard_map/ppermute | solution.py:40
  14.7 3.2 %shard_map.76.w_up = bf16[2048,1792]{1,0:T(8,128)(2,1)S(1)} custom-call(bf16[1,4096,1792]{2,1,0:T(8,128)(2,1)} %weight.7), custom_call_target="tpu_custom_call" | custom-call | tf_op jit(solution)/shard_map/pallas_call | solution.py:190
  17.8 3.2 %shard_map.77.w_gate = bf16[2048,1792]{1,0:T(8,128)(2,1)S(1)} custom-call(bf16[1,4096,1792]{2,1,0:T(8,128)(2,1)} %weight.6), custom_call_target="tpu_custom_call" | custom-call | tf_op jit(solution)/shard_map/pallas_call | solution.py:190
  23.9 4.0 %shard_map.80 = (f32[256,1792]{1,0:T(8,128)S(1)}, f32[256,1792]{1,0:T(8,128)S(1)}, f32[256,128]{1,0:T(8,128)S(1)}) custom-call(bf16[256,1024]{1,0:T(8,128)(2,1)S(1)} %pad_maximum_fusion.mine, bf16[256,1024]{1,0:T(8,128)(2,1)S(1)} %collective-permute-done.8.theirs, bf16[2048,1792]{1,0:T(8,128)(2,1)S(1)} %shard_map.75.w_gate, ...), custom_call_target="tpu_custom_call" | custom-call | flops 3758096384 | bytes 14680064 | tf_op jit(solution)/shard_map/pallas_call | solution.py:270
  27.9 3.2 %shard_map.81.w_up = bf16[2048,1792]{1,0:T(8,128)(2,1)S(1)} custom-call(bf16[1,4096,1792]{2,1,0:T(8,128)(2,1)} %weight.7), custom_call_target="tpu_custom_call" | custom-call | tf_op jit(solution)/shard_map/pallas_call | solution.py:190
  31.4 1.7 %collective-permute-done.10 = bf16[128,1024]{1,0:T(8,128)(2,1)S(1)} collective-permute-done((bf16[128,1024]{1,0:T(8,128)(2,1)S(1)}, bf16[128,1024]{1,0:T(8,128)(2,1)S(1)}, u32[]{:S(2)}, u32[]{:S(2)}) %collective-permute-start.10) | collective-permute-done | bytes 262176 | tf_op jit(solution)/shard_map/ppermute | solution.py:40
  35.1 4.0 %shard_map.82 = (f32[256,1792]{1,0:T(8,128)S(1)}, f32[256,1792]{1,0:T(8,128)S(1)}, f32[256,128]{1,0:T(8,128)S(1)}) custom-call(bf16[256,1024]{1,0:T(8,128)(2,1)S(1)} %constant_dynamic-update-slice_fusion.4.mine, bf16[256,1024]{1,0:T(8,128)(2,1)S(1)} %collective-permute-done.11.theirs, bf16[2048,1792]{1,0:T(8,128)(2,1)S(1)} %shard_map.75.w_gate, ...), custom_call_target="tpu_custom_call" | custom-call | flops 3758096384 | bytes 14680064 | tf_op jit(solution)/shard_map/pallas_call | solution.py:270
  39.8 4.1 %shard_map.83.refs_3_ = bf16[512,1792]{1,0:T(8,128)(2,1)S(1)} custom-call(bf16[256,1024]{1,0:T(8,128)(2,1)S(1)} %constant_dynamic-update-slice_fusion.2.mine, bf16[256,1024]{1,0:T(8,128)(2,1)S(1)} %collective-permute-done.12.theirs, bf16[2048,1792]{1,0:T(8,128)(2,1)S(1)} %shard_map.77.w_gate, bf16[2048,1792]{1,0:T(8,128)(2,1)S(1)} %shard_map.81.w_up, ...), custom_call_target="tpu_custom_call" | custom-call | flops 3758096384 | bytes 14680064 | tf_op jit(solution)/shard_map/pallas_call | solution.py:270
  44.0 4.4 %shard_map.84.hidden = bf16[512,1792]{1,0:T(8,128)(2,1)S(1)} custom-call(bf16[256,1024]{1,0:T(8,128)(2,1)S(1)} %constant_dynamic-update-slice_fusion.6.mine, bf16[256,1024]{1,0:T(8,128)(2,1)S(1)} %collective-permute-done.13.theirs, bf16[2048,1792]{1,0:T(8,128)(2,1)S(1)} %shard_map.77.w_gate, ...), custom_call_target="tpu_custom_call", output_to_operand_aliasing={{}: (7, {})} | custom-call | flops 3758096384 | bytes 14680064 | tf_op jit(solution)/shard_map/pallas_call | solution.py:270
  50.1 2.1 %shard_map.86 = (bf16[256,1024]{1,0:T(8,128)(2,1)S(1)}, bf16[256,1024]{1,0:T(8,128)(2,1)S(1)}) custom-call(bf16[512,1792]{1,0:T(8,128)(2,1)S(1)} %shard_map.84.hidden, bf16[1,1792,4096]{2,1,0:T(8,128)(2,1)S(1)} %bitcast.1), custom_call_target="tpu_custom_call" | custom-call | tf_op jit(solution)/shard_map/pallas_call | solution.py:303
  52.4 2.1 %shard_map.87 = (bf16[256,1024]{1,0:T(8,128)(2,1)S(1)}, bf16[256,1024]{1,0:T(8,128)(2,1)S(1)}) custom-call(bf16[512,1792]{1,0:T(8,128)(2,1)S(1)} %shard_map.84.hidden, bf16[1,1792,4096]{2,1,0:T(8,128)(2,1)S(1)} %bitcast.1), custom_call_target="tpu_custom_call" | custom-call | tf_op jit(solution)/shard_map/pallas_call | solution.py:303
  57.3 3.1 %shard_map.88 = (bf16[256,1024]{1,0:T(8,128)(2,1)S(1)}, bf16[256,1024]{1,0:T(8,128)(2,1)S(1)}, bf16[256,1024]{1,0:T(8,128)(2,1)S(1)}) custom-call(bf16[512,1792]{1,0:T(8,128)(2,1)S(1)} %shard_map.84.hidden, bf16[1,1792,4096]{2,1,0:T(8,128)(2,1)S(1)} %bitcast.1), custom_call_target="tpu_custom_call" | custom-call | tf_op jit(solution)/shard_map/pallas_call | solution.py:303
  63.3 1.5 %collective-permute-done.17 = bf16[128,1024]{1,0:T(8,128)(2,1)S(1)} collective-permute-done((bf16[128,1024]{1,0:T(8,128)(2,1)S(1)}, bf16[128,1024]{1,0:T(8,128)(2,1)S(1)}, u32[]{:S(2)}, u32[]{:S(2)}) %collective-permute-start.17) | collective-permute-done | bytes 262176 | tf_op jit(solution)/shard_map/ppermute | solution.py:40
  66.6 1.3 %collective-permute-done.23 = bf16[64,1024]{1,0:T(8,128)(2,1)S(1)} collective-permute-done((bf16[64,1024]{1,0:T(8,128)(2,1)S(1)}, bf16[64,1024]{1,0:T(8,128)(2,1)S(1)}, u32[]{:S(2)}, u32[]{:S(2)}) %collective-permute-start.23) | collective-permute-done | bytes 131104 | tf_op jit(solution)/shard_map/ppermute | solution.py:40
  68.0 3.7 %collective-permute-start.28 = (bf16[64,1024]{1,0:T(8,128)(2,1)S(1)}, bf16[64,1024]{1,0:T(8,128)(2,1)S(1)}, u32[]{:S(2)}, u32[]{:S(2)}) collective-permute-start(bf16[64,1024]{1,0:T(8,128)(2,1)S(1)} %add_convert_fusion.9), channel_id=1, source_target_pairs={{0,3},{1,2},{2,1},{3,0},{4,7},{5,6},{6,5},{7,4},{8,11},{9,10},{10,... | collective-permute-start | bytes 393224 | tf_op jit(solution)/shard_map/ppermute | solution.py:34
  75.3 1.5 %collective-permute-done.25 = bf16[64,1024]{1,0:T(8,128)(2,1)S(1)} collective-permute-done((bf16[64,1024]{1,0:T(8,128)(2,1)S(1)}, bf16[64,1024]{1,0:T(8,128)(2,1)S(1)}, u32[]{:S(2)}, u32[]{:S(2)}) %collective-permute-start.25) | collective-permute-done | bytes 131104 | tf_op jit(solution)/shard_map/ppermute | solution.py:40
  77.0 2.2 %collective-permute-done.24 = bf16[64,1024]{1,0:T(8,128)(2,1)S(1)} collective-permute-done((bf16[64,1024]{1,0:T(8,128)(2,1)S(1)}, bf16[64,1024]{1,0:T(8,128)(2,1)S(1)}, u32[]{:S(2)}, u32[]{:S(2)}) %collective-permute-start.24) | collective-permute-done | bytes 131104 | tf_op jit(solution)/shard_map/ppermute | solution.py:40
  79.2 1.3 %collective-permute-done.27.refs_2_ = bf16[64,1024]{1,0:T(8,128)(2,1)S(1)} collective-permute-done((bf16[64,1024]{1,0:T(8,128)(2,1)S(1)}, bf16[64,1024]{1,0:T(8,128)(2,1)S(1)}, u32[]{:S(2)}, u32[]{:S(2)}) %collective-permute-start.27) | collective-permute-done | bytes 131104 | tf_op jit(solution)/shard_map/ppermute | solution.py:34
  80.5 2.0 %collective-permute-done.26.refs_1_ = bf16[64,1024]{1,0:T(8,128)(2,1)S(1)} collective-permute-done((bf16[64,1024]{1,0:T(8,128)(2,1)S(1)}, bf16[64,1024]{1,0:T(8,128)(2,1)S(1)}, u32[]{:S(2)}, u32[]{:S(2)}) %collective-permute-start.26) | collective-permute-done | bytes 131104 | tf_op jit(solution)/shard_map/ppermute | solution.py:34
  83.6 1.5 %collective-permute-done.29.received = bf16[2,64,1024]{2,1,0:T(8,128)(2,1)S(1)} collective-permute-done((bf16[2,64,1024]{2,1,0:T(8,128)(2,1)S(1)}, bf16[2,64,1024]{2,1,0:T(8,128)(2,1)S(1)}, u32[]{:S(2)}, u32[]{:S(2)}) %collective-permute-start.29) | collective-permute-done | bytes 262176 | tf_op jit(solution)/shard_map/ppermute | solution.py:34
  (91 shorter events, 23.7 us)
Async XLA Ops:
  2.5 8.8 %collective-permute-start.3 = (bf16[64,1024]{1,0:T(8,128)(2,1)S(1)}, bf16[64,1024]{1,0:T(8,128)(2,1)S(1)}, u32[]{:S(2)}, u32[]{:S(2)}) collective-permute-start(bf16[64,1024]{1,0:T(8,128)(2,1)S(1)} %get-tuple-element.60), channel_id=1, source_target_pairs={{0,1},{1,0},{2,3},{3,2},{4,5},{5,4},{6,7},{7,6},{8,9},{9,8},{10,11... | collective-permute-start | bytes 393224 | tf_op jit(solution)/shard_map/ppermute | solution.py:34
  5.6 15.5 %collective-permute-start.1 = (bf16[64,1024]{1,0:T(8,128)(2,1)S(1)}, bf16[64,1024]{1,0:T(8,128)(2,1)S(1)}, u32[]{:S(2)}, u32[]{:S(2)}) collective-permute-start(bf16[64,1024]{1,0:T(8,128)(2,1)S(1)} %get-tuple-element.57), channel_id=1, source_target_pairs={{0,2},{1,3},{2,0},{3,1},{4,6},{5,7},{6,4},{7,5},{8,10},{9,11},{10,... | collective-permute-start | bytes 393224 | tf_op jit(solution)/shard_map/ppermute | solution.py:34
  8.1 12.9 %collective-permute-start.2 = (bf16[64,1024]{1,0:T(8,128)(2,1)S(1)}, bf16[64,1024]{1,0:T(8,128)(2,1)S(1)}, u32[]{:S(2)}, u32[]{:S(2)}) collective-permute-start(bf16[64,1024]{1,0:T(8,128)(2,1)S(1)} %get-tuple-element.58), channel_id=1, source_target_pairs={{0,3},{1,2},{2,1},{3,0},{4,7},{5,6},{6,5},{7,4},{8,11},{9,10},{10,... | collective-permute-start | bytes 393224 | tf_op jit(solution)/shard_map/ppermute | solution.py:34
  11.4 9.7 %collective-permute-start.5 = (bf16[128,1024]{1,0:T(8,128)(2,1)S(1)}, bf16[128,1024]{1,0:T(8,128)(2,1)S(1)}, u32[]{:S(2)}, u32[]{:S(2)}) collective-permute-start(bf16[128,1024]{1,0:T(8,128)(2,1)S(1)} %pad_maximum_fusion.1), channel_id=1, source_target_pairs={{0,16},{4,12},{8,24},{12,4},{16,0},{20,28},{24,8},{28,20},{1,17},{... | collective-permute-start | bytes 786440 | tf_op jit(solution)/shard_map/ppermute | solution.py:40
  13.2 7.9 %collective-permute-start.4 = (bf16[128,1024]{1,0:T(8,128)(2,1)S(1)}, bf16[128,1024]{1,0:T(8,128)(2,1)S(1)}, u32[]{:S(2)}, u32[]{:S(2)}) collective-permute-start(bf16[128,1024]{1,0:T(8,128)(2,1)S(1)} %pad_maximum_fusion.1), channel_id=1, source_target_pairs={{0,8},{4,20},{8,0},{12,28},{16,24},{20,4},{24,16},{28,12},{1,9},{5... | collective-permute-start | bytes 786440 | tf_op jit(solution)/shard_map/ppermute | solution.py:40
  21.3 9.8 %collective-permute-start.6 = (bf16[128,1024]{1,0:T(8,128)(2,1)S(1)}, bf16[128,1024]{1,0:T(8,128)(2,1)S(1)}, u32[]{:S(2)}, u32[]{:S(2)}) collective-permute-start(bf16[128,1024]{1,0:T(8,128)(2,1)S(1)} %constant_dynamic-update-slice_fusion), channel_id=1, source_target_pairs={{0,16},{4,12},{8,24},{12,4},{16,0},{20,28},{24,8},{28,20},{1,17},{... | collective-permute-start | bytes 786440 | tf_op jit(solution)/shard_map/ppermute | solution.py:40
  22.2 9.2 %collective-permute-start.7 = (bf16[128,1024]{1,0:T(8,128)(2,1)S(1)}, bf16[128,1024]{1,0:T(8,128)(2,1)S(1)}, u32[]{:S(2)}, u32[]{:S(2)}) collective-permute-start(bf16[128,1024]{1,0:T(8,128)(2,1)S(1)} %constant_dynamic-update-slice_fusion), channel_id=1, source_target_pairs={{0,8},{4,20},{8,0},{12,28},{16,24},{20,4},{24,16},{28,12},{1,9},{5... | collective-permute-start | bytes 786440 | tf_op jit(solution)/shard_map/ppermute | solution.py:40
  22.7 10.4 %collective-permute-start.10 = (bf16[128,1024]{1,0:T(8,128)(2,1)S(1)}, bf16[128,1024]{1,0:T(8,128)(2,1)S(1)}, u32[]{:S(2)}, u32[]{:S(2)}) collective-permute-start(bf16[128,1024]{1,0:T(8,128)(2,1)S(1)} %shard_map.79), channel_id=1, source_target_pairs={{0,16},{4,12},{8,24},{12,4},{16,0},{20,28},{24,8},{28,20},{1,17},{... | collective-permute-start | bytes 786440 | tf_op jit(solution)/shard_map/ppermute | solution.py:40
  33.2 6.4 %collective-permute-start.9 = (bf16[128,1024]{1,0:T(8,128)(2,1)S(1)}, bf16[128,1024]{1,0:T(8,128)(2,1)S(1)}, u32[]{:S(2)}, u32[]{:S(2)}) collective-permute-start(bf16[128,1024]{1,0:T(8,128)(2,1)S(1)} %collective-permute-done.7), channel_id=1, source_target_pairs={{0,16},{4,12},{8,24},{12,4},{16,0},{20,28},{24,8},{28,20},{1,17},{... | collective-permute-start | bytes 786440 | tf_op jit(solution)/shard_map/ppermute | solution.py:40
  34.1 5.6 %collective-permute-start.12 = (bf16[256,1024]{1,0:T(8,128)(2,1)S(1)}, bf16[256,1024]{1,0:T(8,128)(2,1)S(1)}, u32[]{:S(2)}, u32[]{:S(2)}) collective-permute-start(bf16[256,1024]{1,0:T(8,128)(2,1)S(1)} %constant_dynamic-update-slice_fusion.2.mine), channel_id=1, source_target_pairs={{0,4},{4,0},{8,12},{12,8},{16,20},{20,16},{24,28},{28,24},{1,5},{5... | collective-permute-start | bytes 1572872 | tf_op jit(solution)/shard_map/ppermute | solution.py:34
  39.7 4.3 %collective-permute-start.13 = (bf16[256,1024]{1,0:T(8,128)(2,1)S(1)}, bf16[256,1024]{1,0:T(8,128)(2,1)S(1)}, u32[]{:S(2)}, u32[]{:S(2)}) collective-permute-start(bf16[256,1024]{1,0:T(8,128)(2,1)S(1)} %constant_dynamic-update-slice_fusion.6.mine), channel_id=1, source_target_pairs={{0,4},{4,0},{8,12},{12,8},{16,20},{20,16},{24,28},{28,24},{1,5},{5... | collective-permute-start | bytes 1572872 | tf_op jit(solution)/shard_map/ppermute | solution.py:34
  54.5 7.8 %collective-permute-start.18 = (bf16[256,1024]{1,0:T(8,128)(2,1)S(1)}, bf16[256,1024]{1,0:T(8,128)(2,1)S(1)}, u32[]{:S(2)}, u32[]{:S(2)}) collective-permute-start(bf16[256,1024]{1,0:T(8,128)(2,1)S(1)} %get-tuple-element.89), channel_id=1, source_target_pairs={{0,4},{4,0},{8,12},{12,8},{16,20},{20,16},{24,28},{28,24},{1,5},{5... | collective-permute-start | bytes 1572872 | tf_op jit(solution)/shard_map/ppermute | solution.py:34
  55.1 6.4 %collective-permute-start.19 = (bf16[128,1024]{1,0:T(8,128)(2,1)S(1)}, bf16[128,1024]{1,0:T(8,128)(2,1)S(1)}, u32[]{:S(2)}, u32[]{:S(2)}) collective-permute-start(bf16[128,1024]{1,0:T(8,128)(2,1)S(1)} %add_convert_fusion.3), channel_id=1, source_target_pairs={{0,16},{4,12},{8,24},{12,4},{16,0},{20,28},{24,8},{28,20},{1,17},{... | collective-permute-start | bytes 786440 | tf_op jit(solution)/shard_map/ppermute | solution.py:40
  56.0 8.7 %collective-permute-start.17 = (bf16[128,1024]{1,0:T(8,128)(2,1)S(1)}, bf16[128,1024]{1,0:T(8,128)(2,1)S(1)}, u32[]{:S(2)}, u32[]{:S(2)}) collective-permute-start(bf16[128,1024]{1,0:T(8,128)(2,1)S(1)} %add_convert_fusion.2), channel_id=1, source_target_pairs={{0,16},{4,12},{8,24},{12,4},{16,0},{20,28},{24,8},{28,20},{1,17},{... | collective-permute-start | bytes 786440 | tf_op jit(solution)/shard_map/ppermute | solution.py:40
  60.4 5.3 %collective-permute-start.16 = (bf16[256,1024]{1,0:T(8,128)(2,1)S(1)}, bf16[256,1024]{1,0:T(8,128)(2,1)S(1)}, u32[]{:S(2)}, u32[]{:S(2)}) collective-permute-start(bf16[256,1024]{1,0:T(8,128)(2,1)S(1)} %get-tuple-element.87), channel_id=1, source_target_pairs={{0,4},{4,0},{8,12},{12,8},{16,20},{20,16},{24,28},{28,24},{1,5},{5... | collective-permute-start | bytes 1572872 | tf_op jit(solution)/shard_map/ppermute | solution.py:34
  61.5 6.4 %collective-permute-start.23 = (bf16[64,1024]{1,0:T(8,128)(2,1)S(1)}, bf16[64,1024]{1,0:T(8,128)(2,1)S(1)}, u32[]{:S(2)}, u32[]{:S(2)}) collective-permute-start(bf16[64,1024]{1,0:T(8,128)(2,1)S(1)} %add_convert_fusion.11), channel_id=1, source_target_pairs={{0,8},{4,20},{8,0},{12,28},{16,24},{20,4},{24,16},{28,12},{1,9},{5... | collective-permute-start | bytes 393224 | tf_op jit(solution)/shard_map/ppermute | solution.py:40
  62.4 9.3 %collective-permute-start.22 = (bf16[128,1024]{1,0:T(8,128)(2,1)S(1)}, bf16[128,1024]{1,0:T(8,128)(2,1)S(1)}, u32[]{:S(2)}, u32[]{:S(2)}) collective-permute-start(bf16[128,1024]{1,0:T(8,128)(2,1)S(1)} %add_convert_fusion.1), channel_id=1, source_target_pairs={{0,16},{4,12},{8,24},{12,4},{16,0},{20,28},{24,8},{28,20},{1,17},{... | collective-permute-start | bytes 786440 | tf_op jit(solution)/shard_map/ppermute | solution.py:40
  64.8 7.7 %collective-permute-start.21 = (bf16[64,1024]{1,0:T(8,128)(2,1)S(1)}, bf16[64,1024]{1,0:T(8,128)(2,1)S(1)}, u32[]{:S(2)}, u32[]{:S(2)}) collective-permute-start(bf16[64,1024]{1,0:T(8,128)(2,1)S(1)} %add_convert_fusion.10), channel_id=1, source_target_pairs={{0,8},{4,20},{8,0},{12,28},{16,24},{20,4},{24,16},{28,12},{1,9},{5... | collective-permute-start | bytes 393224 | tf_op jit(solution)/shard_map/ppermute | solution.py:40
  65.7 8.3 %collective-permute-start.20 = (bf16[128,1024]{1,0:T(8,128)(2,1)S(1)}, bf16[128,1024]{1,0:T(8,128)(2,1)S(1)}, u32[]{:S(2)}, u32[]{:S(2)}) collective-permute-start(bf16[128,1024]{1,0:T(8,128)(2,1)S(1)} %add_convert_fusion), channel_id=1, source_target_pairs={{0,16},{4,12},{8,24},{12,4},{16,0},{20,28},{24,8},{28,20},{1,17},{... | collective-permute-start | bytes 786440 | tf_op jit(solution)/shard_map/ppermute | solution.py:40
  68.0 11.3 %collective-permute-start.28 = (bf16[64,1024]{1,0:T(8,128)(2,1)S(1)}, bf16[64,1024]{1,0:T(8,128)(2,1)S(1)}, u32[]{:S(2)}, u32[]{:S(2)}) collective-permute-start(bf16[64,1024]{1,0:T(8,128)(2,1)S(1)} %add_convert_fusion.9), channel_id=1, source_target_pairs={{0,3},{1,2},{2,1},{3,0},{4,7},{5,6},{6,5},{7,4},{8,11},{9,10},{10,... | collective-permute-start | bytes 393224 | tf_op jit(solution)/shard_map/ppermute | solution.py:34
  71.7 5.0 %collective-permute-start.25 = (bf16[64,1024]{1,0:T(8,128)(2,1)S(1)}, bf16[64,1024]{1,0:T(8,128)(2,1)S(1)}, u32[]{:S(2)}, u32[]{:S(2)}) collective-permute-start(bf16[64,1024]{1,0:T(8,128)(2,1)S(1)} %add_convert_fusion.8), channel_id=1, source_target_pairs={{0,8},{4,20},{8,0},{12,28},{16,24},{20,4},{24,16},{28,12},{1,9},{5... | collective-permute-start | bytes 393224 | tf_op jit(solution)/shard_map/ppermute | solution.py:40
  72.6 7.9 %collective-permute-start.27 = (bf16[64,1024]{1,0:T(8,128)(2,1)S(1)}, bf16[64,1024]{1,0:T(8,128)(2,1)S(1)}, u32[]{:S(2)}, u32[]{:S(2)}) collective-permute-start(bf16[64,1024]{1,0:T(8,128)(2,1)S(1)} %add_convert_fusion.7), channel_id=1, source_target_pairs={{0,2},{1,3},{2,0},{3,1},{4,6},{5,7},{6,4},{7,5},{8,10},{9,11},{10,... | collective-permute-start | bytes 393224 | tf_op jit(solution)/shard_map/ppermute | solution.py:34
  74.1 5.0 %collective-permute-start.24 = (bf16[64,1024]{1,0:T(8,128)(2,1)S(1)}, bf16[64,1024]{1,0:T(8,128)(2,1)S(1)}, u32[]{:S(2)}, u32[]{:S(2)}) collective-permute-start(bf16[64,1024]{1,0:T(8,128)(2,1)S(1)} %add_convert_fusion.6), channel_id=1, source_target_pairs={{0,8},{4,20},{8,0},{12,28},{16,24},{20,4},{24,16},{28,12},{1,9},{5... | collective-permute-start | bytes 393224 | tf_op jit(solution)/shard_map/ppermute | solution.py:40
  76.8 5.7 %collective-permute-start.26 = (bf16[64,1024]{1,0:T(8,128)(2,1)S(1)}, bf16[64,1024]{1,0:T(8,128)(2,1)S(1)}, u32[]{:S(2)}, u32[]{:S(2)}) collective-permute-start(bf16[64,1024]{1,0:T(8,128)(2,1)S(1)} %add_convert_fusion.5), channel_id=1, source_target_pairs={{0,1},{1,0},{2,3},{3,2},{4,5},{5,4},{6,7},{7,6},{8,9},{9,8},{10,11... | collective-permute-start | bytes 393224 | tf_op jit(solution)/shard_map/ppermute | solution.py:34
  (13 other events, 120.6 us)
